TPU v7x, 1024 devices: a whole 8x8x8 slice. The times are simulated.
1024 devices in a mesh: dom: 64 (over x, z), feat: 16 (over y, core).
Axes of the slice: x: 8, y: 8, z: 8, core: 2. Of those that a mesh axis runs over, the one named last changes fastest.
Arguments:
- node_feats: bfloat16 [16384, 1024], P('dom', 'feat'), may hold values from -6 to 6
- history: bfloat16 [16384, 1024], P('dom', 'feat'), may hold values from -6 to 6
- halo_blocks: int32 [64, 32], replicated, may hold values from 0 to 127, as said below
- tile_index: int32 [128, 24], P('dom'), may hold values from 0 to 33, as said below
- tile_weight: bfloat16 [128, 24, 128, 128], P('dom'), may hold values from 0.001 to 10, as said below
- self_one: bfloat16 [1024, 1024], P(None, 'feat'), may hold values from -0.1875 to 0.1875
- neigh_one: bfloat16 [1024, 1024], P(None, 'feat'), may hold values from -3 to 3
- self_two: bfloat16 [1024, 1024], P(None, 'feat'), may hold values from -0.1875 to 0.1875
- neigh_two: bfloat16 [1024, 1024], P(None, 'feat'), may hold values from -3 to 3
- batch_ids: int32 [8192], P('dom'), may hold values from 0 to 255
- cotangent: bfloat16 [8192, 1024], P('dom', 'feat'), may hold values from -0.06591797 to 0.06591797
Outputs:
- node_out: bfloat16 [16384, 1024], P('dom', 'feat')
- grad_self_one: float32 [1024, 1024], P(None, 'feat')
- grad_neigh_one: float32 [1024, 1024], P(None, 'feat')
- grad_self_two: float32 [1024, 1024], P(None, 'feat')
- grad_neigh_two: float32 [1024, 1024], P(None, 'feat')
Inputs may be any that keep to these rules, and one draw needn't show every extreme that they name: `halo_blocks`: row p names 32 blocks that belong to 32 different partitions, none of them p: exactly one block from each partition it reads; some partitions are read by far more partitions than others. `tile_index`: each partition's tiles together name every one of its 34 table blocks. `tile_weight`: positive edge weights.
All inputs are finite; a program needn't handle non-finite values.
Results may differ from a plain program's by a relative error of at most 0.024.
Values may be sent and summed in bfloat16 or wider, within the bound.
No kernel may reach another device: no remote copies, remote signals or barrier semaphores. Data moves between devices by JAX's collectives and lax.ppermute only.
A program may use at most 32 MiB of HBM per device.

v0:
```python
import jax
import jax.numpy as jnp
from jax import lax
from jax.sharding import PartitionSpec as P


def aggregate(source_rows, tile_index, tile_weight):
    picked = source_rows[tile_index]
    summed = jnp.einsum("bkvc,bkcf->bvf", tile_weight, picked, preferred_element_type=jnp.float32)
    row_total = jnp.sum(tile_weight, axis=(1, 3), dtype=jnp.float32)
    return (summed, row_total)


def widen(own_rows, mean_rows):
    return (
        lax.all_gather(own_rows, "feat", axis=1, tiled=True),
        lax.all_gather(mean_rows, "feat", axis=1, tiled=True),
    )


def on_device(
    node_feats,
    history,
    halo_blocks,
    tile_index,
    tile_weight,
    self_one,
    neigh_one,
    self_two,
    neigh_two,
    batch_ids,
    cotangent,
):
    own_blocks = tile_index.shape[0]
    block_rows = tile_weight.shape[2]
    slice_width = node_feats.shape[1]
    owned_rows = node_feats.shape[0]
    position = lax.axis_index("dom")
    wanted = lax.dynamic_index_in_dim(halo_blocks, position, 0, keepdims=False)
    own_feats = node_feats.reshape(own_blocks, block_rows, slice_width)
    empty = jnp.zeros((wanted.shape[0], block_rows, slice_width), node_feats.dtype)
    pieces = (
        lax.all_gather(node_feats, "dom", axis=0, tiled=True),
        lax.all_gather(history, "dom", axis=0, tiled=True),
    )
    piece_blocks = pieces[0].shape[0] // block_rows
    inside = (wanted >= 0) & (wanted < piece_blocks)
    clipped = jnp.clip(wanted, 0, piece_blocks - 1)
    new_feats = pieces[0].reshape(piece_blocks, block_rows, slice_width)[clipped]
    new_history = pieces[1].reshape(piece_blocks, block_rows, slice_width)[clipped]
    inside_mask = inside[:, None, None]
    halo_feats = jnp.where(inside_mask, new_feats, empty)
    halo_history = jnp.where(inside_mask, new_history, empty)
    summed_one, row_total = aggregate(
        jnp.concatenate([own_feats, halo_feats], axis=0), tile_index, tile_weight
    )
    agg_one = (
        (summed_one / row_total[:, :, None]).astype(jnp.bfloat16).reshape(owned_rows, slice_width)
    )
    whole_feats, whole_agg_one = widen(node_feats, agg_one)
    pre_one = jnp.dot(whole_feats, self_one, preferred_element_type=jnp.float32) + jnp.dot(
        whole_agg_one, neigh_one, preferred_element_type=jnp.float32
    )
    hidden_one = jax.nn.silu(pre_one).astype(jnp.bfloat16)
    own_hidden = hidden_one.reshape(own_blocks, block_rows, slice_width)
    summed_two, unused_total = aggregate(
        jnp.concatenate([own_hidden, halo_history], axis=0), tile_index, tile_weight
    )
    agg_two = (
        (summed_two / row_total[:, :, None]).astype(jnp.bfloat16).reshape(owned_rows, slice_width)
    )
    whole_hidden, whole_agg_two = widen(hidden_one, agg_two)
    pre_two = jnp.dot(whole_hidden, self_two, preferred_element_type=jnp.float32) + jnp.dot(
        whole_agg_two, neigh_two, preferred_element_type=jnp.float32
    )
    node_out = pre_two.astype(jnp.bfloat16)
    seed_rows = (batch_ids[:, None] == jnp.arange(owned_rows, dtype=jnp.int32)[None, :]).astype(
        jnp.bfloat16
    )
    grad_two = jnp.einsum(
        "sr,sc->rc", seed_rows, cotangent, preferred_element_type=jnp.float32
    ).astype(jnp.bfloat16)
    part_self_two = jnp.einsum(
        "rh,rc->hc", whole_hidden, grad_two, preferred_element_type=jnp.float32
    )
    part_neigh_two = jnp.einsum(
        "rh,rc->hc", whole_agg_two, grad_two, preferred_element_type=jnp.float32
    )
    grad_self_two, grad_neigh_two = lax.psum((part_self_two, part_neigh_two), "dom")
    term_self = jnp.einsum("rc,hc->rh", grad_two, self_two, preferred_element_type=jnp.float32)
    term_neigh = jnp.einsum("rc,hc->rh", grad_two, neigh_two, preferred_element_type=jnp.float32)
    back_self, back_neigh = (
        lax.psum_scatter(
            term_self.astype(jnp.bfloat16), "feat", scatter_dimension=1, tiled=True
        ).astype(jnp.float32),
        lax.psum_scatter(
            term_neigh.astype(jnp.bfloat16), "feat", scatter_dimension=1, tiled=True
        ).astype(jnp.float32),
    )
    scaled = (
        back_neigh.reshape(own_blocks, block_rows, slice_width) / row_total[:, :, None]
    ).astype(jnp.bfloat16)
    contrib = jnp.einsum("bkvc,bvf->bkcf", tile_weight, scaled, preferred_element_type=jnp.float32)
    onehot = (
        tile_index[:, :, None] == jnp.arange(own_blocks, dtype=jnp.int32)[None, None, :]
    ).astype(jnp.float32)
    own_grad = jnp.einsum(
        "bkn,bkcf->ncf", onehot, contrib, precision=lax.Precision.HIGHEST
    ).reshape(owned_rows, slice_width)
    unused_out, pull = jax.vjp(jax.nn.silu, pre_one)
    grad_one = pull(back_self + own_grad)[0].astype(jnp.bfloat16)
    part_self_one = jnp.einsum(
        "rh,rc->hc", whole_feats, grad_one, preferred_element_type=jnp.float32
    )
    part_neigh_one = jnp.einsum(
        "rh,rc->hc", whole_agg_one, grad_one, preferred_element_type=jnp.float32
    )
    grad_self_one, grad_neigh_one = lax.psum((part_self_one, part_neigh_one), "dom")
    return (node_out, grad_self_one, grad_neigh_one, grad_self_two, grad_neigh_two)


def solution(mesh):
    return jax.shard_map(
        on_device,
        mesh=mesh,
        in_specs=(
            P("dom", "feat"),
            P("dom", "feat"),
            P(),
            P("dom", None),
            P("dom", None, None, None),
            P(None, "feat"),
            P(None, "feat"),
            P(None, "feat"),
            P(None, "feat"),
            P("dom"),
            P("dom", "feat"),
        ),
        out_specs=(
            P("dom", "feat"),
            P(None, "feat"),
            P(None, "feat"),
            P(None, "feat"),
            P(None, "feat"),
        ),
        check_vma=False,
    )
```

profile of v0, /device:TPU:1, one launch (start us, length us, event | category | flops | bytes accessed | tf_op | source)
XLA Modules:
  0.0 452.9 jit_solution(15039447327602353017)
XLA Ops:
  8.1 1.0 convolution_convert_fusion.2
  9.1 2.2 convolution_convert_fusion
  12.5 1.1 convolution_convert_fusion.1
  14.1 29.7 %all_gather.18 = bf16[256,1024]{0,1:T(8,128)(2,1)S(1)} all-gather(bf16[256,64]{0,1:T(8,128)(2,1)S(1)} %copy-done.7), channel_id=1, replica_groups=mesh['dom'=64,'feat'=16] {'feat'}, dimensions={1}, use_global_device_ids=true | all-gather | bytes 557056 | tf_op jit(solution)/shard_map/all_gather | solution.py:16
  44.5 42.1 %reduce-scatter.5.cloned.1.call-done = bf16[256,64]{0,1:T(8,128)(2,1)} async-done(((bf16[256,1024]{0,1:T(8,128)(2,1)}), bf16[256,64]{0,1:T(8,128)(2,1)}) %reduce-scatter.5.cloned.1.call-update) | async-done | bytes 32784 | tf_op jit(solution)/shard_map/reduce_scatter | solution.py:96
  86.6 1.1 convolution_bitcast_fusion
  87.7 1.5 fusion
  89.2 25.3 %all-gather.3.cloned.1.call-done = bf16[16384,64]{0,1:T(8,128)(2,1)} async-done(((bf16[256,64]{0,1:T(8,128)(2,1)}), bf16[16384,64]{0,1:T(8,128)(2,1)}) %all-gather.3.cloned.1.call-update) | async-done | bytes 2097168 | tf_op jit(solution)/shard_map/all_gather | solution.py:43
  114.6 3.5 copy_bitcast_fusion.1
  118.1 2.2 gather_fusion
  120.3 84.3 %all-gather.5.cloned.1.call-done = bf16[16384,64]{0,1:T(8,128)(2,1)} async-done(((bf16[256,64]{0,1:T(8,128)(2,1)}), bf16[16384,64]{0,1:T(8,128)(2,1)}) %all-gather.5.cloned.1.call-update) | async-done | bytes 2097168 | tf_op jit(solution)/shard_map/all_gather | solution.py:44
  204.6 3.5 copy_bitcast_fusion
  208.2 2.2 gather_fusion.2
  210.4 0.9 broadcast_select_fusion
  211.4 0.7 gather_fusion.1
  212.1 0.6 fusion.7
  212.8 23.1 %all_gather.20 = bf16[256,1024]{0,1:T(8,128)(2,1)S(1)} all-gather(bf16[256,64]{0,1:T(8,128)(2,1)S(1)} %bitcast.116), channel_id=1, replica_groups=mesh['dom'=64,'feat'=16] {'feat'}, dimensions={1}, use_global_device_ids=true | all-gather | bytes 557056 | tf_op jit(solution)/shard_map/all_gather | solution.py:17
  235.9 1.1 fusion.11
  237.0 18.0 %all_gather.21 = bf16[256,1024]{0,1:T(8,128)(2,1)} all-gather(bf16[256,64]{0,1:T(8,128)(2,1)S(1)} %get-tuple-element.10), channel_id=1, replica_groups=mesh['dom'=64,'feat'=16] {'feat'}, dimensions={1}, use_global_device_ids=true | all-gather | bytes 557056 | tf_op jit(solution)/shard_map/all_gather | solution.py:16
  255.0 1.0 fusion.21
  255.9 1.0 convolution_bitcast_fusion.1
  257.0 0.7 gather_fusion.3
  257.7 0.6 fusion.8
  258.4 16.6 %all_gather.23 = bf16[256,1024]{0,1:T(8,128)(2,1)S(1)} all-gather(bf16[256,64]{0,1:T(8,128)(2,1)S(1)} %bitcast.117), channel_id=1, replica_groups=mesh['dom'=64,'feat'=16] {'feat'}, dimensions={1}, use_global_device_ids=true | all-gather | bytes 557056 | tf_op jit(solution)/shard_map/all_gather | solution.py:17
  274.9 1.0 fusion.23
  275.9 1.0 fusion.22
  277.2 0.8 fusion.4
  278.0 161.5 %all-reduce.3.cloned.1.call-done = (f32[1024,64]{0,1:T(8,128)}, f32[1024,64]{0,1:T(8,128)}, f32[1024,64]{0,1:T(8,128)}, f32[1024,64]{0,1:T(8,128)}) async-done(((f32[1024,64]{0,1:T(8,128)}, f32[1024,64]{0,1:T(8,128)}, f32[1024,64]{0,1:T(8,128)}, f32[1024,64]{0,1:T(8,128)}), (f32[1024,64]{0,1:T(8,128)}, f32[1024,64]{0,1:T(8,128)}, f32[1024,64]{0,1:T(8,128)}, ...) | async-done | bytes 1048592 | tf_op jit(solution)/shard_map/psum | solution.py:118
  439.5 1.7 copy.62
  441.3 1.7 copy.63
  442.9 1.7 copy.64
  444.6 0.7 copy.65
  (53 shorter events, 2.7 us)
Async XLA Ops:
  8.0 4.5 copy-start
  8.0 6.1 %copy-start.7 = (bf16[256,64]{0,1:T(8,128)(2,1)S(1)}, bf16[256,64]{0,1:T(8,128)(2,1)}, u32[]{:S(2)}) copy-start(bf16[256,64]{0,1:T(8,128)(2,1)} %param.11) | copy-start | bytes 98308
  8.0 5.7 %copy-start.10 = (s32[64,32]{0,1:T(8,128)S(1)}, s32[64,32]{0,1:T(8,128)}, u32[]{:S(2)}) copy-start(s32[64,32]{0,1:T(8,128)} %param.13) | copy-start | bytes 24580
  8.0 78.6 %reduce-scatter.5.cloned.1.call-start = ((), (), s32[]{:S(2)}) async-start(), calls=%async_computation.5 | async-start | bytes 557056 | tf_op jit(solution)/shard_map/reduce_scatter | solution.py:96
  9.0 34.8 %copy-start.11 = (s32[2,24]{1,0:T(2,128)S(1)}, s32[2,24]{1,0:T(2,128)}, u32[]{:S(2)}) copy-start(s32[2,24]{1,0:T(2,128)} %param.14) | copy-start | bytes 580
  9.0 34.9 %copy-start.1 = (bf16[2,24,128,128]{3,2,1,0:T(8,128)(2,1)S(1)}, bf16[2,24,128,128]{3,2,1,0:T(8,128)(2,1)}, u32[]{:S(2)}) copy-start(bf16[2,24,128,128]{3,2,1,0:T(8,128)(2,1)} %param.15) | copy-start | bytes 4718596
  11.3 103.3 %all-gather.3.cloned.1.call-start = ((), (), s32[]{:S(2)}) async-start(), calls=%async_computation.2 | async-start | bytes 2129920 | tf_op jit(solution)/shard_map/all_gather | solution.py:43
  11.8 192.8 %all-gather.5.cloned.1.call-start = ((), (), s32[]{:S(2)}) async-start(), calls=%async_computation.3 | async-start | bytes 2129920 | tf_op jit(solution)/shard_map/all_gather | solution.py:44
  12.4 31.8 %copy-start.9 = (bf16[1024,64]{0,1:T(8,128)(2,1)S(1)}, bf16[1024,64]{0,1:T(8,128)(2,1)}, u32[]{:S(2)}) copy-start(bf16[1024,64]{0,1:T(8,128)(2,1)} %param.16) | copy-start | bytes 393220
  12.4 223.5 %reduce-scatter.3.cloned.1.call-start = ((), (), s32[]{:S(2)}) async-start(), calls=%async_computation.4 | async-start | bytes 557056 | tf_op jit(solution)/shard_map/reduce_scatter | solution.py:93
  13.7 425.9 %all-reduce.3.cloned.1.call-start = ((), (), s32[]{:S(2)}) async-start(), calls=%async_computation.6 | async-start | bytes 2097152 | tf_op jit(solution)/shard_map/psum | solution.py:118
  43.8 43.9 %copy-start.2 = (bf16[256,1024]{0,1:T(8,128)(2,1)}, bf16[256,1024]{0,1:T(8,128)(2,1)S(1)}, u32[]{:S(2)}) copy-start(bf16[256,1024]{0,1:T(8,128)(2,1)S(1)} %all_gather.18) | copy-start | bytes 1572868
  212.1 23.8 %copy-start.12 = (bf16[1024,64]{0,1:T(8,128)(2,1)S(1)}, bf16[1024,64]{0,1:T(8,128)(2,1)}, u32[]{:S(2)}) copy-start(bf16[1024,64]{0,1:T(8,128)(2,1)} %param.17) | copy-start | bytes 393220
  212.8 43.2 %copy-start.3 = (bf16[256,1024]{0,1:T(8,128)(2,1)S(1)}, bf16[256,1024]{0,1:T(8,128)(2,1)}, u32[]{:S(2)}) copy-start(bf16[256,1024]{0,1:T(8,128)(2,1)} %copy-done.2) | copy-start | bytes 1572868
  235.9 21.0 %copy-start.5 = (bf16[32,128,64]{1,2,0:T(8,128)(2,1)S(1)}, bf16[32,128,64]{1,2,0:T(8,128)(2,1)}, u32[]{:S(2)}) copy-start(bf16[32,128,64]{1,2,0:T(8,128)(2,1)} %get-tuple-element.11) | copy-start | bytes 1572868
  257.7 18.2 %copy-start.4 = (bf16[256,1024]{0,1:T(8,128)(2,1)S(1)}, bf16[256,1024]{0,1:T(8,128)(2,1)}, u32[]{:S(2)}) copy-start(bf16[256,1024]{0,1:T(8,128)(2,1)} %all_gather.21) | copy-start | bytes 1572868
  274.9 2.2 copy-start.6
  439.5 5.1 %copy-start.8 = (f32[1024,64]{0,1:T(8,128)S(1)}, f32[1024,64]{0,1:T(8,128)}, u32[]{:S(2)}) copy-start(f32[1024,64]{0,1:T(8,128)} %get-tuple-element.17) | copy-start | bytes 786436
Sparse Core Ops, SparseCore 0:
  12.2 74.3 reduce-scatter.4
  90.3 60.7 reduce-scatter.2
Sparse Core Ops, SparseCore 1:
  15.9 98.6 all-gather.2
  118.6 86.0 all-gather.4
  277.0 162.5 all-reduce.2
where the time goes:
time: 457 us; the launch traced here: 453 us
  waiting for transfers between devices  314 us (69%)
  blocking collectives  87.4 us (19%)
  local copies, waits for them, and re-layouts  18.8 us (4%)
  between operations  15.9 us (3%)
  matrix products  14.4 us (3%)
    psum x1, waiting for transfers between devices, on_device(): lax.psum((part_self_one, part_neigh_one), 'dom')  162 us
    all_gather x1, waiting for transfers between devices, on_device(): lax.all_gather(history, 'dom', axis=0, tiled=True)  84.3 us
    all_gather x2, blocking collectives, widen(): lax.all_gather(own_rows, 'feat', axis=1, tiled=True)  47.7 us
    reduce_scatter x1, waiting for transfers between devices, on_device(): lax.psum_scatter(term_neigh.astype(jnp.bfloat16), 'feat', scatter_dimensi...  42.1 us
    all_gather x2, blocking collectives, widen(): lax.all_gather(mean_rows, 'feat', axis=1, tiled=True)  39.7 us
    all_gather x1, waiting for transfers between devices, on_device(): lax.all_gather(node_feats, 'dom', axis=0, tiled=True)  25.3 us
  transfers between devices with their start and end apart: 5, of which 4 were waited for; matrix products, arithmetic and copies ran while one was open for 4% of the time, Pallas kernels for 0%

commit v1 on v0

v1 whole, which is shorter than its diff:
```python
import jax
import jax.numpy as jnp
from jax import lax
from jax.sharding import PartitionSpec as P

BF = jnp.bfloat16
F32 = jnp.float32


def mm(a, b, dims):
    return lax.dot_general(a, b, (dims, ((), ())), preferred_element_type=F32)


def on_device(
    node_feats,
    history,
    halo_blocks,
    tile_index,
    tile_weight,
    self_one,
    neigh_one,
    self_two,
    neigh_two,
    batch_ids,
    cotangent,
):
    own_blocks, tiles = tile_index.shape
    rows = tile_weight.shape[2]
    width = node_feats.shape[1]
    owned = node_feats.shape[0]
    parts = halo_blocks.shape[0]
    seeds = cotangent.shape[0]
    me = lax.axis_index("dom")

    feats_t = node_feats.T
    cot_t = cotangent.T
    self_one_t, neigh_one_t, self_two_t, neigh_two_t = (
        self_one.T,
        neigh_one.T,
        self_two.T,
        neigh_two.T,
    )

    def blocks_first(array_t):
        return array_t.reshape(width, own_blocks, rows).transpose(1, 0, 2)

    all_history = lax.all_gather(blocks_first(history.T), "dom", axis=0, tiled=True)
    whole = lax.all_gather(jnp.concatenate([feats_t, cot_t], axis=1), "feat", axis=0, tiled=True)
    whole_feats, whole_cot = whole[:, :owned], whole[:, owned:]

    feat_blocks = blocks_first(feats_t)
    second = jnp.any(halo_blocks == own_blocks * me + 1, axis=1)
    send = jnp.where(second[:, None, None], feat_blocks[1][None], feat_blocks[0][None])
    got = lax.all_to_all(send, "dom", 0, 0, tiled=True)

    wanted = lax.dynamic_index_in_dim(halo_blocks, me, 0, keepdims=False)
    is_own = tile_index < own_blocks
    tile_block = wanted[jnp.clip(tile_index - own_blocks, 0, wanted.shape[0] - 1)]
    tile_block = jnp.clip(tile_block, 0, own_blocks * parts - 1)

    onehot = tile_index[:, :, None] == jnp.arange(own_blocks, dtype=jnp.int32)[None, None, :]
    dense = jnp.sum(
        jnp.where(onehot[:, :, :, None, None], tile_weight[:, :, None].astype(F32), 0.0), axis=1
    )
    dense = dense.transpose(0, 2, 1, 3).reshape(owned, owned).astype(BF)
    row_total = jnp.sum(tile_weight, axis=(1, 3), dtype=F32).reshape(1, owned)
    inverse = 1.0 / row_total

    def halo_sum(picked):
        picked = jnp.where(is_own[:, :, None, None], jnp.zeros((), BF), picked)
        out = jnp.einsum("bkfc,bkvc->fbv", picked, tile_weight, preferred_element_type=F32)
        return out.reshape(width, owned)

    both = jnp.concatenate(
        [
            self_two_t.reshape(width, -1, width).transpose(1, 0, 2),
            neigh_two_t.reshape(width, -1, width).transpose(1, 0, 2),
        ],
        axis=2,
    )
    columns = lax.all_to_all(both, "feat", 0, 0, tiled=True).reshape(-1, 2 * width)

    mean_one = (halo_sum(got[tile_block // own_blocks]) + mm(feats_t, dense, ((1,), (1,)))) * inverse
    whole_mean_one = lax.all_gather(mean_one.astype(BF), "feat", axis=0, tiled=True)
    pre_one = mm(self_one_t, whole_feats, ((1,), (0,))) + mm(
        neigh_one_t, whole_mean_one, ((1,), (0,))
    )
    gate = jax.nn.sigmoid(pre_one)
    hidden = (pre_one * gate).astype(BF)

    whole_hidden = lax.all_gather(hidden, "feat", axis=0, tiled=True)
    halo_two = (halo_sum(all_history[tile_block]) * inverse).astype(BF)
    whole_halo_two = lax.all_gather(halo_two, "feat", axis=0, tiled=True)
    whole_mean_two = (
        mm(whole_hidden, dense, ((1,), (1,))) * inverse + whole_halo_two.astype(F32)
    ).astype(BF)
    node_out = mm(self_two_t, whole_hidden, ((1,), (0,))) + mm(
        neigh_two_t, whole_mean_two, ((1,), (0,))
    )

    seed_rows = (
        batch_ids[:, None] == jnp.arange(owned, dtype=jnp.int32)[None, :]
    ).astype(BF)
    whole_grad_two = mm(whole_cot, seed_rows, ((1,), (0,))).astype(BF)
    grad_two = mm(cot_t, seed_rows, ((1,), (0,))).astype(BF)
    back = mm(columns, whole_grad_two, ((0,), (0,)))
    scaled = (back[width:] * inverse).astype(BF)
    own_grad = mm(scaled, dense, ((1,), (0,)))
    slope = gate * (1.0 + pre_one * (1.0 - gate))
    grad_one = ((back[:width] + own_grad) * slope).astype(BF)
    ones = mm(
        grad_one, jnp.concatenate([whole_feats, whole_mean_one], axis=0), ((1,), (1,))
    )
    twos = mm(
        grad_two, jnp.concatenate([whole_hidden, whole_mean_two], axis=0), ((1,), (1,))
    )
    total = jnp.concatenate([ones, twos], axis=1).astype(BF)
    depth = self_one.shape[0]
    low, high = 8, width // 8
    wide = parts // high
    lanes = depth // wide
    pieces = total.reshape(high, low, 4, wide, lanes).transpose(0, 3, 2, 1, 4)
    pieces = pieces.reshape(parts, 4, low, lanes)
    mine = lax.all_to_all(pieces, "dom", 0, 0, tiled=True)
    mine = jnp.sum(mine.astype(F32), axis=0, keepdims=True).astype(BF)
    spread = jnp.broadcast_to(mine, (parts, 4, low, lanes))
    sums = lax.all_to_all(spread, "dom", 0, 0, tiled=True)
    sums = sums.reshape(high, wide, 4, low, lanes).transpose(2, 0, 3, 1, 4)
    sums = sums.reshape(4, width, depth).astype(F32)
    return (
        node_out.astype(BF).T,
        sums[0].T,
        sums[1].T,
        sums[2].T,
        sums[3].T,
    )


def solution(mesh):
    return jax.shard_map(
        on_device,
        mesh=mesh,
        in_specs=(
            P("dom", "feat"),
            P("dom", "feat"),
            P(),
            P("dom", None),
            P("dom", None, None, None),
            P(None, "feat"),
            P(None, "feat"),
            P(None, "feat"),
            P(None, "feat"),
            P("dom"),
            P("dom", "feat"),
        ),
        out_specs=(
            P("dom", "feat"),
            P(None, "feat"),
            P(None, "feat"),
            P(None, "feat"),
            P(None, "feat"),
        ),
        check_vma=False,
    )
```

time: 457 us -> 218 us (0.48)
  waiting for transfers between devices: 314 us -> 36.7 us
  starting transfers between devices: 0.21 us -> 38.5 us
  blocking collectives: 87.4 us -> 99.9 us
  matrix products: 14.4 us -> 8.52 us
  local copies, waits for them, and re-layouts: 18.8 us -> 13.2 us
    psum x1 -> x0, waiting for transfers between devices: 162 us -> none  [on_device(): lax.psum((part_self_one, part_neigh_one), 'dom')]
    all_gather x2 -> x1, waiting for transfers between devices: 110 us -> 5.74 us  [on_device(): lax.all_gather(blocks_first(history.T), 'dom', axis=0, tiled=True)]
    reduce_scatter x2 -> x0, waiting for transfers between devices: 42.1 us -> none  [the longest x1 42.1 us: on_device(): lax.psum_scatter(term_neigh.astype(jnp.bfloat16), 'feat', scatter_dimensi...]
    all_to_all x0 -> x3, starting transfers between devices: none -> 38.4 us  [the longest x1 17.5 us: on_device(): lax.all_to_all(both, 'feat', 0, 0, tiled=True).reshape(-1, 2 * width)]
    all_to_all x0 -> x3, waiting for transfers between devices: none -> 30.9 us  [the longest x1 15.3 us: on_device(): sums = lax.all_to_all(spread, 'dom', 0, 0, tiled=True)]
    all_to_all x0 -> x1, blocking collectives: none -> 25.6 us  [on_device(): mine = lax.all_to_all(pieces, 'dom', 0, 0, tiled=True)]
    all_gather x4, blocking collectives: 87.4 us -> 74.3 us  [the longest x1 22.8 us: on_device(): whole_halo_two = lax.all_gather(halo_two, 'feat', axis=0, tiled=True)]
    dot_general x15 -> x11, matrix products: 14.4 us -> 8.52 us  [the longest x9 5.92 us: mm(): return lax.dot_general(a, b, (dims, ((), ())), preferred_element_type=F32)]
  transfers between devices with their start and end apart: 5 -> 4, of which waited for: 4 -> 4; matrix products, arithmetic and copies ran while one was open for 4% -> 8% of each run, Pallas kernels for 0% -> 0%
where the time goes in v1:
time: 218 us; the launch traced here: 215 us
  blocking collectives  99.9 us (46%)
  starting transfers between devices  38.5 us (18%)
  waiting for transfers between devices  36.7 us (17%)
  between operations  14.4 us (7%)
  local copies, waits for them, and re-layouts  13.2 us (6%)
  matrix products  8.52 us (4%)
  other arithmetic  3.47 us (2%)
    all_to_all x1, blocking collectives, on_device(): mine = lax.all_to_all(pieces, 'dom', 0, 0, tiled=True)  25.6 us
    all_gather x1, blocking collectives, on_device(): whole_halo_two = lax.all_gather(halo_two, 'feat', axis=0, tiled=True)  22.8 us
    all_to_all x1, starting transfers between devices, on_device(): lax.all_to_all(both, 'feat', 0, 0, tiled=True).reshape(-1, 2 * width)  17.5 us
    all_gather x1, blocking collectives, on_device(): whole_hidden = lax.all_gather(hidden, 'feat', axis=0, tiled=True)  17.4 us
    all_gather x1, blocking collectives, on_device(): lax.all_gather(mean_one.astype(BF), 'feat', axis=0, tiled=True)  17.2 us
    all_gather x1, blocking collectives, on_device(): lax.all_gather(jnp.concatenate([feats_t, cot_t], axis=1), 'feat', axis=0,...  16.9 us
    all_to_all x1, waiting for transfers between devices, on_device(): sums = lax.all_to_all(spread, 'dom', 0, 0, tiled=True)  15.3 us
    all_to_all x1, starting transfers between devices, on_device(): got = lax.all_to_all(send, 'dom', 0, 0, tiled=True)  13.8 us
  transfers between devices with their start and end apart: 4, of which 4 were waited for; matrix products, arithmetic and copies ran while one was open for 8% of the time, Pallas kernels for 0%

profile of v1, /device:TPU:1, one launch (start us, length us, event | category | flops | bytes accessed | tf_op | source)
XLA Modules:
  0.0 214.6 jit_solution(101253495292238487)
XLA Ops:
  7.3 0.8 reshape.151
  8.1 0.6 copy.38
  8.7 1.1 reshape.154
  9.8 1.1 reshape.153
  11.1 0.8 copy.40
  11.9 17.5 %all-to-all-start.1 = ((bf16[16,64,128]{2,1,0:T(8,128)(2,1)}), bf16[16,64,128]{2,1,0:T(8,128)(2,1)S(1)}, u32[]{:S(2)}, u32[]{:S(2)}) async-start(bf16[16,64,128]{2,1,0:T(8,128)(2,1)} %copy.40), calls=%async_computation.1 | async-start | bytes 524288 | tf_op jit(solution)/shard_map/all_to_all | solution.py:81
  29.7 0.8 gather_fusion
  30.8 0.6 pad_maximum_fusion.2
  31.4 1.1 broadcast_select_fusion
  32.5 8.7 %all-to-all-done.1 = bf16[16,64,128]{2,1,0:T(8,128)(2,1)S(1)} async-done(((bf16[16,64,128]{2,1,0:T(8,128)(2,1)}), bf16[16,64,128]{2,1,0:T(8,128)(2,1)S(1)}, u32[]{:S(2)}, u32[]{:S(2)}) %all-to-all-start.1) | async-done | bytes 262176 | tf_op jit(solution)/shard_map/all_to_all | solution.py:81
  41.2 0.7 copy-done.5
  41.9 13.8 %all-to-all-start = ((bf16[64,64,128]{2,1,0:T(8,128)(2,1)}), bf16[64,64,128]{2,1,0:T(8,128)(2,1)S(1)}, u32[]{:S(2)}, u32[]{:S(2)}) async-start(bf16[64,64,128]{2,1,0:T(8,128)(2,1)} %broadcast_select_fusion), calls=%async_computation | async-start | bytes 2097152 | tf_op jit(solution)/shard_map/all_to_all | solution.py:54
  55.7 16.9 %all_gather.15 = bf16[1024,384]{1,0:T(8,128)(2,1)S(1)} all-gather(bf16[64,384]{1,0:T(8,128)(2,1)} %pad_maximum_fusion.2), channel_id=1, replica_groups=mesh['dom'=64,'feat'=16] {'feat'}, dimensions={0}, use_global_device_ids=true | all-gather | bytes 835584 | tf_op jit(solution)/shard_map/all_gather | solution.py:48
  73.6 0.8 copy.37
  74.7 0.8 fusion.53
  75.6 2.2 %fusion.2 = f32[128,256]{1,0:T(8,128)} fusion(bf16[1024,128]{1,0:T(8,128)(2,1)} %bitcast.116, bf16[1024,384]{1,0:T(8,128)(2,1)S(1)} %all_gather.15, s32[128]{0:T(128)} %param.20), kind=kOutput, calls=%fused_computation.10 | convolution fusion | flops 134512640 | bytes 655872 | tf_op jit(solution)/shard_map/dot_general | solution.py:11
  77.8 7.0 %all-to-all-done = bf16[64,64,128]{2,1,0:T(8,128)(2,1)S(1)} async-done(((bf16[64,64,128]{2,1,0:T(8,128)(2,1)}), bf16[64,64,128]{2,1,0:T(8,128)(2,1)S(1)}, u32[]{:S(2)}, u32[]{:S(2)}) %all-to-all-start) | async-done | bytes 1048608 | tf_op jit(solution)/shard_map/all_to_all | solution.py:54
  84.7 1.6 gather_fusion.1
  86.3 1.9 convolution_bitcast_fusion.2
  88.4 17.2 %all_gather.16 = bf16[1024,256]{1,0:T(8,128)(2,1)S(1)} all-gather(bf16[64,256]{1,0:T(8,128)(2,1)S(1)} %fusion.7), channel_id=1, replica_groups=mesh['dom'=64,'feat'=16] {'feat'}, dimensions={0}, use_global_device_ids=true | all-gather | bytes 557056 | tf_op jit(solution)/shard_map/all_gather | solution.py:84
  106.4 17.4 %all_gather.17 = bf16[1024,256]{1,0:T(8,128)(2,1)S(1)} all-gather(bf16[64,256]{1,0:T(8,128)(2,1)S(1)} %get-tuple-element.13), channel_id=1, replica_groups=mesh['dom'=64,'feat'=16] {'feat'}, dimensions={0}, use_global_device_ids=true | all-gather | bytes 557056 | tf_op jit(solution)/shard_map/all_gather | solution.py:91
  123.8 5.7 %all-gather.2.cloned.1.call-done = bf16[128,64,128]{2,1,0:T(8,128)(2,1)} async-done(((bf16[2,64,128]{2,1,0:T(8,128)(2,1)}), bf16[128,64,128]{2,1,0:T(8,128)(2,1)}) %all-gather.2.cloned.1.call-update) | async-done | bytes 2097168 | tf_op jit(solution)/shard_map/all_gather | solution.py:47
  129.6 2.3 %gather_fusion.2 = bf16[48,64,128]{2,1,0:T(8,128)(2,1)S(1)} fusion(bf16[128,64,128]{2,1,0:T(8,128)(2,1)} %all-gather.2.cloned.1.call-done, s32[1024]{0:T(1024)S(1)} %pad_clamp_fusion), kind=kCustom, calls=%fused_computation.2 | custom fusion | bytes 1573056 | tf_op jit(solution)/shard_map/gather | solution.py:92
  131.9 0.7 convolution_bitcast_fusion.1
  132.6 22.8 %all_gather.19 = bf16[1024,256]{1,0:T(8,128)(2,1)S(1)} all-gather(bf16[64,256]{1,0:T(8,128)(2,1)S(1)} %fusion.32), channel_id=1, replica_groups=mesh['dom'=64,'feat'=16] {'feat'}, dimensions={0}, use_global_device_ids=true | all-gather | bytes 557056 | tf_op jit(solution)/shard_map/all_gather | solution.py:93
  155.8 0.6 convolution_convert_fusion
  156.6 25.6 %all_to_all.20 = bf16[64,4,8,128]{3,2,1,0:T(8,128)(2,1)S(1)} all-to-all(bf16[64,4,8,128]{3,2,1,0:T(8,128)(2,1)S(1)} %bitcast.110), channel_id=1, replica_groups=mesh['dom'=64,'feat'=16] {'dom'}, dimensions={0} | all-to-all | bytes 1048576 | tf_op jit(solution)/shard_map/all_to_all | solution.py:124
  182.2 0.9 broadcast_in_dim.95
  183.1 7.2 %all-to-all-start.3 = ((bf16[64,4,8,128]{3,2,1,0:T(8,128)(2,1)}), bf16[64,4,8,128]{3,2,1,0:T(8,128)(2,1)S(1)}, u32[]{:S(2)}, u32[]{:S(2)}) async-start(bf16[64,4,8,128]{3,2,1,0:T(8,128)(2,1)} %broadcast_in_dim.95), calls=%async_computation.3 | async-start | bytes 1048576 | tf_op jit(solution)/shard_map/all_to_all | solution.py:127
  190.5 0.8 fusion.9
  191.4 15.3 %all-to-all-done.3 = bf16[64,4,8,128]{3,2,1,0:T(8,128)(2,1)S(1)} async-done(((bf16[64,4,8,128]{3,2,1,0:T(8,128)(2,1)}), bf16[64,4,8,128]{3,2,1,0:T(8,128)(2,1)S(1)}, u32[]{:S(2)}, u32[]{:S(2)}) %all-to-all-start.3) | async-done | bytes 524320 | tf_op jit(solution)/shard_map/all_to_all | solution.py:127
  206.7 1.0 slice_bitcast_fusion
  (70 shorter events, 3.9 us)
Async XLA Ops:
  7.2 98.5 %copy-start = (bf16[1024,64]{0,1:T(8,128)(2,1)S(1)}, bf16[1024,64]{0,1:T(8,128)(2,1)}, u32[]{:S(2)}) copy-start(bf16[1024,64]{0,1:T(8,128)(2,1)} %param.17) | copy-start | bytes 393220
  7.2 22.2 %copy-start.16 = (s32[2,24]{1,0:T(2,128)S(1)}, s32[2,24]{1,0:T(2,128)}, u32[]{:S(2)}) copy-start(s32[2,24]{1,0:T(2,128)} %param.14) | copy-start | bytes 580
  7.2 22.3 %copy-start.13 = (s32[64,32]{0,1:T(8,128)S(1)}, s32[64,32]{0,1:T(8,128)}, u32[]{:S(2)}) copy-start(s32[64,32]{0,1:T(8,128)} %param.13) | copy-start | bytes 24580
  7.2 23.3 %copy-start.8 = (bf16[256,64]{0,1:T(8,128)(2,1)S(1)}, bf16[256,64]{0,1:T(8,128)(2,1)}, u32[]{:S(2)}) copy-start(bf16[256,64]{0,1:T(8,128)(2,1)} %param.11) | copy-start | bytes 98308
  7.2 23.6 %copy-start.14 = (bf16[128,64]{0,1:T(8,128)(2,1)S(1)}, bf16[128,64]{0,1:T(8,128)(2,1)}, u32[]{:S(2)}) copy-start(bf16[128,64]{0,1:T(8,128)(2,1)} %param.21) | copy-start | bytes 49156
  7.2 122.3 %all-gather.2.cloned.1.call-start = ((), (), s32[]{:S(2)}) async-start(), calls=%async_computation.4 | async-start | bytes 2129920 | tf_op jit(solution)/shard_map/all_gather | solution.py:47
  11.9 29.3 %all-to-all-start.1 = ((bf16[16,64,128]{2,1,0:T(8,128)(2,1)}), bf16[16,64,128]{2,1,0:T(8,128)(2,1)S(1)}, u32[]{:S(2)}, u32[]{:S(2)}) async-start(bf16[16,64,128]{2,1,0:T(8,128)(2,1)} %copy.40), calls=%async_computation.1 | async-start | bytes 524288 | tf_op jit(solution)/shard_map/all_to_all | solution.py:81
  32.5 40.1 %copy-start.1 = (bf16[2,24,128,128]{3,2,1,0:T(8,128)(2,1)S(1)}, bf16[2,24,128,128]{3,2,1,0:T(8,128)(2,1)}, u32[]{:S(2)}) copy-start(bf16[2,24,128,128]{3,2,1,0:T(8,128)(2,1)} %param.15) | copy-start | bytes 4718596
  41.2 0.7 copy-start.5
  41.9 42.8 %all-to-all-start = ((bf16[64,64,128]{2,1,0:T(8,128)(2,1)}), bf16[64,64,128]{2,1,0:T(8,128)(2,1)S(1)}, u32[]{:S(2)}, u32[]{:S(2)}) async-start(bf16[64,64,128]{2,1,0:T(8,128)(2,1)} %broadcast_select_fusion), calls=%async_computation | async-start | bytes 2097152 | tf_op jit(solution)/shard_map/all_to_all | solution.py:54
  72.6 2.9 %copy-start.2 = (bf16[1024,384]{1,0:T(8,128)(2,1)}, bf16[1024,384]{1,0:T(8,128)(2,1)S(1)}, u32[]{:S(2)}) copy-start(bf16[1024,384]{1,0:T(8,128)(2,1)S(1)} %all_gather.15) | copy-start | bytes 2359300
  73.1 1.6 copy-start.11
  77.8 10.5 %copy-start.3 = (bf16[2,128,2,128]{3,2,1,0:T(2,128)(2,1)S(1)}, bf16[2,128,2,128]{3,2,1,0:T(2,128)(2,1)}, u32[]{:S(2)}) copy-start(bf16[2,128,2,128]{3,2,1,0:T(2,128)(2,1)} %copy.37) | copy-start | bytes 393220
  77.8 10.5 %copy-start.9 = (bf16[256,64]{0,1:T(8,128)(2,1)S(1)}, bf16[256,64]{0,1:T(8,128)(2,1)}, u32[]{:S(2)}) copy-start(bf16[256,64]{0,1:T(8,128)(2,1)} %param.11) | copy-start | bytes 98308
  86.3 19.3 %copy-start.10 = (f32[256,64]{0,1:T(8,128)S(1)}, f32[256,64]{0,1:T(8,128)}, u32[]{:S(2)}) copy-start(f32[256,64]{0,1:T(8,128)} %fusion.53) | copy-start | bytes 196612
  86.3 19.5 %slice-start = ((bf16[1024,384]{1,0:T(8,128)(2,1)}), bf16[1024,256]{1,0:T(8,128)(2,1)S(1)}, s32[]{:S(2)}) async-start(bf16[1024,384]{1,0:T(8,128)(2,1)} %copy-done.2), calls=%async_computation.5 | async-start | bytes 1048576 | tf_op jit(solution)/shard_map/slice | solution.py:49
  86.3 19.6 %copy-start.4 = (bf16[2,128,2,128]{3,2,1,0:T(2,128)(2,1)S(1)}, bf16[2,128,2,128]{3,2,1,0:T(2,128)(2,1)}, u32[]{:S(2)}) copy-start(bf16[2,128,2,128]{3,2,1,0:T(2,128)(2,1)} %copy.37) | copy-start | bytes 393220
  86.3 19.6 %copy-start.12 = (f32[128,256]{1,0:T(8,128)S(1)}, f32[128,256]{1,0:T(8,128)}, u32[]{:S(2)}) copy-start(f32[128,256]{1,0:T(8,128)} %fusion.2) | copy-start | bytes 393220
  131.9 23.9 %copy-start.15 = (bf16[128,64]{0,1:T(8,128)(2,1)S(1)}, bf16[128,64]{0,1:T(8,128)(2,1)}, u32[]{:S(2)}) copy-start(bf16[128,64]{0,1:T(8,128)(2,1)} %param.21) | copy-start | bytes 49156
  131.9 23.9 %copy-start.17 = (s32[128]{0:T(128)S(1)}, s32[128]{0:T(128)}, u32[]{:S(2)}) copy-start(s32[128]{0:T(128)} %param.20) | copy-start | bytes 1540
  156.4 33.9 %copy-start.6 = (bf16[1024,64]{0,1:T(8,128)(2,1)S(1)}, bf16[1024,64]{0,1:T(8,128)(2,1)}, u32[]{:S(2)}) copy-start(bf16[1024,64]{0,1:T(8,128)(2,1)} %param.18) | copy-start | bytes 393220
  156.5 34.0 %copy-start.7 = (bf16[1024,64]{0,1:T(8,128)(2,1)S(1)}, bf16[1024,64]{0,1:T(8,128)(2,1)}, u32[]{:S(2)}) copy-start(bf16[1024,64]{0,1:T(8,128)(2,1)} %param.19) | copy-start | bytes 393220
  183.1 23.5 %all-to-all-start.3 = ((bf16[64,4,8,128]{3,2,1,0:T(8,128)(2,1)}), bf16[64,4,8,128]{3,2,1,0:T(8,128)(2,1)S(1)}, u32[]{:S(2)}, u32[]{:S(2)}) async-start(bf16[64,4,8,128]{3,2,1,0:T(8,128)(2,1)} %broadcast_in_dim.95), calls=%async_computation.3 | async-start | bytes 1048576 | tf_op jit(solution)/shard_map/all_to_all | solution.py:127
Sparse Core Ops, SparseCore 0:
  12.8 116.7 all-gather.1

commit v2 on v1

v2 whole, which is shorter than its diff:
```python
import jax
import jax.numpy as jnp
from jax import lax
from jax.experimental.layout import Layout, with_layout_constraint
from jax.sharding import PartitionSpec as P

BF = jnp.bfloat16
F32 = jnp.float32


def mm(a, b, dims):
    return lax.dot_general(a, b, (dims, ((), ())), preferred_element_type=F32)


def after(value, *others):
    return lax.optimization_barrier((value, *others))[0]


def on_device(
    node_feats,
    history,
    halo_blocks,
    tile_index,
    tile_weight,
    self_one,
    neigh_one,
    self_two,
    neigh_two,
    batch_ids,
    cotangent,
):
    own_blocks, tiles = tile_index.shape
    rows = tile_weight.shape[2]
    width = node_feats.shape[1]
    owned = node_feats.shape[0]
    parts = halo_blocks.shape[0]
    seeds = cotangent.shape[0]
    me = lax.axis_index("dom")

    feats_t = node_feats.T
    cot_t = cotangent.T
    self_one_t, neigh_one_t, self_two_t, neigh_two_t = (
        self_one.T,
        neigh_one.T,
        self_two.T,
        neigh_two.T,
    )

    second = jnp.any(halo_blocks == own_blocks * me + 1, axis=1)[:, None, None]

    def pick(array_t):
        return jnp.where(second, array_t[None, :, rows:], array_t[None, :, :rows])

    send_feats, self_two_t, neigh_two_t = lax.optimization_barrier(
        (pick(feats_t), self_two_t, neigh_two_t)
    )
    halo_feats = lax.all_to_all(send_feats, "dom", 0, 0, tiled=True)
    whole = lax.all_gather(jnp.concatenate([feats_t, cot_t], axis=1), "feat", axis=0, tiled=True)
    whole_feats, whole_cot = whole[:, :owned], whole[:, owned:]

    wanted = lax.dynamic_index_in_dim(halo_blocks, me, 0, keepdims=False)
    is_own = tile_index < own_blocks
    tile_block = wanted[jnp.clip(tile_index - own_blocks, 0, wanted.shape[0] - 1)]
    tile_owner = jnp.clip(tile_block // own_blocks, 0, parts - 1)

    onehot = tile_index[:, :, None] == jnp.arange(own_blocks, dtype=jnp.int32)[None, None, :]
    dense = jnp.sum(
        jnp.where(onehot[:, :, :, None, None], tile_weight[:, :, None].astype(F32), 0.0), axis=1
    )
    dense = dense.transpose(0, 2, 1, 3).reshape(owned, owned).astype(BF)
    row_total = jnp.sum(tile_weight, axis=(1, 3), dtype=F32).reshape(1, owned)
    inverse = 1.0 / row_total

    def halo_sum(picked):
        picked = jnp.where(is_own[:, :, None, None], jnp.zeros((), BF), picked)
        out = jnp.einsum("bkfc,bkvc->fbv", picked, tile_weight, preferred_element_type=F32)
        return out.reshape(width, owned)

    both = jnp.concatenate(
        [
            self_two_t.reshape(width, -1, width).transpose(1, 0, 2),
            neigh_two_t.reshape(width, -1, width).transpose(1, 0, 2),
        ],
        axis=2,
    )
    both = with_layout_constraint(both, Layout(major_to_minor=(0, 1, 2)))
    columns = lax.all_gather(both, "feat", axis=0, tiled=False)
    columns = lax.dynamic_index_in_dim(columns, lax.axis_index("feat"), 1, keepdims=False)
    columns = columns.reshape(-1, 2 * width)

    send_history = after(pick(history.T), whole, dense, inverse, halo_feats)
    halo_history = lax.all_to_all(send_history, "dom", 0, 0, tiled=True)

    mean_one = (halo_sum(halo_feats[tile_owner]) + mm(feats_t, dense, ((1,), (1,)))) * inverse
    whole_mean_one = lax.all_gather(mean_one.astype(BF), "feat", axis=0, tiled=True)
    pre_one = mm(self_one_t, whole_feats, ((1,), (0,))) + mm(
        neigh_one_t, whole_mean_one, ((1,), (0,))
    )
    gate = jax.nn.sigmoid(pre_one)
    hidden = (pre_one * gate).astype(BF)

    whole_hidden = lax.all_gather(hidden, "feat", axis=0, tiled=True)
    seed_rows = (
        batch_ids[:, None] == jnp.arange(owned, dtype=jnp.int32)[None, :]
    ).astype(BF)
    whole_grad_two = mm(whole_cot, seed_rows, ((1,), (0,))).astype(BF)
    grad_two = mm(cot_t, seed_rows, ((1,), (0,))).astype(BF)
    back = mm(columns, whole_grad_two, ((0,), (0,)))
    scaled = (back[width:] * inverse).astype(BF)
    own_grad = mm(scaled, dense, ((1,), (0,)))
    slope = gate * (1.0 + pre_one * (1.0 - gate))
    grad_one = ((back[:width] + own_grad) * slope).astype(BF)
    depth = self_one.shape[0]
    low, high = 8, width // 8
    wide = parts // high
    lanes = depth // wide

    def pieces_of(total):
        n = total.shape[1] // depth
        pieces = total.astype(BF).reshape(high, low, n, wide, lanes).transpose(0, 3, 2, 1, 4)
        return pieces.reshape(parts, n, low, lanes)

    def summed(pieces):
        got = lax.all_to_all(pieces, "dom", 0, 0, tiled=True)
        return jnp.sum(got.astype(F32), axis=0, keepdims=True).astype(BF)

    ones = mm(
        grad_one, jnp.concatenate([whole_feats, whole_mean_one], axis=0), ((1,), (1,))
    )
    self_part = mm(grad_two, whole_hidden, ((1,), (1,)))
    first = pieces_of(jnp.concatenate([ones, self_part], axis=1))
    halo_history = after(halo_history, whole_hidden, first)
    first = after(first, halo_history)
    halo_two = (halo_sum(halo_history[tile_owner]) * inverse).astype(BF)
    whole_halo_two = lax.all_gather(halo_two, "feat", axis=0, tiled=True)
    whole_mean_two = (
        mm(whole_hidden, dense, ((1,), (1,))) * inverse + whole_halo_two.astype(F32)
    ).astype(BF)
    node_out = mm(self_two_t, whole_hidden, ((1,), (0,))) + mm(
        neigh_two_t, whole_mean_two, ((1,), (0,))
    )

    last = pieces_of(mm(grad_two, whole_mean_two, ((1,), (1,))))
    first = summed(first)
    mine = jnp.concatenate([first, summed(after(last, first))], axis=1)
    spread = jnp.broadcast_to(mine, (parts, *mine.shape[1:]))
    sums = lax.all_to_all(spread, "dom", 0, 0, tiled=True)
    sums = sums.reshape(high, wide, -1, low, lanes).transpose(2, 0, 3, 1, 4)
    sums = sums.reshape(-1, width, depth).astype(F32)
    return (node_out.astype(BF).T, sums[0].T, sums[1].T, sums[2].T, sums[3].T)


def solution(mesh):
    return jax.shard_map(
        on_device,
        mesh=mesh,
        in_specs=(
            P("dom", "feat"),
            P("dom", "feat"),
            P(),
            P("dom", None),
            P("dom", None, None, None),
            P(None, "feat"),
            P(None, "feat"),
            P(None, "feat"),
            P(None, "feat"),
            P("dom"),
            P("dom", "feat"),
        ),
        out_specs=(
            P("dom", "feat"),
            P(None, "feat"),
            P(None, "feat"),
            P(None, "feat"),
            P(None, "feat"),
        ),
        check_vma=False,
    )
```

time: 218 us -> 215 us (0.986)
  the two profiles are of different devices: /device:TPU:1 before, /device:TPU:20 now
where the time goes in v2:
time: 215 us; the launch traced here: 214 us
  blocking collectives  97.5 us (45%)
  starting transfers between devices  51.7 us (24%)
  waiting for transfers between devices  20.9 us (10%)
  between operations  14.4 us (7%)
  local copies, waits for them, and re-layouts  13.5 us (6%)
  matrix products  11.1 us (5%)
  other arithmetic  4.77 us (2%)
    all_to_all x1, blocking collectives, summed(): got = lax.all_to_all(pieces, 'dom', 0, 0, tiled=True)  24.1 us
    all_to_all x1, starting transfers between devices, on_device(): halo_feats = lax.all_to_all(send_feats, 'dom', 0, 0, tiled=True)  22.9 us
    all_gather x1, blocking collectives, on_device(): lax.all_gather(jnp.concatenate([feats_t, cot_t], axis=1), 'feat', axis=0,...  22 us
    all_gather x1, blocking collectives, on_device(): lax.all_gather(mean_one.astype(BF), 'feat', axis=0, tiled=True)  18.3 us
    all_gather x1, blocking collectives, on_device(): whole_halo_two = lax.all_gather(halo_two, 'feat', axis=0, tiled=True)  17.4 us
    all_to_all x1, waiting for transfers between devices, on_device(): sums = lax.all_to_all(spread, 'dom', 0, 0, tiled=True)  17.2 us
    all_gather x1, blocking collectives, on_device(): whole_hidden = lax.all_gather(hidden, 'feat', axis=0, tiled=True)  15.7 us
    all_to_all x1, starting transfers between devices, summed(): got = lax.all_to_all(pieces, 'dom', 0, 0, tiled=True)  12.8 us
  transfers between devices with their start and end apart: 5, of which 2 were waited for; matrix products, arithmetic and copies ran while one was open for 9% of the time, Pallas kernels for 0%

profile of v2, /device:TPU:20, one launch (start us, length us, event | category | flops | bytes accessed | tf_op | source)
XLA Modules:
  0.0 213.9 jit_solution(16232866447695896710)
XLA Ops:
  7.3 0.8 fusion.43
  8.1 0.7 fusion.42
  8.8 0.7 compare_reduce_fusion
  9.6 1.6 broadcast_select_fusion
  11.7 0.9 pad_maximum_fusion.1
  12.6 22.9 %all-to-all-start = ((bf16[64,64,128]{2,1,0:T(8,128)(2,1)}), bf16[64,64,128]{2,1,0:T(8,128)(2,1)}, u32[]{:S(2)}, u32[]{:S(2)}) async-start(bf16[64,64,128]{2,1,0:T(8,128)(2,1)} %get-tuple-element.12), calls=%async_computation | async-start | bytes 2097152 | tf_op jit(solution)/shard_map/all_to_all | solution.py:57
  35.8 0.8 gather_fusion
  37.9 22.0 %all_gather.18 = bf16[1024,384]{1,0:T(8,128)(2,1)S(1)} all-gather(bf16[64,384]{1,0:T(8,128)(2,1)S(1)} %pad_maximum_fusion.2), channel_id=1, replica_groups=mesh['dom'=64,'feat'=16] {'feat'}, dimensions={0}, use_global_device_ids=true | all-gather | bytes 835584 | tf_op jit(solution)/shard_map/all_gather | solution.py:58
  59.9 0.9 slice.60
  61.1 0.8 convolution_convert_fusion.4
  62.2 3.7 %all-to-all-done = bf16[64,64,128]{2,1,0:T(8,128)(2,1)} async-done(((bf16[64,64,128]{2,1,0:T(8,128)(2,1)}), bf16[64,64,128]{2,1,0:T(8,128)(2,1)}, u32[]{:S(2)}, u32[]{:S(2)}) %all-to-all-start) | async-done | bytes 1048608 | tf_op jit(solution)/shard_map/all_to_all | solution.py:57
  65.9 9.7 %all-to-all-start.1 = ((bf16[64,64,128]{2,1,0:T(8,128)(2,1)}), bf16[64,64,128]{2,1,0:T(8,128)(2,1)}, u32[]{:S(2)}, u32[]{:S(2)}) async-start(bf16[64,64,128]{2,1,0:T(8,128)(2,1)} %get-tuple-element.14), calls=%async_computation.1 | async-start | bytes 2097152 | tf_op jit(solution)/shard_map/all_to_all | solution.py:92
  75.6 2.8 %gather_fusion.1 = bf16[48,64,128]{2,1,0:T(8,128)(2,1)} fusion(bf16[64,64,128]{2,1,0:T(8,128)(2,1)} %all-to-all-done, s32[1024]{0:T(1024)S(1)} %pad_clamp_fusion), kind=kCustom, calls=%fused_computation.1 | custom fusion | bytes 1573056 | tf_op jit(solution)/shard_map/gather | solution.py:94
  78.4 1.8 convolution_bitcast_fusion.2
  80.4 18.3 %all_gather.19 = bf16[1024,256]{1,0:T(8,128)(2,1)S(1)} all-gather(bf16[64,256]{1,0:T(8,128)(2,1)S(1)} %fusion.7), channel_id=1, replica_groups=mesh['dom'=64,'feat'=16] {'feat'}, dimensions={0}, use_global_device_ids=true | all-gather | bytes 557056 | tf_op jit(solution)/shard_map/all_gather | solution.py:95
  98.7 0.8 multiply_convert_fusion
  99.5 15.7 %all_gather.20 = bf16[1024,256]{1,0:T(8,128)(2,1)S(1)} all-gather(bf16[64,256]{1,0:T(8,128)(2,1)S(1)} %get-tuple-element.29), channel_id=1, replica_groups=mesh['dom'=64,'feat'=16] {'feat'}, dimensions={0}, use_global_device_ids=true | all-gather | bytes 557056 | tf_op jit(solution)/shard_map/all_gather | solution.py:102
  115.2 0.9 convolution_convert_fusion.3
  116.2 1.7 constant_dynamic-slice_fusion
  117.9 2.2 %fusion.2 = f32[128,256]{1,0:T(8,128)} fusion(bf16[1024,128]{1,0:T(8,128)(2,1)} %bitcast.113, bf16[1024,384]{1,0:T(8,128)(2,1)S(1)} %all_gather.18, s32[128]{0:T(128)S(1)} %copy-done.16), kind=kOutput, calls=%fused_computation.9 | convolution fusion | flops 134512640 | bytes 655872 | tf_op jit(solution)/shard_map/dot_general | solution.py:12
  120.1 1.8 convolution_convert_fusion
  121.9 0.8 copy.31
  122.7 1.9 gather_fusion.2
  124.7 12.8 %all-to-all-start.2 = ((bf16[64,3,8,128]{3,2,1,0:T(8,128)(2,1)}), bf16[64,3,8,128]{3,2,1,0:T(8,128)(2,1)S(1)}, u32[]{:S(2)}, u32[]{:S(2)}) async-start(bf16[64,3,8,128]{3,2,1,0:T(8,128)(2,1)} %bitcast.19), calls=%async_computation.2 | async-start | bytes 786432 | tf_op jit(solution)/shard_map/all_to_all | solution.py:124
  137.5 0.7 convolution_bitcast_fusion.1
  138.2 17.4 %all_gather.23 = bf16[1024,256]{1,0:T(8,128)(2,1)S(1)} all-gather(bf16[64,256]{1,0:T(8,128)(2,1)S(1)} %fusion.21), channel_id=1, replica_groups=mesh['dom'=64,'feat'=16] {'feat'}, dimensions={0}, use_global_device_ids=true | all-gather | bytes 557056 | tf_op jit(solution)/shard_map/all_gather | solution.py:135
  156.4 24.1 %all_to_all.25 = bf16[64,1,8,128]{3,2,1,0:T(8,128)(2,1)S(1)} all-to-all(bf16[64,1,8,128]{3,2,1,0:T(8,128)(2,1)S(1)} %bitcast.119), channel_id=1, replica_groups=mesh['dom'=64,'feat'=16] {'dom'}, dimensions={0} | all-to-all | bytes 262144 | tf_op jit(solution)/shard_map/all_to_all | solution.py:124
  180.5 0.9 broadcast_in_dim.112
  181.4 6.2 %all-to-all-start.4 = ((bf16[64,4,8,128]{3,2,1,0:T(8,128)(2,1)}), bf16[64,4,8,128]{3,2,1,0:T(8,128)(2,1)S(1)}, u32[]{:S(2)}, u32[]{:S(2)}) async-start(bf16[64,4,8,128]{3,2,1,0:T(8,128)(2,1)} %broadcast_in_dim.112), calls=%async_computation.4 | async-start | bytes 1048576 | tf_op jit(solution)/shard_map/all_to_all | solution.py:147
  187.8 0.8 fusion.9
  188.7 17.2 %all-to-all-done.4 = bf16[64,4,8,128]{3,2,1,0:T(8,128)(2,1)S(1)} async-done(((bf16[64,4,8,128]{3,2,1,0:T(8,128)(2,1)}), bf16[64,4,8,128]{3,2,1,0:T(8,128)(2,1)S(1)}, u32[]{:S(2)}, u32[]{:S(2)}) %all-to-all-start.4) | async-done | bytes 524320 | tf_op jit(solution)/shard_map/all_to_all | solution.py:147
  206.0 1.0 slice_bitcast_fusion
  (69 shorter events, 4.1 us)
Async XLA Ops:
  7.2 91.5 %copy-start = (bf16[1024,64]{0,1:T(8,128)(2,1)S(1)}, bf16[1024,64]{0,1:T(8,128)(2,1)}, u32[]{:S(2)}) copy-start(bf16[1024,64]{0,1:T(8,128)(2,1)} %param.17) | copy-start | bytes 393220
  7.2 3.9 %copy-start.4 = (bf16[1024,64]{0,1:T(8,128)(2,1)S(1)}, bf16[1024,64]{0,1:T(8,128)(2,1)}, u32[]{:S(2)}) copy-start(bf16[1024,64]{0,1:T(8,128)(2,1)} %param.18) | copy-start | bytes 393220
  7.2 4.1 %copy-start.6 = (bf16[1024,64]{0,1:T(8,128)(2,1)S(1)}, bf16[1024,64]{0,1:T(8,128)(2,1)}, u32[]{:S(2)}) copy-start(bf16[1024,64]{0,1:T(8,128)(2,1)} %param.19) | copy-start | bytes 393220
  7.2 109.0 %all-gather.3.cloned.1.call-start = ((), (), s32[]{:S(2)}) async-start(), calls=%async_computation.5 | async-start | bytes 4456448 | tf_op jit(solution)/shard_map/all_gather | solution.py:87
  11.5 23.9 %copy-start.15 = (s32[2,24]{1,0:T(2,128)S(1)}, s32[2,24]{1,0:T(2,128)}, u32[]{:S(2)}) copy-start(s32[2,24]{1,0:T(2,128)} %param.14) | copy-start | bytes 580
  11.5 24.0 %copy-start.13 = (s32[64,32]{0,1:T(8,128)S(1)}, s32[64,32]{0,1:T(8,128)}, u32[]{:S(2)}) copy-start(s32[64,32]{0,1:T(8,128)} %param.13) | copy-start | bytes 24580
  11.7 25.1 %copy-start.1 = (bf16[2,24,128,128]{3,2,1,0:T(8,128)(2,1)S(1)}, bf16[2,24,128,128]{3,2,1,0:T(8,128)(2,1)}, u32[]{:S(2)}) copy-start(bf16[2,24,128,128]{3,2,1,0:T(8,128)(2,1)} %param.15) | copy-start | bytes 4718596
  12.6 53.3 %all-to-all-start = ((bf16[64,64,128]{2,1,0:T(8,128)(2,1)}), bf16[64,64,128]{2,1,0:T(8,128)(2,1)}, u32[]{:S(2)}, u32[]{:S(2)}) async-start(bf16[64,64,128]{2,1,0:T(8,128)(2,1)} %get-tuple-element.12), calls=%async_computation | async-start | bytes 2097152 | tf_op jit(solution)/shard_map/all_to_all | solution.py:57
  37.2 0.8 copy-start.9
  37.2 0.8 copy-start.14
  37.7 23.4 %copy-start.16 = (s32[128]{0:T(128)S(1)}, s32[128]{0:T(128)}, u32[]{:S(2)}) copy-start(s32[128]{0:T(128)} %param.20) | copy-start | bytes 1540
  37.7 24.2 %copy-start.10 = (bf16[1024,64]{0,1:T(8,128)(2,1)S(1)}, bf16[1024,64]{0,1:T(8,128)(2,1)}, u32[]{:S(2)}) copy-start(bf16[1024,64]{0,1:T(8,128)(2,1)} %param.16) | copy-start | bytes 393220
  37.9 42.4 %copy-start.2 = (bf16[2,128,2,128]{3,2,1,0:T(2,128)(2,1)}, bf16[2,128,2,128]{3,2,1,0:T(2,128)(2,1)S(1)}, u32[]{:S(2)}) copy-start(bf16[2,128,2,128]{3,2,1,0:T(2,128)(2,1)S(1)} %copy.28) | copy-start | bytes 393220
  65.9 56.8 %all-to-all-start.1 = ((bf16[64,64,128]{2,1,0:T(8,128)(2,1)}), bf16[64,64,128]{2,1,0:T(8,128)(2,1)}, u32[]{:S(2)}, u32[]{:S(2)}) async-start(bf16[64,64,128]{2,1,0:T(8,128)(2,1)} %get-tuple-element.14), calls=%async_computation.1 | async-start | bytes 2097152 | tf_op jit(solution)/shard_map/all_to_all | solution.py:92
  78.4 36.8 %copy-start.11 = (bf16[256,64]{0,1:T(8,128)(2,1)S(1)}, bf16[256,64]{0,1:T(8,128)(2,1)}, u32[]{:S(2)}) copy-start(bf16[256,64]{0,1:T(8,128)(2,1)} %convolution_convert_fusion.4) | copy-start | bytes 98308
  120.1 1.8 copy-start.8
  124.6 31.0 %copy-start.3 = (bf16[2,128,2,128]{3,2,1,0:T(2,128)(2,1)S(1)}, bf16[2,128,2,128]{3,2,1,0:T(2,128)(2,1)}, u32[]{:S(2)}) copy-start(bf16[2,128,2,128]{3,2,1,0:T(2,128)(2,1)} %copy-done.2) | copy-start | bytes 393220
  124.7 31.6 %all-to-all-start.2 = ((bf16[64,3,8,128]{3,2,1,0:T(8,128)(2,1)}), bf16[64,3,8,128]{3,2,1,0:T(8,128)(2,1)S(1)}, u32[]{:S(2)}, u32[]{:S(2)}) async-start(bf16[64,3,8,128]{3,2,1,0:T(8,128)(2,1)} %bitcast.19), calls=%async_computation.2 | async-start | bytes 786432 | tf_op jit(solution)/shard_map/all_to_all | solution.py:124
  137.5 18.5 %copy-start.12 = (bf16[256,64]{0,1:T(8,128)(2,1)S(1)}, bf16[256,64]{0,1:T(8,128)(2,1)}, u32[]{:S(2)}) copy-start(bf16[256,64]{0,1:T(8,128)(2,1)} %convolution_convert_fusion.4) | copy-start | bytes 98308
  155.7 32.0 %copy-start.5 = (bf16[1024,64]{0,1:T(8,128)(2,1)S(1)}, bf16[1024,64]{0,1:T(8,128)(2,1)}, u32[]{:S(2)}) copy-start(bf16[1024,64]{0,1:T(8,128)(2,1)} %param.18) | copy-start | bytes 393220
  156.0 31.8 %copy-start.7 = (bf16[1024,64]{0,1:T(8,128)(2,1)S(1)}, bf16[1024,64]{0,1:T(8,128)(2,1)}, u32[]{:S(2)}) copy-start(bf16[1024,64]{0,1:T(8,128)(2,1)} %param.19) | copy-start | bytes 393220
  181.4 24.5 %all-to-all-start.4 = ((bf16[64,4,8,128]{3,2,1,0:T(8,128)(2,1)}), bf16[64,4,8,128]{3,2,1,0:T(8,128)(2,1)S(1)}, u32[]{:S(2)}, u32[]{:S(2)}) async-start(bf16[64,4,8,128]{3,2,1,0:T(8,128)(2,1)} %broadcast_in_dim.112), calls=%async_computation.4 | async-start | bytes 1048576 | tf_op jit(solution)/shard_map/all_to_all | solution.py:147
Sparse Core Ops, SparseCore 0:
  12.7 60.2 all-gather.2

commit v3 on v2

--- a/solution.py
+++ b/solution.py
@@ -51,13 +51,10 @@
     def pick(array_t):
         return jnp.where(second, array_t[None, :, rows:], array_t[None, :, :rows])
 
-    send_feats, self_two_t, neigh_two_t = lax.optimization_barrier(
-        (pick(feats_t), self_two_t, neigh_two_t)
+    send_feats, feats_t, self_two_t, neigh_two_t = lax.optimization_barrier(
+        (pick(feats_t), feats_t, self_two_t, neigh_two_t)
     )
     halo_feats = lax.all_to_all(send_feats, "dom", 0, 0, tiled=True)
-    whole = lax.all_gather(jnp.concatenate([feats_t, cot_t], axis=1), "feat", axis=0, tiled=True)
-    whole_feats, whole_cot = whole[:, :owned], whole[:, owned:]
-
     wanted = lax.dynamic_index_in_dim(halo_blocks, me, 0, keepdims=False)
     is_own = tile_index < own_blocks
     tile_block = wanted[jnp.clip(tile_index - own_blocks, 0, wanted.shape[0] - 1)]
@@ -76,19 +73,31 @@
         out = jnp.einsum("bkfc,bkvc->fbv", picked, tile_weight, preferred_element_type=F32)
         return out.reshape(width, owned)
 
-    both = jnp.concatenate(
+    side = jnp.concatenate(
         [
-            self_two_t.reshape(width, -1, width).transpose(1, 0, 2),
-            neigh_two_t.reshape(width, -1, width).transpose(1, 0, 2),
+            feats_t.reshape(width, own_blocks, rows).transpose(1, 0, 2),
+            cot_t.reshape(width, 1, seeds).transpose(1, 0, 2),
+            jnp.concatenate(
+                [
+                    self_two_t.reshape(width, -1, width).transpose(1, 0, 2),
+                    neigh_two_t.reshape(width, -1, width).transpose(1, 0, 2),
+                ],
+                axis=2,
+            ),
         ],
-        axis=2,
+        axis=0,
     )
-    both = with_layout_constraint(both, Layout(major_to_minor=(0, 1, 2)))
-    columns = lax.all_gather(both, "feat", axis=0, tiled=False)
-    columns = lax.dynamic_index_in_dim(columns, lax.axis_index("feat"), 1, keepdims=False)
-    columns = columns.reshape(-1, 2 * width)
+    side = with_layout_constraint(side, Layout(major_to_minor=(0, 1, 2)))
+    whole = lax.all_gather(side, "feat", axis=0, tiled=False)
+    whole_feats = jnp.concatenate(
+        [whole[:, i].reshape(-1, rows) for i in range(own_blocks)], axis=1
+    )
+    whole_cot = whole[:, own_blocks].reshape(-1, seeds)
+    columns = lax.dynamic_index_in_dim(
+        whole, own_blocks + 1 + lax.axis_index("feat"), 1, keepdims=False
+    ).reshape(-1, 2 * width)
 
-    send_history = after(pick(history.T), whole, dense, inverse, halo_feats)
+    send_history = after(pick(history.T), dense, inverse, halo_feats)
     halo_history = lax.all_to_all(send_history, "dom", 0, 0, tiled=True)
 
     mean_one = (halo_sum(halo_feats[tile_owner]) + mm(feats_t, dense, ((1,), (1,)))) * inverse
@@ -120,17 +129,7 @@
         pieces = total.astype(BF).reshape(high, low, n, wide, lanes).transpose(0, 3, 2, 1, 4)
         return pieces.reshape(parts, n, low, lanes)
 
-    def summed(pieces):
-        got = lax.all_to_all(pieces, "dom", 0, 0, tiled=True)
-        return jnp.sum(got.astype(F32), axis=0, keepdims=True).astype(BF)
-
-    ones = mm(
-        grad_one, jnp.concatenate([whole_feats, whole_mean_one], axis=0), ((1,), (1,))
-    )
-    self_part = mm(grad_two, whole_hidden, ((1,), (1,)))
-    first = pieces_of(jnp.concatenate([ones, self_part], axis=1))
-    halo_history = after(halo_history, whole_hidden, first)
-    first = after(first, halo_history)
+    halo_history = after(halo_history, whole_hidden)
     halo_two = (halo_sum(halo_history[tile_owner]) * inverse).astype(BF)
     whole_halo_two = lax.all_gather(halo_two, "feat", axis=0, tiled=True)
     whole_mean_two = (
@@ -140,9 +139,16 @@
         neigh_two_t, whole_mean_two, ((1,), (0,))
     )
 
-    last = pieces_of(mm(grad_two, whole_mean_two, ((1,), (1,))))
-    first = summed(first)
-    mine = jnp.concatenate([first, summed(after(last, first))], axis=1)
+    ones = mm(
+        grad_one, jnp.concatenate([whole_feats, whole_mean_one], axis=0), ((1,), (1,))
+    )
+    twos = mm(
+        grad_two, jnp.concatenate([whole_hidden, whole_mean_two], axis=0), ((1,), (1,))
+    )
+    mine = lax.all_to_all(
+        pieces_of(jnp.concatenate([ones, twos], axis=1)), "dom", 0, 0, tiled=True
+    )
+    mine = jnp.sum(mine.astype(F32), axis=0, keepdims=True).astype(BF)
     spread = jnp.broadcast_to(mine, (parts, *mine.shape[1:]))
     sums = lax.all_to_all(spread, "dom", 0, 0, tiled=True)
     sums = sums.reshape(high, wide, -1, low, lanes).transpose(2, 0, 3, 1, 4)

time: 215 us -> 205 us (0.953)
  the two profiles are of different devices: /device:TPU:20 before, /device:TPU:1 now
where the time goes in v3:
time: 205 us; the launch traced here: 202 us
  blocking collectives  83.7 us (41%)
  starting transfers between devices  39.7 us (19%)
  waiting for transfers between devices  38.2 us (19%)
  between operations  14.5 us (7%)
  local copies, waits for them, and re-layouts  10.4 us (5%)
  matrix products  8.67 us (4%)
  other arithmetic  6.41 us (3%)
    all_to_all x1, blocking collectives, on_device(): lax.all_to_all(pieces_of(jnp.concatenate([ones, twos], axis=1)), 'dom', 0...  29.6 us
    all_to_all x1, starting transfers between devices, on_device(): halo_feats = lax.all_to_all(send_feats, 'dom', 0, 0, tiled=True)  23.2 us
    all_to_all x1, waiting for transfers between devices, on_device(): halo_feats = lax.all_to_all(send_feats, 'dom', 0, 0, tiled=True)  22.9 us
    all_gather x1, blocking collectives, on_device(): lax.all_gather(mean_one.astype(BF), 'feat', axis=0, tiled=True)  20.9 us
    all_gather x1, blocking collectives, on_device(): whole_halo_two = lax.all_gather(halo_two, 'feat', axis=0, tiled=True)  17.2 us
    all_gather x1, blocking collectives, on_device(): whole_hidden = lax.all_gather(hidden, 'feat', axis=0, tiled=True)  16 us
    all_to_all x1, waiting for transfers between devices, on_device(): sums = lax.all_to_all(spread, 'dom', 0, 0, tiled=True)  15.3 us
    all_to_all x1, starting transfers between devices, on_device(): halo_history = lax.all_to_all(send_history, 'dom', 0, 0, tiled=True)  9.37 us
  transfers between devices with their start and end apart: 4, of which 2 were waited for; matrix products, arithmetic and copies ran while one was open for 6% of the time, Pallas kernels for 0%

profile of v3, /device:TPU:1, one launch (start us, length us, event | category | flops | bytes accessed | tf_op | source)
XLA Modules:
  0.0 201.6 jit_solution(9777400464017686726)
XLA Ops:
  7.3 0.9 fusion.50
  8.1 0.7 compare_reduce_fusion
  8.9 1.6 broadcast_select_fusion
  11.0 0.9 maximum_maximum_fusion
  11.9 23.2 %all-to-all-start = ((bf16[64,64,128]{2,1,0:T(8,128)(2,1)}), bf16[64,64,128]{2,1,0:T(8,128)(2,1)S(1)}, u32[]{:S(2)}, u32[]{:S(2)}) async-start(bf16[64,64,128]{2,1,0:T(8,128)(2,1)} %get-tuple-element.14), calls=%async_computation | async-start | bytes 2097152 | tf_op jit(solution)/shard_map/all_to_all | solution.py:57
  35.4 0.8 gather_fusion
  36.4 0.4 convert_element_type.69
  36.8 0.5 select_reduce_fusion
  37.4 0.8 copy.38
  38.4 0.5 broadcast_compare_fusion
  38.9 22.9 %all-to-all-done = bf16[64,64,128]{2,1,0:T(8,128)(2,1)S(1)} async-done(((bf16[64,64,128]{2,1,0:T(8,128)(2,1)}), bf16[64,64,128]{2,1,0:T(8,128)(2,1)S(1)}, u32[]{:S(2)}, u32[]{:S(2)}) %all-to-all-start) | async-done | bytes 1048608 | tf_op jit(solution)/shard_map/all_to_all | solution.py:57
  61.8 9.4 %all-to-all-start.1 = ((bf16[64,64,128]{2,1,0:T(8,128)(2,1)}), bf16[64,64,128]{2,1,0:T(8,128)(2,1)}, u32[]{:S(2)}, u32[]{:S(2)}) async-start(bf16[64,64,128]{2,1,0:T(8,128)(2,1)} %get-tuple-element.15), calls=%async_computation.1 | async-start | bytes 2097152 | tf_op jit(solution)/shard_map/all_to_all | solution.py:101
  71.2 0.6 pad_clamp_fusion
  71.8 0.6 divide_bitcast_fusion
  72.4 0.8 gather_fusion.1
  73.3 1.4 convolution_bitcast_fusion.1
  74.9 20.9 %all_gather.17 = bf16[1024,256]{1,0:T(8,128)(2,1)S(1)} all-gather(bf16[64,256]{1,0:T(8,128)(2,1)S(1)} %fusion.6), channel_id=1, replica_groups=mesh['dom'=64,'feat'=16] {'feat'}, dimensions={0}, use_global_device_ids=true | all-gather | bytes 557056 | tf_op jit(solution)/shard_map/all_gather | solution.py:104
  95.7 2.1 %fusion.49 = (bf16[16,1,64,128]{3,2,1,0:T(8,128)(2,1)}, bf16[16,1,64,128]{3,2,1,0:T(8,128)(2,1)S(1)}, bf16[16,1,64,128]{3,2,1,0:T(8,128)(2,1)}, bf16[16,1,64,128]{3,2,1,0:T(8,128)(2,1)S(1)}) fusion(bf16[16,19,64,128]{3,2,1,0:T(8,128)(2,1)} %bitcast.128, s32[]{:T(128)S(6)} %select_n.61), kind=kLoop, calls=%fused_computation.93 | loop fusion | bytes 2097156 | tf_op jit(solution)/shard_map/slice | solution.py:95
  98.0 0.8 multiply_convert_fusion
  98.9 16.0 %all_gather.18 = bf16[1024,256]{1,0:T(8,128)(2,1)S(1)} all-gather(bf16[64,256]{1,0:T(8,128)(2,1)S(1)} %get-tuple-element.31), channel_id=1, replica_groups=mesh['dom'=64,'feat'=16] {'feat'}, dimensions={0}, use_global_device_ids=true | all-gather | bytes 557056 | tf_op jit(solution)/shard_map/all_gather | solution.py:111
  114.9 2.0 %gather_fusion.2 = bf16[48,64,128]{2,1,0:T(8,128)(2,1)S(1)} fusion(bf16[64,64,128]{2,1,0:T(8,128)(2,1)} %all-to-all-done.1, s32[1024]{0:T(1024)} %pad_clamp_fusion), kind=kCustom, calls=%fused_computation.2 | custom fusion | bytes 1573056 | tf_op jit(solution)/shard_map/gather | solution.py:133
  117.0 1.4 convolution_bitcast_fusion
  118.4 17.2 %all_gather.19 = bf16[1024,256]{1,0:T(8,128)(2,1)S(1)} all-gather(bf16[64,256]{1,0:T(8,128)(2,1)S(1)} %fusion.27), channel_id=1, replica_groups=mesh['dom'=64,'feat'=16] {'feat'}, dimensions={0}, use_global_device_ids=true | all-gather | bytes 557056 | tf_op jit(solution)/shard_map/all_gather | solution.py:134
  136.0 1.3 convolution_convert_fusion
  137.3 0.6 fusion.2
  138.0 1.4 convolution_convert_fusion.1
  139.6 29.6 %all_to_all.20 = bf16[64,4,8,128]{3,2,1,0:T(8,128)(2,1)S(1)} all-to-all(bf16[64,4,8,128]{3,2,1,0:T(8,128)(2,1)S(1)} %bitcast.108), channel_id=1, replica_groups=mesh['dom'=64,'feat'=16] {'dom'}, dimensions={0} | all-to-all | bytes 1048576 | tf_op jit(solution)/shard_map/all_to_all | solution.py:148
  169.2 0.9 broadcast_in_dim.108
  170.1 7.2 %all-to-all-start.3 = ((bf16[64,4,8,128]{3,2,1,0:T(8,128)(2,1)}), bf16[64,4,8,128]{3,2,1,0:T(8,128)(2,1)S(1)}, u32[]{:S(2)}, u32[]{:S(2)}) async-start(bf16[64,4,8,128]{3,2,1,0:T(8,128)(2,1)} %broadcast_in_dim.108), calls=%async_computation.3 | async-start | bytes 1048576 | tf_op jit(solution)/shard_map/all_to_all | solution.py:153
  177.5 0.8 fusion.8
  178.4 15.3 %all-to-all-done.3 = bf16[64,4,8,128]{3,2,1,0:T(8,128)(2,1)S(1)} async-done(((bf16[64,4,8,128]{3,2,1,0:T(8,128)(2,1)}), bf16[64,4,8,128]{3,2,1,0:T(8,128)(2,1)S(1)}, u32[]{:S(2)}, u32[]{:S(2)}) %all-to-all-start.3) | async-done | bytes 524320 | tf_op jit(solution)/shard_map/all_to_all | solution.py:153
  193.7 1.0 slice_bitcast_fusion
  (77 shorter events, 2.8 us)
Async XLA Ops:
  7.2 90.9 %copy-start = (bf16[1024,64]{0,1:T(8,128)(2,1)S(1)}, bf16[1024,64]{0,1:T(8,128)(2,1)}, u32[]{:S(2)}) copy-start(bf16[1024,64]{0,1:T(8,128)(2,1)} %param.17) | copy-start | bytes 393220
  7.2 3.8 %copy-start.11 = (bf16[256,64]{0,1:T(8,128)(2,1)S(1)}, bf16[256,64]{0,1:T(8,128)(2,1)}, u32[]{:S(2)}) copy-start(bf16[256,64]{0,1:T(8,128)(2,1)} %param.11) | copy-start | bytes 98308
  7.2 3.5 %copy-start.7 = (bf16[1024,64]{0,1:T(8,128)(2,1)S(1)}, bf16[1024,64]{0,1:T(8,128)(2,1)}, u32[]{:S(2)}) copy-start(bf16[1024,64]{0,1:T(8,128)(2,1)} %param.18) | copy-start | bytes 393220
  7.2 3.2 %copy-start.9 = (bf16[1024,64]{0,1:T(8,128)(2,1)S(1)}, bf16[1024,64]{0,1:T(8,128)(2,1)}, u32[]{:S(2)}) copy-start(bf16[1024,64]{0,1:T(8,128)(2,1)} %param.19) | copy-start | bytes 393220
  7.2 88.5 %all-gather.3.cloned.1.call-start = ((), (), s32[]{:S(2)}) async-start(), calls=%async_computation.4 | async-start | bytes 5292032 | tf_op jit(solution)/shard_map/all_gather | solution.py:91
  7.3 3.8 %copy-start.19 = (bf16[128,64]{0,1:T(8,128)(2,1)S(1)}, bf16[128,64]{0,1:T(8,128)(2,1)}, u32[]{:S(2)}) copy-start(bf16[128,64]{0,1:T(8,128)(2,1)} %param.21) | copy-start | bytes 49156
  10.7 24.4 %copy-start.22 = (s32[2,24]{1,0:T(2,128)S(1)}, s32[2,24]{1,0:T(2,128)}, u32[]{:S(2)}) copy-start(s32[2,24]{1,0:T(2,128)} %param.14) | copy-start | bytes 580
  10.7 24.5 %copy-start.18 = (s32[64,32]{0,1:T(8,128)S(1)}, s32[64,32]{0,1:T(8,128)}, u32[]{:S(2)}) copy-start(s32[64,32]{0,1:T(8,128)} %param.13) | copy-start | bytes 24580
  11.0 25.3 %copy-start.1 = (bf16[2,24,128,128]{3,2,1,0:T(8,128)(2,1)S(1)}, bf16[2,24,128,128]{3,2,1,0:T(8,128)(2,1)}, u32[]{:S(2)}) copy-start(bf16[2,24,128,128]{3,2,1,0:T(8,128)(2,1)} %param.15) | copy-start | bytes 4718596
  11.9 49.9 %all-to-all-start = ((bf16[64,64,128]{2,1,0:T(8,128)(2,1)}), bf16[64,64,128]{2,1,0:T(8,128)(2,1)S(1)}, u32[]{:S(2)}, u32[]{:S(2)}) async-start(bf16[64,64,128]{2,1,0:T(8,128)(2,1)} %get-tuple-element.14), calls=%async_computation | async-start | bytes 2097152 | tf_op jit(solution)/shard_map/all_to_all | solution.py:57
  61.8 53.1 %all-to-all-start.1 = ((bf16[64,64,128]{2,1,0:T(8,128)(2,1)}), bf16[64,64,128]{2,1,0:T(8,128)(2,1)}, u32[]{:S(2)}, u32[]{:S(2)}) async-start(bf16[64,64,128]{2,1,0:T(8,128)(2,1)} %get-tuple-element.15), calls=%async_computation.1 | async-start | bytes 2097152 | tf_op jit(solution)/shard_map/all_to_all | solution.py:101
  73.2 1.5 copy-start.2
  73.2 1.5 copy-start.12
  73.2 1.5 copy-start.20
  74.7 23.1 %copy-start.24 = (bf16[1024,64]{0,1:T(8,128)(2,1)S(1)}, bf16[1024,64]{0,1:T(8,128)(2,1)}, u32[]{:S(2)}) copy-start(bf16[1024,64]{0,1:T(8,128)(2,1)} %param.16) | copy-start | bytes 393220
  97.8 1.1 copy-start.13
  97.8 1.1 copy-start.15
  116.9 1.4 copy-start.21
  117.0 18.7 %copy-start.3 = (bf16[2,128,2,128]{3,2,1,0:T(2,128)(2,1)S(1)}, bf16[2,128,2,128]{3,2,1,0:T(2,128)(2,1)}, u32[]{:S(2)}) copy-start(bf16[2,128,2,128]{3,2,1,0:T(2,128)(2,1)} %copy.38) | copy-start | bytes 393220
  118.4 17.7 %copy-start.23 = (s32[128]{0:T(128)S(1)}, s32[128]{0:T(128)}, u32[]{:S(2)}) copy-start(s32[128]{0:T(128)} %param.20) | copy-start | bytes 1540
  118.4 19.0 %copy-start.5 = (bf16[16,1,64,128]{3,2,1,0:T(8,128)(2,1)S(1)}, bf16[16,1,64,128]{3,2,1,0:T(8,128)(2,1)}, u32[]{:S(2)}) copy-start(bf16[16,1,64,128]{3,2,1,0:T(8,128)(2,1)} %get-tuple-element.17) | copy-start | bytes 786436
  118.4 18.9 %copy-start.6 = (bf16[16,1,64,128]{3,2,1,0:T(8,128)(2,1)S(1)}, bf16[16,1,64,128]{3,2,1,0:T(8,128)(2,1)}, u32[]{:S(2)}) copy-start(bf16[16,1,64,128]{3,2,1,0:T(8,128)(2,1)} %get-tuple-element.19) | copy-start | bytes 786436
  135.7 2.3 %copy-start.4 = (bf16[2,128,2,128]{3,2,1,0:T(2,128)(2,1)S(1)}, bf16[2,128,2,128]{3,2,1,0:T(2,128)(2,1)}, u32[]{:S(2)}) copy-start(bf16[2,128,2,128]{3,2,1,0:T(2,128)(2,1)} %copy.38) | copy-start | bytes 393220
  135.7 2.3 %copy-start.14 = (bf16[16,1,64,128]{3,2,1,0:T(8,128)(2,1)S(1)}, bf16[16,1,64,128]{3,2,1,0:T(8,128)(2,1)}, u32[]{:S(2)}) copy-start(bf16[16,1,64,128]{3,2,1,0:T(8,128)(2,1)} %copy-done.13) | copy-start | bytes 786436
  135.7 2.3 %copy-start.16 = (bf16[16,1,64,128]{3,2,1,0:T(8,128)(2,1)S(1)}, bf16[16,1,64,128]{3,2,1,0:T(8,128)(2,1)}, u32[]{:S(2)}) copy-start(bf16[16,1,64,128]{3,2,1,0:T(8,128)(2,1)} %copy-done.15) | copy-start | bytes 786436
  138.0 1.5 copy-start.17
  139.5 37.8 %copy-start.8 = (bf16[1024,64]{0,1:T(8,128)(2,1)S(1)}, bf16[1024,64]{0,1:T(8,128)(2,1)}, u32[]{:S(2)}) copy-start(bf16[1024,64]{0,1:T(8,128)(2,1)} %param.18) | copy-start | bytes 393220
  139.6 38.0 %copy-start.10 = (bf16[1024,64]{0,1:T(8,128)(2,1)S(1)}, bf16[1024,64]{0,1:T(8,128)(2,1)}, u32[]{:S(2)}) copy-start(bf16[1024,64]{0,1:T(8,128)(2,1)} %param.19) | copy-start | bytes 393220
  170.1 23.5 %all-to-all-start.3 = ((bf16[64,4,8,128]{3,2,1,0:T(8,128)(2,1)}), bf16[64,4,8,128]{3,2,1,0:T(8,128)(2,1)S(1)}, u32[]{:S(2)}, u32[]{:S(2)}) async-start(bf16[64,4,8,128]{3,2,1,0:T(8,128)(2,1)} %broadcast_in_dim.108), calls=%async_computation.3 | async-start | bytes 1048576 | tf_op jit(solution)/shard_map/all_to_all | solution.py:153
Sparse Core Ops, SparseCore 0:
  12.1 60.8 all-gather.2

commit v4 on v3

--- a/solution.py
+++ b/solution.py
@@ -1,6 +1,7 @@
 import jax
 import jax.numpy as jnp
 from jax import lax
+from jax.experimental import pallas as pl
 from jax.experimental.layout import Layout, with_layout_constraint
 from jax.sharding import PartitionSpec as P
 
@@ -14,6 +15,33 @@
 
 def after(value, *others):
     return lax.optimization_barrier((value, *others))[0]
+
+
+def add_and_copy(got_ref, out_ref):
+    total = jnp.sum(got_ref[...].astype(F32), axis=0, keepdims=True)
+    out_ref[...] = jnp.broadcast_to(total.astype(out_ref.dtype), out_ref.shape)
+
+
+def unpack(sums_ref, self_one_ref, neigh_one_ref, self_two_ref, neigh_two_ref):
+    parts, _, low, lanes = sums_ref.shape
+    width, depth = self_one_ref.shape
+    high = width // low
+    wide = depth // lanes
+    for i in range(high):
+        down = slice(i * low, (i + 1) * low)
+        for j in range(wide):
+            across = slice(j * lanes, (j + 1) * lanes)
+            base = i * 2 * wide + j
+            self_one_ref[down, across] = sums_ref[base, 0].astype(F32)
+            neigh_one_ref[down, across] = sums_ref[base + wide, 0].astype(F32)
+            left = sums_ref[2 * j * high + i, 1].astype(F32)
+            right = sums_ref[(2 * j + 1) * high + i, 1].astype(F32)
+            self_two_ref[down, across] = jnp.concatenate(
+                [left[:, :width], right[:, :width]], axis=1
+            )
+            neigh_two_ref[down, across] = jnp.concatenate(
+                [left[:, width:], right[:, width:]], axis=1
+            )
 
 
 def on_device(
@@ -108,52 +136,49 @@
     gate = jax.nn.sigmoid(pre_one)
     hidden = (pre_one * gate).astype(BF)
 
-    whole_hidden = lax.all_gather(hidden, "feat", axis=0, tiled=True)
     seed_rows = (
         batch_ids[:, None] == jnp.arange(owned, dtype=jnp.int32)[None, :]
     ).astype(BF)
     whole_grad_two = mm(whole_cot, seed_rows, ((1,), (0,))).astype(BF)
-    grad_two = mm(cot_t, seed_rows, ((1,), (0,))).astype(BF)
     back = mm(columns, whole_grad_two, ((0,), (0,)))
     scaled = (back[width:] * inverse).astype(BF)
     own_grad = mm(scaled, dense, ((1,), (0,)))
     slope = gate * (1.0 + pre_one * (1.0 - gate))
     grad_one = ((back[:width] + own_grad) * slope).astype(BF)
+    ones = mm(
+        grad_one, jnp.concatenate([whole_feats, whole_mean_one], axis=0), ((1,), (1,))
+    )
     depth = self_one.shape[0]
-    low, high = 8, width // 8
-    wide = parts // high
-    lanes = depth // wide
-
-    def pieces_of(total):
-        n = total.shape[1] // depth
-        pieces = total.astype(BF).reshape(high, low, n, wide, lanes).transpose(0, 3, 2, 1, 4)
-        return pieces.reshape(parts, n, low, lanes)
-
-    halo_history = after(halo_history, whole_hidden)
-    halo_two = (halo_sum(halo_history[tile_owner]) * inverse).astype(BF)
-    whole_halo_two = lax.all_gather(halo_two, "feat", axis=0, tiled=True)
-    whole_mean_two = (
-        mm(whole_hidden, dense, ((1,), (1,))) * inverse + whole_halo_two.astype(F32)
+    lanes = 2 * width
+    high = parts * lanes // (2 * depth)
+    low = width // high
+    ones = ones.astype(BF).reshape(high, low, 2 * depth // lanes, lanes).transpose(0, 2, 1, 3)
+    ones = ones.reshape(parts, 1, low, lanes)
+
+    halo_history = after(halo_history, ones)
+    mean_two = (
+        (halo_sum(halo_history[tile_owner]) + mm(hidden, dense, ((1,), (1,)))) * inverse
     ).astype(BF)
+    layer_two = jnp.concatenate([hidden, mean_two], axis=0)
+
+    twos = mm(whole_grad_two, layer_two, ((1,), (1,))).astype(BF)
+    slices = depth // width
+    twos = lax.all_to_all(twos.reshape(slices, width, 2 * width), "feat", 0, 0, tiled=True)
+    whole_two = lax.all_gather(after(layer_two, twos), "feat", axis=0, tiled=False)
+    pieces = jnp.concatenate([ones, twos.reshape(parts, 1, low, lanes)], axis=1)
+    got = lax.all_to_all(pieces, "dom", 0, 0, tiled=True)
+    spread = pl.pallas_call(add_and_copy, out_shape=jax.ShapeDtypeStruct(got.shape, BF))(got)
+    sums = lax.all_to_all(spread, "dom", 0, 0, tiled=True)
+    grads = pl.pallas_call(
+        unpack, out_shape=[jax.ShapeDtypeStruct((width, depth), F32)] * 4
+    )(sums)
+
+    whole_hidden = whole_two[:, :width].reshape(depth, owned)
+    whole_mean_two = whole_two[:, width:].reshape(depth, owned)
     node_out = mm(self_two_t, whole_hidden, ((1,), (0,))) + mm(
         neigh_two_t, whole_mean_two, ((1,), (0,))
     )
-
-    ones = mm(
-        grad_one, jnp.concatenate([whole_feats, whole_mean_one], axis=0), ((1,), (1,))
-    )
-    twos = mm(
-        grad_two, jnp.concatenate([whole_hidden, whole_mean_two], axis=0), ((1,), (1,))
-    )
-    mine = lax.all_to_all(
-        pieces_of(jnp.concatenate([ones, twos], axis=1)), "dom", 0, 0, tiled=True
-    )
-    mine = jnp.sum(mine.astype(F32), axis=0, keepdims=True).astype(BF)
-    spread = jnp.broadcast_to(mine, (parts, *mine.shape[1:]))
-    sums = lax.all_to_all(spread, "dom", 0, 0, tiled=True)
-    sums = sums.reshape(high, wide, -1, low, lanes).transpose(2, 0, 3, 1, 4)
-    sums = sums.reshape(-1, width, depth).astype(F32)
-    return (node_out.astype(BF).T, sums[0].T, sums[1].T, sums[2].T, sums[3].T)
+    return (node_out.astype(BF).T, *[grad.T for grad in grads])
 
 
 def solution(mesh):

time: 205 us -> 188 us (0.917)
  blocking collectives: 83.7 us -> 46.2 us
  waiting for transfers between devices: 38.2 us -> 48.4 us
  starting transfers between devices: 39.7 us -> 48.3 us
  Pallas kernels: 0 us -> 4.07 us
    all_gather x2 -> x0, blocking collectives: 33.2 us -> none  [the longest x1 17.2 us: on_device(): whole_halo_two = lax.all_gather(halo_two, 'feat', axis=0, tiled=True)]
    all_to_all x0 -> x1, waiting for transfers between devices: none -> 11 us  [on_device(): lax.all_to_all(twos.reshape(slices, width, 2 * width), 'feat', 0, 0, tile...]
    all_to_all x0 -> x1, starting transfers between devices: none -> 9.16 us  [on_device(): lax.all_to_all(twos.reshape(slices, width, 2 * width), 'feat', 0, 0, tile...]
    all_to_all x1, blocking collectives: 29.6 us -> 25.4 us  [on_device(): got = lax.all_to_all(pieces, 'dom', 0, 0, tiled=True)]
    pallas_call x0 -> x2, Pallas kernels: none -> 4.07 us  [the longest x1 2.09 us: on_device(): pl.pallas_call(unpack, out_shape=[jax.ShapeDtypeStruct((width, depth), F3...]
    all_to_all x1, waiting for transfers between devices: 15.3 us -> 12.7 us  [on_device(): sums = lax.all_to_all(spread, 'dom', 0, 0, tiled=True)]
    dot_general x9 -> x10, matrix products: 5.87 us -> 6.21 us  [mm(): return lax.dot_general(a, b, (dims, ((), ())), preferred_element_type=F32)]
  transfers between devices with their start and end apart: 4 -> 6, of which waited for: 2 -> 4; matrix products, arithmetic and copies ran while one was open for 6% -> 8% of each run, Pallas kernels for 0% -> 1%
where the time goes in v4:
time: 188 us; the launch traced here: 185 us
  waiting for transfers between devices  48.4 us (26%)
  starting transfers between devices  48.3 us (26%)
  blocking collectives  46.2 us (25%)
  between operations  14.4 us (8%)
  local copies, waits for them, and re-layouts  10.6 us (6%)
  matrix products  7.61 us (4%)
  other arithmetic  5.14 us (3%)
  Pallas kernels  4.07 us (2%)
    all_to_all x1, blocking collectives, on_device(): got = lax.all_to_all(pieces, 'dom', 0, 0, tiled=True)  25.4 us
    all_to_all x1, waiting for transfers between devices, on_device(): halo_feats = lax.all_to_all(send_feats, 'dom', 0, 0, tiled=True)  23.4 us
    all_to_all x1, starting transfers between devices, on_device(): halo_feats = lax.all_to_all(send_feats, 'dom', 0, 0, tiled=True)  23.2 us
    all_gather x1, blocking collectives, on_device(): lax.all_gather(mean_one.astype(BF), 'feat', axis=0, tiled=True)  20.9 us
    all_to_all x1, waiting for transfers between devices, on_device(): sums = lax.all_to_all(spread, 'dom', 0, 0, tiled=True)  12.7 us
    all_to_all x1, waiting for transfers between devices, on_device(): lax.all_to_all(twos.reshape(slices, width, 2 * width), 'feat', 0, 0, tile...  11 us
    all_to_all x1, starting transfers between devices, on_device(): halo_history = lax.all_to_all(send_history, 'dom', 0, 0, tiled=True)  9.37 us
    all_to_all x1, starting transfers between devices, on_device(): lax.all_to_all(twos.reshape(slices, width, 2 * width), 'feat', 0, 0, tile...  9.16 us
  transfers between devices with their start and end apart: 6, of which 4 were waited for; matrix products, arithmetic and copies ran while one was open for 8% of the time, Pallas kernels for 1%

profile of v4, /device:TPU:1, one launch (start us, length us, event | category | flops | bytes accessed | tf_op | source)
XLA Modules:
  0.0 184.9 jit_solution(16064251794386383417)
XLA Ops:
  7.3 0.9 fusion.43
  8.1 0.7 compare_reduce_fusion
  8.9 1.6 broadcast_select_fusion
  11.0 0.9 maximum_maximum_fusion
  11.9 23.2 %all-to-all-start = ((bf16[64,64,128]{2,1,0:T(8,128)(2,1)}), bf16[64,64,128]{2,1,0:T(8,128)(2,1)S(1)}, u32[]{:S(2)}, u32[]{:S(2)}) async-start(bf16[64,64,128]{2,1,0:T(8,128)(2,1)} %get-tuple-element.19), calls=%async_computation | async-start | bytes 2097152 | tf_op jit(solution)/shard_map/all_to_all | solution.py:85
  35.4 0.8 gather_fusion
  36.8 0.5 select_reduce_fusion
  37.4 0.8 copy.39
  38.5 23.4 %all-to-all-done = bf16[64,64,128]{2,1,0:T(8,128)(2,1)S(1)} async-done(((bf16[64,64,128]{2,1,0:T(8,128)(2,1)}), bf16[64,64,128]{2,1,0:T(8,128)(2,1)S(1)}, u32[]{:S(2)}, u32[]{:S(2)}) %all-to-all-start) | async-done | bytes 1048608 | tf_op jit(solution)/shard_map/all_to_all | solution.py:85
  61.8 9.4 %all-to-all-start.1 = ((bf16[64,64,128]{2,1,0:T(8,128)(2,1)}), bf16[64,64,128]{2,1,0:T(8,128)(2,1)}, u32[]{:S(2)}, u32[]{:S(2)}) async-start(bf16[64,64,128]{2,1,0:T(8,128)(2,1)} %get-tuple-element.20), calls=%async_computation.1 | async-start | bytes 2097152 | tf_op jit(solution)/shard_map/all_to_all | solution.py:129
  71.2 0.7 gather_fusion.1
  72.0 0.7 convolution_bitcast_fusion.1
  73.0 20.9 %all_gather.17 = bf16[1024,256]{1,0:T(8,128)(2,1)S(1)} all-gather(bf16[64,256]{1,0:T(8,128)(2,1)S(1)} %fusion.5), channel_id=1, replica_groups=mesh['dom'=64,'feat'=16] {'feat'}, dimensions={0}, use_global_device_ids=true | all-gather | bytes 557056 | tf_op jit(solution)/shard_map/all_gather | solution.py:132
  93.9 1.3 fusion.41
  96.0 0.9 fusion.45
  96.9 2.1 %fusion = bf16[8,8,16,128]{3,1,2,0:T(8,128)(2,1)} fusion(bf16[1024,256]{1,0:T(8,128)(2,1)S(1)} %all_gather.17, bf16[1024,128]{1,0:T(8,128)(2,1)S(1)} %bitcast.121, bf16[1024,128]{1,0:T(8,128)(2,1)S(1)} %bitcast.119, f32[128,256]{1,0:T(8,128)} %fusion.45, f32[64,256]{1,0:T(8,128)S(1)} %get-tuple-element.40, f32[256]{0:T(256)S(1)} %divide_bitcast_fusion, ...), kind=kOutput, calls=%fused_computation.7 | convolution fusion | flops 78970880 | bytes 1639424 | tf_op jit(solution)/shard_map/dot_general | solution.py:13
  99.0 1.0 copy.50
  100.1 1.9 %gather_fusion.2 = bf16[48,64,128]{2,1,0:T(8,128)(2,1)S(1)} fusion(bf16[64,64,128]{2,1,0:T(8,128)(2,1)} %all-to-all-done.1, s32[1024]{0:T(1024)S(1)} %pad_clamp_fusion), kind=kCustom, calls=%fused_computation.2 | custom fusion | bytes 1573056 | tf_op jit(solution)/shard_map/gather | solution.py:160
  102.0 0.7 convolution_bitcast_fusion
  102.9 1.0 convolution_convert_fusion.2
  103.9 9.2 %all-to-all-start.2 = ((bf16[16,64,128]{2,1,0:T(8,128)(2,1)}), bf16[16,64,128]{2,1,0:T(8,128)(2,1)S(1)}, u32[]{:S(2)}, u32[]{:S(2)}) async-start(bf16[16,64,128]{2,1,0:T(8,128)(2,1)} %bitcast.27), calls=%async_computation.2 | async-start | bytes 524288 | tf_op jit(solution)/shard_map/all_to_all | solution.py:166
  113.1 0.6 pad_maximum_fusion.1
  113.8 11.0 %all-to-all-done.2 = bf16[16,64,128]{2,1,0:T(8,128)(2,1)S(1)} async-done(((bf16[16,64,128]{2,1,0:T(8,128)(2,1)}), bf16[16,64,128]{2,1,0:T(8,128)(2,1)S(1)}, u32[]{:S(2)}, u32[]{:S(2)}) %all-to-all-start.2) | async-done | bytes 262176 | tf_op jit(solution)/shard_map/all_to_all | solution.py:166
  124.9 25.4 %all_to_all.25.got_ref = bf16[64,2,16,128]{3,2,1,0:T(8,128)(2,1)} all-to-all(bf16[64,2,16,128]{3,2,1,0:T(8,128)(2,1)S(1)} %pad_maximum_fusion), channel_id=1, replica_groups=mesh['dom'=64,'feat'=16] {'dom'}, dimensions={0} | all-to-all | bytes 1048576 | tf_op jit(solution)/shard_map/all_to_all | solution.py:169
  150.3 2.0 %shard_map.146 = bf16[64,2,16,128]{3,2,1,0:T(8,128)(2,1)} custom-call(bf16[64,2,16,128]{3,2,1,0:T(8,128)(2,1)} %all_to_all.25.got_ref), custom_call_target="tpu_custom_call" | custom-call | tf_op jit(solution)/shard_map/pallas_call | solution.py:170
  152.3 6.6 %all-to-all-start.4 = ((bf16[64,2,16,128]{3,2,1,0:T(8,128)(2,1)}), bf16[64,2,16,128]{3,2,1,0:T(8,128)(2,1)S(1)}, u32[]{:S(2)}, u32[]{:S(2)}) async-start(bf16[64,2,16,128]{3,2,1,0:T(8,128)(2,1)} %shard_map.146), calls=%async_computation.4 | async-start | bytes 1048576 | tf_op jit(solution)/shard_map/all_to_all | solution.py:171
  158.8 1.3 all-gather.7.cloned.1.call-done
  160.1 1.3 fusion.42
  161.6 0.8 fusion.8
  162.4 12.7 %all-to-all-done.4.sums_ref = bf16[64,2,16,128]{3,2,1,0:T(8,128)(2,1)S(1)} async-done(((bf16[64,2,16,128]{3,2,1,0:T(8,128)(2,1)}), bf16[64,2,16,128]{3,2,1,0:T(8,128)(2,1)S(1)}, u32[]{:S(2)}, u32[]{:S(2)}) %all-to-all-start.4) | async-done | bytes 524320 | tf_op jit(solution)/shard_map/all_to_all | solution.py:171
  175.2 0.8 copy-done.2
  176.0 2.1 %shard_map.147 = (f32[64,1024]{1,0:T(8,128)}, f32[64,1024]{1,0:T(8,128)}, f32[64,1024]{1,0:T(8,128)}, f32[64,1024]{1,0:T(8,128)}) custom-call(bf16[64,2,16,128]{3,2,1,0:T(8,128)(2,1)} %copy-done.2), custom_call_target="tpu_custom_call" | custom-call | tf_op jit(solution)/shard_map/pallas_call | solution.py:172
  (63 shorter events, 3.5 us)
Async XLA Ops:
  7.2 88.6 %copy-start = (bf16[1024,64]{0,1:T(8,128)(2,1)S(1)}, bf16[1024,64]{0,1:T(8,128)(2,1)}, u32[]{:S(2)}) copy-start(bf16[1024,64]{0,1:T(8,128)(2,1)} %param.17) | copy-start | bytes 393220
  7.2 3.8 %copy-start.9 = (bf16[256,64]{0,1:T(8,128)(2,1)S(1)}, bf16[256,64]{0,1:T(8,128)(2,1)}, u32[]{:S(2)}) copy-start(bf16[256,64]{0,1:T(8,128)(2,1)} %param.11) | copy-start | bytes 98308
  7.2 3.5 %copy-start.5 = (bf16[1024,64]{0,1:T(8,128)(2,1)S(1)}, bf16[1024,64]{0,1:T(8,128)(2,1)}, u32[]{:S(2)}) copy-start(bf16[1024,64]{0,1:T(8,128)(2,1)} %param.18) | copy-start | bytes 393220
  7.2 3.2 %copy-start.7 = (bf16[1024,64]{0,1:T(8,128)(2,1)S(1)}, bf16[1024,64]{0,1:T(8,128)(2,1)}, u32[]{:S(2)}) copy-start(bf16[1024,64]{0,1:T(8,128)(2,1)} %param.19) | copy-start | bytes 393220
  7.2 86.6 %all-gather.5.cloned.1.call-start = ((), (), s32[]{:S(2)}) async-start(), calls=%async_computation.5 | async-start | bytes 5292032 | tf_op jit(solution)/shard_map/all_gather | solution.py:119
  7.3 3.8 %copy-start.12 = (bf16[128,64]{0,1:T(8,128)(2,1)S(1)}, bf16[128,64]{0,1:T(8,128)(2,1)}, u32[]{:S(2)}) copy-start(bf16[128,64]{0,1:T(8,128)(2,1)} %param.21) | copy-start | bytes 49156
  10.7 24.4 %copy-start.13 = (s32[2,24]{1,0:T(2,128)S(1)}, s32[2,24]{1,0:T(2,128)}, u32[]{:S(2)}) copy-start(s32[2,24]{1,0:T(2,128)} %param.14) | copy-start | bytes 580
  10.7 24.5 %copy-start.11 = (s32[64,32]{0,1:T(8,128)S(1)}, s32[64,32]{0,1:T(8,128)}, u32[]{:S(2)}) copy-start(s32[64,32]{0,1:T(8,128)} %param.13) | copy-start | bytes 24580
  11.0 25.4 %copy-start.1 = (bf16[2,24,128,128]{3,2,1,0:T(8,128)(2,1)S(1)}, bf16[2,24,128,128]{3,2,1,0:T(8,128)(2,1)}, u32[]{:S(2)}) copy-start(bf16[2,24,128,128]{3,2,1,0:T(8,128)(2,1)} %param.15) | copy-start | bytes 4718596
  11.9 49.9 %all-to-all-start = ((bf16[64,64,128]{2,1,0:T(8,128)(2,1)}), bf16[64,64,128]{2,1,0:T(8,128)(2,1)S(1)}, u32[]{:S(2)}, u32[]{:S(2)}) async-start(bf16[64,64,128]{2,1,0:T(8,128)(2,1)} %get-tuple-element.19), calls=%async_computation | async-start | bytes 2097152 | tf_op jit(solution)/shard_map/all_to_all | solution.py:85
  61.8 38.3 %all-to-all-start.1 = ((bf16[64,64,128]{2,1,0:T(8,128)(2,1)}), bf16[64,64,128]{2,1,0:T(8,128)(2,1)}, u32[]{:S(2)}, u32[]{:S(2)}) async-start(bf16[64,64,128]{2,1,0:T(8,128)(2,1)} %get-tuple-element.20), calls=%async_computation.1 | async-start | bytes 2097152 | tf_op jit(solution)/shard_map/all_to_all | solution.py:129
  71.9 0.9 copy-start.3
  71.9 0.9 copy-start.10
  71.9 23.2 %copy-start.15 = (bf16[1024,64]{0,1:T(8,128)(2,1)S(1)}, bf16[1024,64]{0,1:T(8,128)(2,1)}, u32[]{:S(2)}) copy-start(bf16[1024,64]{0,1:T(8,128)(2,1)} %param.16) | copy-start | bytes 393220
  72.7 22.7 %copy-start.14 = (s32[128]{0:T(128)S(1)}, s32[128]{0:T(128)}, u32[]{:S(2)}) copy-start(s32[128]{0:T(128)} %param.20) | copy-start | bytes 1540
  95.1 1.8 copy-start.4
  103.9 20.9 %all-to-all-start.2 = ((bf16[16,64,128]{2,1,0:T(8,128)(2,1)}), bf16[16,64,128]{2,1,0:T(8,128)(2,1)S(1)}, u32[]{:S(2)}, u32[]{:S(2)}) async-start(bf16[16,64,128]{2,1,0:T(8,128)(2,1)} %bitcast.27), calls=%async_computation.2 | async-start | bytes 524288 | tf_op jit(solution)/shard_map/all_to_all | solution.py:166
  113.1 47.0 %all-gather.7.cloned.1.call-start = ((), (), s32[]{:S(2)}) async-start(), calls=%async_computation.6 | async-start | bytes 1114112 | tf_op jit(solution)/shard_map/all_gather | solution.py:167
  150.3 11.1 %copy-start.6 = (bf16[1024,64]{0,1:T(8,128)(2,1)S(1)}, bf16[1024,64]{0,1:T(8,128)(2,1)}, u32[]{:S(2)}) copy-start(bf16[1024,64]{0,1:T(8,128)(2,1)} %param.18) | copy-start | bytes 393220
  152.3 9.3 %copy-start.8 = (bf16[1024,64]{0,1:T(8,128)(2,1)S(1)}, bf16[1024,64]{0,1:T(8,128)(2,1)}, u32[]{:S(2)}) copy-start(bf16[1024,64]{0,1:T(8,128)(2,1)} %param.19) | copy-start | bytes 393220
  152.3 22.9 %all-to-all-start.4 = ((bf16[64,2,16,128]{3,2,1,0:T(8,128)(2,1)}), bf16[64,2,16,128]{3,2,1,0:T(8,128)(2,1)S(1)}, u32[]{:S(2)}, u32[]{:S(2)}) async-start(bf16[64,2,16,128]{3,2,1,0:T(8,128)(2,1)} %shard_map.146), calls=%async_computation.4 | async-start | bytes 1048576 | tf_op jit(solution)/shard_map/all_to_all | solution.py:171
  175.2 0.8 copy-start.2
Sparse Core Ops, SparseCore 0:
  12.1 60.8 all-gather.4
  125.0 35.0 all-gather.6

commit v5 on v4

--- a/solution.py
+++ b/solution.py
@@ -2,6 +2,7 @@
 import jax.numpy as jnp
 from jax import lax
 from jax.experimental import pallas as pl
+from jax.experimental.pallas import tpu as pltpu
 from jax.experimental.layout import Layout, with_layout_constraint
 from jax.sharding import PartitionSpec as P
 
@@ -17,12 +18,32 @@
     return lax.optimization_barrier((value, *others))[0]
 
 
-def add_and_copy(got_ref, out_ref):
-    total = jnp.sum(got_ref[...].astype(F32), axis=0, keepdims=True)
-    out_ref[...] = jnp.broadcast_to(total.astype(out_ref.dtype), out_ref.shape)
-
-
-def unpack(sums_ref, self_one_ref, neigh_one_ref, self_two_ref, neigh_two_ref):
+CHUNKS = 4
+
+
+def pick_blocks(second_ref, halo_ref, rows_ref, out_ref, picked, sems):
+    parts, _, lanes = picked.shape
+    names = jnp.where(halo_ref[...] == second_ref[0], 1.0, 0.0)
+    names = jnp.max(names, axis=0, keepdims=True)
+    names = jnp.broadcast_to(names, (lanes, parts)).T
+    low = rows_ref[:, :lanes].astype(F32)
+    high = rows_ref[:, lanes:].astype(F32)
+    step = parts // CHUNKS
+    copies = []
+    for chunk in range(CHUNKS):
+        for reader in range(chunk * step, (chunk + 1) * step):
+            name = jnp.broadcast_to(names[reader : reader + 1, :], low.shape)
+            picked[reader] = jnp.where(name > 0.5, high, low).astype(picked.dtype)
+        part = pl.ds(chunk * step, step)
+        copy = pltpu.make_async_copy(picked.at[part], out_ref.at[part], sems.at[chunk])
+        copy.start()
+        copies.append(copy)
+    for copy in copies:
+        copy.wait()
+
+
+def unpack(sums_any, self_one_ref, neigh_one_ref, self_two_ref, neigh_two_ref, sums_ref):
+    pltpu.sync_copy(sums_any, sums_ref)
     parts, _, low, lanes = sums_ref.shape
     width, depth = self_one_ref.shape
     high = width // low
@@ -74,13 +95,23 @@
         neigh_two.T,
     )
 
-    second = jnp.any(halo_blocks == own_blocks * me + 1, axis=1)[:, None, None]
-
-    def pick(array_t):
-        return jnp.where(second, array_t[None, :, rows:], array_t[None, :, :rows])
-
+    second = own_blocks * me + 1
+    send_feats = pl.pallas_call(
+        pick_blocks,
+        in_specs=[
+            pl.BlockSpec(memory_space=pltpu.SMEM),
+            pl.BlockSpec(memory_space=pltpu.VMEM),
+            pl.BlockSpec(memory_space=pltpu.VMEM),
+        ],
+        out_specs=pl.BlockSpec(memory_space=pl.ANY),
+        out_shape=jax.ShapeDtypeStruct((parts, width, rows), BF),
+        scratch_shapes=[
+            pltpu.VMEM((parts, width, rows), BF),
+            pltpu.SemaphoreType.DMA((CHUNKS,)),
+        ],
+    )(second.reshape(1).astype(jnp.int32), halo_blocks.T, feats_t)
     send_feats, feats_t, self_two_t, neigh_two_t = lax.optimization_barrier(
-        (pick(feats_t), feats_t, self_two_t, neigh_two_t)
+        (send_feats, feats_t, self_two_t, neigh_two_t)
     )
     halo_feats = lax.all_to_all(send_feats, "dom", 0, 0, tiled=True)
     wanted = lax.dynamic_index_in_dim(halo_blocks, me, 0, keepdims=False)
@@ -125,7 +156,10 @@
         whole, own_blocks + 1 + lax.axis_index("feat"), 1, keepdims=False
     ).reshape(-1, 2 * width)
 
-    send_history = after(pick(history.T), dense, inverse, halo_feats)
+    history_t, halo_late = after((history.T, halo_blocks), dense)
+    named = jnp.any(halo_late == second, axis=1)[:, None, None]
+    send_history = jnp.where(named, history_t[None, :, rows:], history_t[None, :, :rows])
+    send_history = after(send_history, inverse, halo_feats)
     halo_history = lax.all_to_all(send_history, "dom", 0, 0, tiled=True)
 
     mean_one = (halo_sum(halo_feats[tile_owner]) + mm(feats_t, dense, ((1,), (1,)))) * inverse
@@ -166,11 +200,16 @@
     twos = lax.all_to_all(twos.reshape(slices, width, 2 * width), "feat", 0, 0, tiled=True)
     whole_two = lax.all_gather(after(layer_two, twos), "feat", axis=0, tiled=False)
     pieces = jnp.concatenate([ones, twos.reshape(parts, 1, low, lanes)], axis=1)
+    pieces = with_layout_constraint(pieces, Layout(major_to_minor=(0, 1, 2, 3)))
     got = lax.all_to_all(pieces, "dom", 0, 0, tiled=True)
-    spread = pl.pallas_call(add_and_copy, out_shape=jax.ShapeDtypeStruct(got.shape, BF))(got)
+    mine = jnp.sum(got.astype(F32), axis=0, keepdims=True).astype(BF)
+    spread = jnp.broadcast_to(mine, pieces.shape)
     sums = lax.all_to_all(spread, "dom", 0, 0, tiled=True)
     grads = pl.pallas_call(
-        unpack, out_shape=[jax.ShapeDtypeStruct((width, depth), F32)] * 4
+        unpack,
+        in_specs=[pl.BlockSpec(memory_space=pl.ANY)],
+        out_shape=[jax.ShapeDtypeStruct((width, depth), F32)] * 4,
+        scratch_shapes=[pltpu.VMEM(sums.shape, BF)],
     )(sums)
 
     whole_hidden = whole_two[:, :width].reshape(depth, owned)

time: 188 us -> 189 us (level)
  local copies, waits for them, and re-layouts: 10.6 us -> 13.4 us
  waiting for transfers between devices: 48.4 us -> 45.6 us
    all_to_all x1, waiting for transfers between devices: 23.4 us -> 20.5 us  [on_device(): halo_feats = lax.all_to_all(send_feats, 'dom', 0, 0, tiled=True)]
  transfers between devices with their start and end apart: 6 -> 6, of which waited for: 4 -> 4; matrix products, arithmetic and copies ran while one was open for 8% -> 10% of each run, Pallas kernels for 1% -> 0%
where the time goes in v5:
time: 189 us; the launch traced here: 186 us
  starting transfers between devices  47.4 us (25%)
  blocking collectives  46.9 us (25%)
  waiting for transfers between devices  45.6 us (24%)
  between operations  14.4 us (8%)
  local copies, waits for them, and re-layouts  13.4 us (7%)
  matrix products  8.35 us (4%)
  other arithmetic  5.77 us (3%)
  Pallas kernels  4.02 us (2%)
    all_to_all x1, blocking collectives, on_device(): got = lax.all_to_all(pieces, 'dom', 0, 0, tiled=True)  26 us
    all_to_all x1, starting transfers between devices, on_device(): halo_feats = lax.all_to_all(send_feats, 'dom', 0, 0, tiled=True)  23.2 us
    all_gather x1, blocking collectives, on_device(): lax.all_gather(mean_one.astype(BF), 'feat', axis=0, tiled=True)  20.9 us
    all_to_all x1, waiting for transfers between devices, on_device(): halo_feats = lax.all_to_all(send_feats, 'dom', 0, 0, tiled=True)  20.5 us
    all_to_all x1, waiting for transfers between devices, on_device(): sums = lax.all_to_all(spread, 'dom', 0, 0, tiled=True)  11.4 us
    all_to_all x1, waiting for transfers between devices, on_device(): lax.all_to_all(twos.reshape(slices, width, 2 * width), 'feat', 0, 0, tile...  11 us
    all_to_all x1, starting transfers between devices, on_device(): halo_history = lax.all_to_all(send_history, 'dom', 0, 0, tiled=True)  9.37 us
    all_to_all x1, starting transfers between devices, on_device(): lax.all_to_all(twos.reshape(slices, width, 2 * width), 'feat', 0, 0, tile...  8.37 us
  transfers between devices with their start and end apart: 6, of which 4 were waited for; matrix products, arithmetic and copies ran while one was open for 10% of the time, Pallas kernels for 0%

profile of v5, /device:TPU:1, one launch (start us, length us, event | category | flops | bytes accessed | tf_op | source)
XLA Modules:
  0.0 185.9 jit_solution(6744740323593956731)
XLA Ops:
  7.2 1.9 %shard_map.146 = bf16[64,64,128]{2,1,0:T(8,128)(2,1)} custom-call(s32[1]{0:T(128)} %bitcast.second_ref, s32[32,64]{1,0:T(8,128)} %bitcast.121, bf16[64,256]{1,0:T(8,128)(2,1)} %bitcast.113), custom_call_target="tpu_custom_call" | custom-call | tf_op jit(solution)/shard_map/pallas_call | solution.py:99
  9.2 1.1 reshape.140
  10.3 1.1 reshape.141
  11.4 0.8 bitcast_bitcast_fusion
  12.4 0.9 maximum_maximum_fusion
  13.3 23.2 %all-to-all-start = ((bf16[64,64,128]{2,1,0:T(8,128)(2,1)}), bf16[64,64,128]{2,1,0:T(8,128)(2,1)S(1)}, u32[]{:S(2)}, u32[]{:S(2)}) async-start(bf16[64,64,128]{2,1,0:T(8,128)(2,1)} %shard_map.146), calls=%async_computation | async-start | bytes 2097152 | tf_op jit(solution)/shard_map/all_to_all | solution.py:116
  36.8 0.8 gather_fusion
  38.7 0.8 copy.39
  41.5 1.1 broadcast_select_fusion
  42.6 20.5 %all-to-all-done = bf16[64,64,128]{2,1,0:T(8,128)(2,1)S(1)} async-done(((bf16[64,64,128]{2,1,0:T(8,128)(2,1)}), bf16[64,64,128]{2,1,0:T(8,128)(2,1)S(1)}, u32[]{:S(2)}, u32[]{:S(2)}) %all-to-all-start) | async-done | bytes 1048608 | tf_op jit(solution)/shard_map/all_to_all | solution.py:116
  63.2 9.4 %all-to-all-start.1 = ((bf16[64,64,128]{2,1,0:T(8,128)(2,1)}), bf16[64,64,128]{2,1,0:T(8,128)(2,1)}, u32[]{:S(2)}, u32[]{:S(2)}) async-start(bf16[64,64,128]{2,1,0:T(8,128)(2,1)} %broadcast_select_fusion), calls=%async_computation.1 | async-start | bytes 2097152 | tf_op jit(solution)/shard_map/all_to_all | solution.py:163
  72.6 0.8 gather_fusion.1
  73.4 1.4 convolution_bitcast_fusion.1
  75.1 20.9 %all_gather.17 = bf16[1024,256]{1,0:T(8,128)(2,1)S(1)} all-gather(bf16[64,256]{1,0:T(8,128)(2,1)S(1)} %fusion.5), channel_id=1, replica_groups=mesh['dom'=64,'feat'=16] {'feat'}, dimensions={0}, use_global_device_ids=true | all-gather | bytes 557056 | tf_op jit(solution)/shard_map/all_gather | solution.py:166
  95.9 1.3 fusion.41
  98.1 0.9 fusion.44
  99.0 2.1 %fusion = bf16[8,8,16,128]{3,1,2,0:T(8,128)(2,1)} fusion(bf16[1024,256]{1,0:T(8,128)(2,1)S(1)} %all_gather.17, bf16[1024,128]{1,0:T(8,128)(2,1)S(1)} %bitcast.119, bf16[1024,128]{1,0:T(8,128)(2,1)S(1)} %bitcast.117, f32[128,256]{1,0:T(8,128)} %fusion.44, f32[64,256]{1,0:T(8,128)S(1)} %get-tuple-element.40, f32[256]{0:T(256)S(1)} %copy-done.12, ...), kind=kOutput, calls=%fused_computation.7 | convolution fusion | flops 78970880 | bytes 1639424 | tf_op jit(solution)/shard_map/dot_general | solution.py:14
  101.1 1.0 copy.50
  102.2 2.0 %gather_fusion.2 = bf16[48,64,128]{2,1,0:T(8,128)(2,1)S(1)} fusion(bf16[64,64,128]{2,1,0:T(8,128)(2,1)} %all-to-all-done.1, s32[1024]{0:T(1024)} %pad_clamp_fusion), kind=kCustom, calls=%fused_computation.2 | custom fusion | bytes 1573056 | tf_op jit(solution)/shard_map/gather | solution.py:194
  104.3 0.7 convolution_bitcast_fusion
  105.1 1.0 convolution_convert_fusion.2
  106.2 8.4 %all-to-all-start.2 = ((bf16[16,64,128]{2,1,0:T(8,128)(2,1)}), bf16[16,64,128]{2,1,0:T(8,128)(2,1)S(1)}, u32[]{:S(2)}, u32[]{:S(2)}) async-start(bf16[16,64,128]{2,1,0:T(8,128)(2,1)} %bitcast.29), calls=%async_computation.2 | async-start | bytes 524288 | tf_op jit(solution)/shard_map/all_to_all | solution.py:200
  115.2 11.0 %all-to-all-done.2 = bf16[16,64,128]{2,1,0:T(8,128)(2,1)S(1)} async-done(((bf16[16,64,128]{2,1,0:T(8,128)(2,1)}), bf16[16,64,128]{2,1,0:T(8,128)(2,1)S(1)}, u32[]{:S(2)}, u32[]{:S(2)}) %all-to-all-start.2) | async-done | bytes 262176 | tf_op jit(solution)/shard_map/all_to_all | solution.py:200
  126.4 26.0 %all_to_all.25 = bf16[64,2,16,128]{3,2,1,0:T(8,128)(2,1)S(1)} all-to-all(bf16[64,2,16,128]{3,2,1,0:T(8,128)(2,1)S(1)} %pad_maximum_fusion), channel_id=1, replica_groups=mesh['dom'=64,'feat'=16] {'dom'}, dimensions={0} | all-to-all | bytes 1048576 | tf_op jit(solution)/shard_map/all_to_all | solution.py:204
  152.5 0.9 broadcast_in_dim.91
  153.4 6.4 %all-to-all-start.4 = ((bf16[64,2,16,128]{3,2,1,0:T(8,128)(2,1)}), bf16[64,2,16,128]{3,2,1,0:T(8,128)(2,1)S(1)}, u32[]{:S(2)}, u32[]{:S(2)}) async-start(bf16[64,2,16,128]{3,2,1,0:T(8,128)(2,1)} %broadcast_in_dim.91), calls=%async_computation.4 | async-start | bytes 1048576 | tf_op jit(solution)/shard_map/all_to_all | solution.py:207
  159.8 2.5 %all-gather.7.cloned.1.call-done = bf16[2048,256]{1,0:T(8,128)(2,1)} async-done(((bf16[128,256]{1,0:T(8,128)(2,1)}), bf16[2048,256]{1,0:T(8,128)(2,1)}) %all-gather.7.cloned.1.call-update) | async-done | bytes 1048592 | tf_op jit(solution)/shard_map/all_gather | solution.py:201
  162.4 1.3 fusion.42
  163.9 0.8 fusion.8
  164.7 11.4 %all-to-all-done.4.sums_any = bf16[64,2,16,128]{3,2,1,0:T(8,128)(2,1)S(1)} async-done(((bf16[64,2,16,128]{3,2,1,0:T(8,128)(2,1)}), bf16[64,2,16,128]{3,2,1,0:T(8,128)(2,1)S(1)}, u32[]{:S(2)}, u32[]{:S(2)}) %all-to-all-start.4) | async-done | bytes 524320 | tf_op jit(solution)/shard_map/all_to_all | solution.py:207
  176.1 0.8 copy-done.2
  177.0 2.1 %shard_map.147 = (f32[64,1024]{1,0:T(8,128)}, f32[64,1024]{1,0:T(8,128)}, f32[64,1024]{1,0:T(8,128)}, f32[64,1024]{1,0:T(8,128)}) custom-call(bf16[64,2,16,128]{3,2,1,0:T(8,128)(2,1)} %copy-done.2), custom_call_target="tpu_custom_call" | custom-call | tf_op jit(solution)/shard_map/pallas_call | solution.py:208
  (66 shorter events, 5.9 us)
Async XLA Ops:
  7.2 90.7 %copy-start = (bf16[1024,64]{0,1:T(8,128)(2,1)S(1)}, bf16[1024,64]{0,1:T(8,128)(2,1)}, u32[]{:S(2)}) copy-start(bf16[1024,64]{0,1:T(8,128)(2,1)} %param.17) | copy-start | bytes 393220
  7.2 5.2 %copy-start.10 = (bf16[128,64]{0,1:T(8,128)(2,1)S(1)}, bf16[128,64]{0,1:T(8,128)(2,1)}, u32[]{:S(2)}) copy-start(bf16[128,64]{0,1:T(8,128)(2,1)} %param.21) | copy-start | bytes 49156
  7.2 88.7 %all-gather.5.cloned.1.call-start = ((), (), s32[]{:S(2)}) async-start(), calls=%async_computation.5 | async-start | bytes 5292032 | tf_op jit(solution)/shard_map/all_gather | solution.py:150
  12.2 24.3 %copy-start.14 = (s32[2,24]{1,0:T(2,128)S(1)}, s32[2,24]{1,0:T(2,128)}, u32[]{:S(2)}) copy-start(s32[2,24]{1,0:T(2,128)} %param.14) | copy-start | bytes 580
  12.2 24.4 %copy-start.8 = (s32[64,32]{0,1:T(8,128)S(1)}, s32[64,32]{0,1:T(8,128)}, u32[]{:S(2)}) copy-start(s32[64,32]{0,1:T(8,128)} %param.13) | copy-start | bytes 24580
  12.4 25.4 %copy-start.1 = (bf16[2,24,128,128]{3,2,1,0:T(8,128)(2,1)S(1)}, bf16[2,24,128,128]{3,2,1,0:T(8,128)(2,1)}, u32[]{:S(2)}) copy-start(bf16[2,24,128,128]{3,2,1,0:T(8,128)(2,1)} %param.15) | copy-start | bytes 4718596
  13.3 49.9 %all-to-all-start = ((bf16[64,64,128]{2,1,0:T(8,128)(2,1)}), bf16[64,64,128]{2,1,0:T(8,128)(2,1)S(1)}, u32[]{:S(2)}, u32[]{:S(2)}) async-start(bf16[64,64,128]{2,1,0:T(8,128)(2,1)} %shard_map.146), calls=%async_computation | async-start | bytes 2097152 | tf_op jit(solution)/shard_map/all_to_all | solution.py:116
  38.2 3.3 %copy-start.9 = (bf16[256,64]{0,1:T(8,128)(2,1)S(1)}, bf16[256,64]{0,1:T(8,128)(2,1)}, u32[]{:S(2)}) copy-start(bf16[256,64]{0,1:T(8,128)(2,1)} %param.12) | copy-start | bytes 98308
  63.2 39.0 %all-to-all-start.1 = ((bf16[64,64,128]{2,1,0:T(8,128)(2,1)}), bf16[64,64,128]{2,1,0:T(8,128)(2,1)}, u32[]{:S(2)}, u32[]{:S(2)}) async-start(bf16[64,64,128]{2,1,0:T(8,128)(2,1)} %broadcast_select_fusion), calls=%async_computation.1 | async-start | bytes 2097152 | tf_op jit(solution)/shard_map/all_to_all | solution.py:163
  73.4 1.5 copy-start.3
  73.4 1.5 copy-start.7
  73.4 1.5 copy-start.11
  73.4 23.8 %copy-start.16 = (bf16[1024,64]{0,1:T(8,128)(2,1)S(1)}, bf16[1024,64]{0,1:T(8,128)(2,1)}, u32[]{:S(2)}) copy-start(bf16[1024,64]{0,1:T(8,128)(2,1)} %param.16) | copy-start | bytes 393220
  74.9 22.6 %copy-start.15 = (s32[128]{0:T(128)S(1)}, s32[128]{0:T(128)}, u32[]{:S(2)}) copy-start(s32[128]{0:T(128)} %param.20) | copy-start | bytes 1540
  97.2 1.8 copy-start.4
  97.2 1.8 copy-start.12
  101.1 3.2 %copy-start.13 = (pred[2,24]{1,0:T(4,128)(4,1)S(1)}, pred[2,24]{1,0:T(4,128)(4,1)}, u32[]{:S(2)}) copy-start(pred[2,24]{1,0:T(4,128)(4,1)} %broadcast_compare_fusion) | copy-start | bytes 148
  106.2 20.1 %all-to-all-start.2 = ((bf16[16,64,128]{2,1,0:T(8,128)(2,1)}), bf16[16,64,128]{2,1,0:T(8,128)(2,1)S(1)}, u32[]{:S(2)}, u32[]{:S(2)}) async-start(bf16[16,64,128]{2,1,0:T(8,128)(2,1)} %bitcast.29), calls=%async_computation.2 | async-start | bytes 524288 | tf_op jit(solution)/shard_map/all_to_all | solution.py:200
  114.6 47.8 %all-gather.7.cloned.1.call-start = ((), (), s32[]{:S(2)}) async-start(), calls=%async_computation.6 | async-start | bytes 1114112 | tf_op jit(solution)/shard_map/all_gather | solution.py:201
  152.4 11.2 %copy-start.5 = (bf16[1024,64]{0,1:T(8,128)(2,1)S(1)}, bf16[1024,64]{0,1:T(8,128)(2,1)}, u32[]{:S(2)}) copy-start(bf16[1024,64]{0,1:T(8,128)(2,1)} %param.18) | copy-start | bytes 393220
  152.5 11.4 %copy-start.6 = (bf16[1024,64]{0,1:T(8,128)(2,1)S(1)}, bf16[1024,64]{0,1:T(8,128)(2,1)}, u32[]{:S(2)}) copy-start(bf16[1024,64]{0,1:T(8,128)(2,1)} %param.19) | copy-start | bytes 393220
  153.4 22.8 %all-to-all-start.4 = ((bf16[64,2,16,128]{3,2,1,0:T(8,128)(2,1)}), bf16[64,2,16,128]{3,2,1,0:T(8,128)(2,1)S(1)}, u32[]{:S(2)}, u32[]{:S(2)}) async-start(bf16[64,2,16,128]{3,2,1,0:T(8,128)(2,1)} %broadcast_in_dim.91), calls=%async_computation.4 | async-start | bytes 1048576 | tf_op jit(solution)/shard_map/all_to_all | solution.py:207
  176.1 0.8 copy-start.2
Sparse Core Ops, SparseCore 0:
  13.4 60.8 all-gather.4
  126.4 35.9 all-gather.6

commit v6 on v5

--- a/solution.py
+++ b/solution.py
@@ -14,15 +14,13 @@
     return lax.dot_general(a, b, (dims, ((), ())), preferred_element_type=F32)
 
 
-def after(value, *others):
-    return lax.optimization_barrier((value, *others))[0]
-
-
 CHUNKS = 4
 
 
-def pick_blocks(second_ref, halo_ref, rows_ref, out_ref, picked, sems):
-    parts, _, lanes = picked.shape
+def lay_out(
+    second_ref, halo_ref, rows_ref, seeds_ref, self_ref, neigh_ref, out_ref, side_ref, picked, sems
+):
+    parts, width, lanes = picked.shape
     names = jnp.where(halo_ref[...] == second_ref[0], 1.0, 0.0)
     names = jnp.max(names, axis=0, keepdims=True)
     names = jnp.broadcast_to(names, (lanes, parts)).T
@@ -38,6 +36,17 @@
         copy = pltpu.make_async_copy(picked.at[part], out_ref.at[part], sems.at[chunk])
         copy.start()
         copies.append(copy)
+    side_ref[0] = rows_ref[:, :lanes]
+    side_ref[1] = rows_ref[:, lanes:]
+    side_ref[2] = seeds_ref[...]
+    for pair in range(self_ref.shape[1] // lanes):
+        across = slice(pair * lanes, (pair + 1) * lanes)
+        own = self_ref[:, across].astype(F32)
+        near = neigh_ref[:, across].astype(F32)
+        left = jnp.concatenate([own[:, :width], near[:, :width]], axis=1)
+        right = jnp.concatenate([own[:, width:], near[:, width:]], axis=1)
+        side_ref[3 + 2 * pair] = left.astype(side_ref.dtype)
+        side_ref[4 + 2 * pair] = right.astype(side_ref.dtype)
     for copy in copies:
         copy.wait()
 
@@ -96,22 +105,27 @@
     )
 
     second = own_blocks * me + 1
-    send_feats = pl.pallas_call(
-        pick_blocks,
-        in_specs=[
-            pl.BlockSpec(memory_space=pltpu.SMEM),
-            pl.BlockSpec(memory_space=pltpu.VMEM),
-            pl.BlockSpec(memory_space=pltpu.VMEM),
+    slices = self_two_t.shape[1] // width
+    send_feats, side = pl.pallas_call(
+        lay_out,
+        in_specs=[pl.BlockSpec(memory_space=pltpu.SMEM)]
+        + [pl.BlockSpec(memory_space=pltpu.VMEM)] * 5,
+        out_specs=[pl.BlockSpec(memory_space=pl.ANY), pl.BlockSpec(memory_space=pltpu.VMEM)],
+        out_shape=[
+            jax.ShapeDtypeStruct((parts, width, rows), BF),
+            jax.ShapeDtypeStruct((own_blocks + 1 + slices, width, rows), BF),
         ],
-        out_specs=pl.BlockSpec(memory_space=pl.ANY),
-        out_shape=jax.ShapeDtypeStruct((parts, width, rows), BF),
         scratch_shapes=[
             pltpu.VMEM((parts, width, rows), BF),
             pltpu.SemaphoreType.DMA((CHUNKS,)),
         ],
-    )(second.reshape(1).astype(jnp.int32), halo_blocks.T, feats_t)
-    send_feats, feats_t, self_two_t, neigh_two_t = lax.optimization_barrier(
-        (send_feats, feats_t, self_two_t, neigh_two_t)
+    )(
+        second.reshape(1).astype(jnp.int32),
+        halo_blocks.T,
+        feats_t,
+        cot_t,
+        self_two_t,
+        neigh_two_t,
     )
     halo_feats = lax.all_to_all(send_feats, "dom", 0, 0, tiled=True)
     wanted = lax.dynamic_index_in_dim(halo_blocks, me, 0, keepdims=False)
@@ -127,40 +141,27 @@
     row_total = jnp.sum(tile_weight, axis=(1, 3), dtype=F32).reshape(1, owned)
     inverse = 1.0 / row_total
 
+    whole = lax.all_gather(side, "feat", axis=0, tiled=False)
+    whole_feats = jnp.concatenate(
+        [whole[:, i].reshape(-1, rows) for i in range(own_blocks)], axis=1
+    )
+    whole_cot = whole[:, own_blocks].reshape(-1, seeds)
+    columns = lax.dynamic_index_in_dim(
+        whole, own_blocks + 1 + lax.axis_index("feat"), 1, keepdims=False
+    ).reshape(-1, 2 * width)
+
+    named = jnp.any(halo_blocks == second, axis=1)[:, None, None]
+    history_t, named = lax.optimization_barrier((history.T, named))
+    send_history = jnp.where(named, history_t[None, :, rows:], history_t[None, :, :rows])
+    send_history, dense, inverse, tile_owner, is_own, halo_feats = lax.optimization_barrier(
+        (send_history, dense, inverse, tile_owner, is_own, halo_feats)
+    )
+    halo_history = lax.all_to_all(send_history, "dom", 0, 0, tiled=True)
+
     def halo_sum(picked):
         picked = jnp.where(is_own[:, :, None, None], jnp.zeros((), BF), picked)
         out = jnp.einsum("bkfc,bkvc->fbv", picked, tile_weight, preferred_element_type=F32)
         return out.reshape(width, owned)
-
-    side = jnp.concatenate(
-        [
-            feats_t.reshape(width, own_blocks, rows).transpose(1, 0, 2),
-            cot_t.reshape(width, 1, seeds).transpose(1, 0, 2),
-            jnp.concatenate(
-                [
-                    self_two_t.reshape(width, -1, width).transpose(1, 0, 2),
-                    neigh_two_t.reshape(width, -1, width).transpose(1, 0, 2),
-                ],
-                axis=2,
-            ),
-        ],
-        axis=0,
-    )
-    side = with_layout_constraint(side, Layout(major_to_minor=(0, 1, 2)))
-    whole = lax.all_gather(side, "feat", axis=0, tiled=False)
-    whole_feats = jnp.concatenate(
-        [whole[:, i].reshape(-1, rows) for i in range(own_blocks)], axis=1
-    )
-    whole_cot = whole[:, own_blocks].reshape(-1, seeds)
-    columns = lax.dynamic_index_in_dim(
-        whole, own_blocks + 1 + lax.axis_index("feat"), 1, keepdims=False
-    ).reshape(-1, 2 * width)
-
-    history_t, halo_late = after((history.T, halo_blocks), dense)
-    named = jnp.any(halo_late == second, axis=1)[:, None, None]
-    send_history = jnp.where(named, history_t[None, :, rows:], history_t[None, :, :rows])
-    send_history = after(send_history, inverse, halo_feats)
-    halo_history = lax.all_to_all(send_history, "dom", 0, 0, tiled=True)
 
     mean_one = (halo_sum(halo_feats[tile_owner]) + mm(feats_t, dense, ((1,), (1,)))) * inverse
     whole_mean_one = lax.all_gather(mean_one.astype(BF), "feat", axis=0, tiled=True)
@@ -189,16 +190,18 @@
     ones = ones.astype(BF).reshape(high, low, 2 * depth // lanes, lanes).transpose(0, 2, 1, 3)
     ones = ones.reshape(parts, 1, low, lanes)
 
-    halo_history = after(halo_history, ones)
+    halo_history, ones, hidden, whole_grad_two = lax.optimization_barrier(
+        (halo_history, ones, hidden, whole_grad_two)
+    )
     mean_two = (
         (halo_sum(halo_history[tile_owner]) + mm(hidden, dense, ((1,), (1,)))) * inverse
     ).astype(BF)
     layer_two = jnp.concatenate([hidden, mean_two], axis=0)
 
     twos = mm(whole_grad_two, layer_two, ((1,), (1,))).astype(BF)
-    slices = depth // width
     twos = lax.all_to_all(twos.reshape(slices, width, 2 * width), "feat", 0, 0, tiled=True)
-    whole_two = lax.all_gather(after(layer_two, twos), "feat", axis=0, tiled=False)
+    layer_two, twos = lax.optimization_barrier((layer_two, twos))
+    whole_two = lax.all_gather(layer_two, "feat", axis=0, tiled=False)
     pieces = jnp.concatenate([ones, twos.reshape(parts, 1, low, lanes)], axis=1)
     pieces = with_layout_constraint(pieces, Layout(major_to_minor=(0, 1, 2, 3)))
     got = lax.all_to_all(pieces, "dom", 0, 0, tiled=True)

time: 189 us -> 187 us (0.989)
  local copies, waits for them, and re-layouts: 13.4 us -> 10.1 us
    reshape x2 -> x0, local copies, waits for them, and re-layouts: 2.24 us -> none  [the longest x1 1.12 us: on_device(): self_two_t.reshape(width, -1, width).transpose(1, 0, 2)]
where the time goes in v6:
time: 187 us; the launch traced here: 184 us
  blocking collectives  47.5 us (25%)
  starting transfers between devices  46.8 us (25%)
  waiting for transfers between devices  46.2 us (25%)
  between operations  14.4 us (8%)
  local copies, waits for them, and re-layouts  10.1 us (5%)
  matrix products  9 us (5%)
  Pallas kernels  5.1 us (3%)
  other arithmetic  4.32 us (2%)
    all_to_all x1, blocking collectives, on_device(): got = lax.all_to_all(pieces, 'dom', 0, 0, tiled=True)  26.7 us
    all_to_all x1, starting transfers between devices, on_device(): halo_feats = lax.all_to_all(send_feats, 'dom', 0, 0, tiled=True)  23.2 us
    all_to_all x1, waiting for transfers between devices, on_device(): halo_feats = lax.all_to_all(send_feats, 'dom', 0, 0, tiled=True)  21.2 us
    all_gather x1, blocking collectives, on_device(): lax.all_gather(mean_one.astype(BF), 'feat', axis=0, tiled=True)  20.9 us
    all_to_all x1, waiting for transfers between devices, on_device(): sums = lax.all_to_all(spread, 'dom', 0, 0, tiled=True)  11.5 us
    all_to_all x1, waiting for transfers between devices, on_device(): lax.all_to_all(twos.reshape(slices, width, 2 * width), 'feat', 0, 0, tile...  11 us
    all_to_all x1, starting transfers between devices, on_device(): halo_history = lax.all_to_all(send_history, 'dom', 0, 0, tiled=True)  9.37 us
    all_to_all x1, starting transfers between devices, on_device(): lax.all_to_all(twos.reshape(slices, width, 2 * width), 'feat', 0, 0, tile...  7.76 us
  transfers between devices with their start and end apart: 6, of which 4 were waited for; matrix products, arithmetic and copies ran while one was open for 10% of the time, Pallas kernels for 0%

profile of v6, /device:TPU:1, one launch (start us, length us, event | category | flops | bytes accessed | tf_op | source)
XLA Modules:
  0.0 183.6 jit_solution(1050999652511436168)
XLA Ops:
  7.3 3.0 %shard_map.146 = (bf16[64,64,128]{2,1,0:T(8,128)(2,1)}, bf16[19,64,128]{2,1,0:T(8,128)(2,1)}) custom-call(s32[1]{0:T(128)} %bitcast.5.second_ref, s32[32,64]{1,0:T(8,128)} %bitcast.112, bf16[64,256]{1,0:T(8,128)(2,1)} %bitcast.113, bf16[64,128]{1,0:T(8,128)(2,1)} %bitcast.115, bf16[64,1024]{1,0:T(8,128)(2,1)} %bitcast.104, bf16[64,1024]{1,0:T(8,128)(2,1)} %bitcast.105), custom_call_target="tpu_custom_call" | custom-call | tf_op jit(solution)/shard_map/pallas_call | solution.py:109
  10.3 23.2 %all-to-all-start = ((bf16[64,64,128]{2,1,0:T(8,128)(2,1)}), bf16[64,64,128]{2,1,0:T(8,128)(2,1)S(1)}, u32[]{:S(2)}, u32[]{:S(2)}) async-start(bf16[64,64,128]{2,1,0:T(8,128)(2,1)} %get-tuple-element.27), calls=%async_computation | async-start | bytes 2097152 | tf_op jit(solution)/shard_map/all_to_all | solution.py:130
  34.7 0.7 copy.44
  35.6 0.8 gather_fusion
  36.8 0.5 broadcast_compare_fusion
  37.3 0.6 broadcast_divide_fusion
  37.9 1.1 broadcast_select_fusion
  39.0 21.2 %all-to-all-done = bf16[64,64,128]{2,1,0:T(8,128)(2,1)S(1)} async-done(((bf16[64,64,128]{2,1,0:T(8,128)(2,1)}), bf16[64,64,128]{2,1,0:T(8,128)(2,1)S(1)}, u32[]{:S(2)}, u32[]{:S(2)}) %all-to-all-start) | async-done | bytes 1048608 | tf_op jit(solution)/shard_map/all_to_all | solution.py:130
  60.2 9.4 %all-to-all-start.1 = ((bf16[64,64,128]{2,1,0:T(8,128)(2,1)}), bf16[64,64,128]{2,1,0:T(8,128)(2,1)}, u32[]{:S(2)}, u32[]{:S(2)}) async-start(bf16[64,64,128]{2,1,0:T(8,128)(2,1)} %broadcast_select_fusion), calls=%async_computation.1 | async-start | bytes 2097152 | tf_op jit(solution)/shard_map/all_to_all | solution.py:159
  69.7 0.7 gather_fusion.1
  70.4 1.4 convolution_bitcast_fusion.2
  71.9 0.8 fusion.7
  72.7 20.9 %all_gather.17 = bf16[1024,256]{1,0:T(8,128)(2,1)S(1)} all-gather(bf16[64,256]{1,0:T(8,128)(2,1)S(1)} %fusion.7), channel_id=1, replica_groups=mesh['dom'=64,'feat'=16] {'feat'}, dimensions={0}, use_global_device_ids=true | all-gather | bytes 557056 | tf_op jit(solution)/shard_map/all_gather | solution.py:167
  93.6 1.3 fusion.43
  95.7 0.9 fusion.46
  96.7 2.1 %fusion = bf16[8,8,16,128]{3,1,2,0:T(8,128)(2,1)} fusion(bf16[256,256]{1,0:T(8,128)(2,1)S(1)} %bitcast.95, bf16[1024,256]{1,0:T(8,128)(2,1)S(1)} %all_gather.17, bf16[1024,128]{1,0:T(8,128)(2,1)S(1)} %bitcast.110, bf16[1024,128]{1,0:T(8,128)(2,1)S(1)} %bitcast.108, f32[128,256]{1,0:T(8,128)} %fusion.46, f32[64,256]{1,0:T(8,128)S(1)} %get-tuple-element.54, ...), kind=kOutput, calls=%fused_computation.7 | convolution fusion | flops 78970880 | bytes 1639424 | tf_op jit(solution)/shard_map/dot_general | solution.py:14
  98.8 1.0 copy.40
  99.9 2.0 %gather_fusion.2 = bf16[48,64,128]{2,1,0:T(8,128)(2,1)S(1)} fusion(bf16[64,64,128]{2,1,0:T(8,128)(2,1)} %all-to-all-done.1, s32[1024]{0:T(1024)} %copy-done.11), kind=kCustom, calls=%fused_computation.2 | custom fusion | bytes 1573056 | tf_op jit(solution)/shard_map/gather | solution.py:197
  101.9 0.7 convolution_bitcast_fusion.1
  102.8 1.0 convolution_convert_fusion.2
  103.8 7.8 %all-to-all-start.2 = ((bf16[16,64,128]{2,1,0:T(8,128)(2,1)}), bf16[16,64,128]{2,1,0:T(8,128)(2,1)S(1)}, u32[]{:S(2)}, u32[]{:S(2)}) async-start(bf16[16,64,128]{2,1,0:T(8,128)(2,1)} %bitcast.29), calls=%async_computation.2 | async-start | bytes 524288 | tf_op jit(solution)/shard_map/all_to_all | solution.py:202
  111.6 0.6 pad_maximum_fusion.1
  112.3 11.0 %all-to-all-done.2 = bf16[16,64,128]{2,1,0:T(8,128)(2,1)S(1)} async-done(((bf16[16,64,128]{2,1,0:T(8,128)(2,1)}), bf16[16,64,128]{2,1,0:T(8,128)(2,1)S(1)}, u32[]{:S(2)}, u32[]{:S(2)}) %all-to-all-start.2) | async-done | bytes 262176 | tf_op jit(solution)/shard_map/all_to_all | solution.py:202
  123.4 26.7 %all_to_all.25 = bf16[64,2,16,128]{3,2,1,0:T(8,128)(2,1)S(1)} all-to-all(bf16[64,2,16,128]{3,2,1,0:T(8,128)(2,1)S(1)} %pad_maximum_fusion), channel_id=1, replica_groups=mesh['dom'=64,'feat'=16] {'dom'}, dimensions={0} | all-to-all | bytes 1048576 | tf_op jit(solution)/shard_map/all_to_all | solution.py:207
  150.2 0.9 broadcast_in_dim.100
  151.1 6.4 %all-to-all-start.4 = ((bf16[64,2,16,128]{3,2,1,0:T(8,128)(2,1)}), bf16[64,2,16,128]{3,2,1,0:T(8,128)(2,1)S(1)}, u32[]{:S(2)}, u32[]{:S(2)}) async-start(bf16[64,2,16,128]{3,2,1,0:T(8,128)(2,1)} %broadcast_in_dim.100), calls=%async_computation.4 | async-start | bytes 1048576 | tf_op jit(solution)/shard_map/all_to_all | solution.py:210
  157.5 2.5 %all-gather.7.cloned.1.call-done = bf16[2048,256]{1,0:T(8,128)(2,1)} async-done(((bf16[128,256]{1,0:T(8,128)(2,1)}), bf16[2048,256]{1,0:T(8,128)(2,1)}) %all-gather.7.cloned.1.call-update) | async-done | bytes 1048592 | tf_op jit(solution)/shard_map/all_gather | solution.py:204
  160.0 1.3 fusion.44
  161.5 0.8 fusion.9
  162.4 11.5 %all-to-all-done.4.sums_any = bf16[64,2,16,128]{3,2,1,0:T(8,128)(2,1)S(1)} async-done(((bf16[64,2,16,128]{3,2,1,0:T(8,128)(2,1)}), bf16[64,2,16,128]{3,2,1,0:T(8,128)(2,1)S(1)}, u32[]{:S(2)}, u32[]{:S(2)}) %all-to-all-start.4) | async-done | bytes 524320 | tf_op jit(solution)/shard_map/all_to_all | solution.py:210
  173.8 0.8 copy-done.2
  174.6 2.1 %shard_map.147 = (f32[64,1024]{1,0:T(8,128)}, f32[64,1024]{1,0:T(8,128)}, f32[64,1024]{1,0:T(8,128)}, f32[64,1024]{1,0:T(8,128)}) custom-call(bf16[64,2,16,128]{3,2,1,0:T(8,128)(2,1)} %copy-done.2), custom_call_target="tpu_custom_call" | custom-call | tf_op jit(solution)/shard_map/pallas_call | solution.py:211
  (61 shorter events, 3.4 us)
Async XLA Ops:
  7.2 88.3 %copy-start = (bf16[1024,64]{0,1:T(8,128)(2,1)S(1)}, bf16[1024,64]{0,1:T(8,128)(2,1)}, u32[]{:S(2)}) copy-start(bf16[1024,64]{0,1:T(8,128)(2,1)} %param.17) | copy-start | bytes 393220
  7.2 26.4 %copy-start.7 = (s32[64,32]{0,1:T(8,128)S(1)}, s32[64,32]{0,1:T(8,128)}, u32[]{:S(2)}) copy-start(s32[64,32]{0,1:T(8,128)} %param.13) | copy-start | bytes 24580
  7.2 26.3 %copy-start.13 = (s32[2,24]{1,0:T(2,128)S(1)}, s32[2,24]{1,0:T(2,128)}, u32[]{:S(2)}) copy-start(s32[2,24]{1,0:T(2,128)} %param.14) | copy-start | bytes 580
  7.2 26.4 %copy-start.1 = (bf16[2,24,128,128]{3,2,1,0:T(8,128)(2,1)S(1)}, bf16[2,24,128,128]{3,2,1,0:T(8,128)(2,1)}, u32[]{:S(2)}) copy-start(bf16[2,24,128,128]{3,2,1,0:T(8,128)(2,1)} %param.15) | copy-start | bytes 4718596
  7.2 86.4 %all-gather.5.cloned.1.call-start = ((), (), s32[]{:S(2)}) async-start(), calls=%async_computation.5 | async-start | bytes 5292032 | tf_op jit(solution)/shard_map/all_gather | solution.py:144
  10.3 49.9 %all-to-all-start = ((bf16[64,64,128]{2,1,0:T(8,128)(2,1)}), bf16[64,64,128]{2,1,0:T(8,128)(2,1)S(1)}, u32[]{:S(2)}, u32[]{:S(2)}) async-start(bf16[64,64,128]{2,1,0:T(8,128)(2,1)} %get-tuple-element.27), calls=%async_computation | async-start | bytes 2097152 | tf_op jit(solution)/shard_map/all_to_all | solution.py:130
  34.5 3.4 %copy-start.9 = (bf16[256,64]{0,1:T(8,128)(2,1)S(1)}, bf16[256,64]{0,1:T(8,128)(2,1)}, u32[]{:S(2)}) copy-start(bf16[256,64]{0,1:T(8,128)(2,1)} %param.12) | copy-start | bytes 98308
  60.2 39.7 %all-to-all-start.1 = ((bf16[64,64,128]{2,1,0:T(8,128)(2,1)}), bf16[64,64,128]{2,1,0:T(8,128)(2,1)}, u32[]{:S(2)}, u32[]{:S(2)}) async-start(bf16[64,64,128]{2,1,0:T(8,128)(2,1)} %broadcast_select_fusion), calls=%async_computation.1 | async-start | bytes 2097152 | tf_op jit(solution)/shard_map/all_to_all | solution.py:159
  69.7 0.7 copy-start.11
  70.4 1.5 copy-start.3
  70.4 1.5 copy-start.8
  70.4 24.5 %copy-start.15 = (bf16[1024,64]{0,1:T(8,128)(2,1)S(1)}, bf16[1024,64]{0,1:T(8,128)(2,1)}, u32[]{:S(2)}) copy-start(bf16[1024,64]{0,1:T(8,128)(2,1)} %param.16) | copy-start | bytes 393220
  71.9 23.3 %copy-start.14 = (s32[128]{0:T(128)S(1)}, s32[128]{0:T(128)}, u32[]{:S(2)}) copy-start(s32[128]{0:T(128)} %param.20) | copy-start | bytes 1540
  94.9 1.8 copy-start.4
  94.9 1.8 copy-start.10
  96.7 5.3 %copy-start.12 = (pred[2,24]{1,0:T(4,128)(4,1)S(1)}, pred[2,24]{1,0:T(4,128)(4,1)}, u32[]{:S(2)}) copy-start(pred[2,24]{1,0:T(4,128)(4,1)} %broadcast_compare_fusion) | copy-start | bytes 148
  103.8 19.5 %all-to-all-start.2 = ((bf16[16,64,128]{2,1,0:T(8,128)(2,1)}), bf16[16,64,128]{2,1,0:T(8,128)(2,1)S(1)}, u32[]{:S(2)}, u32[]{:S(2)}) async-start(bf16[16,64,128]{2,1,0:T(8,128)(2,1)} %bitcast.29), calls=%async_computation.2 | async-start | bytes 524288 | tf_op jit(solution)/shard_map/all_to_all | solution.py:202
  111.6 48.4 %all-gather.7.cloned.1.call-start = ((), (), s32[]{:S(2)}) async-start(), calls=%async_computation.6 | async-start | bytes 1114112 | tf_op jit(solution)/shard_map/all_gather | solution.py:204
  150.1 11.2 %copy-start.5 = (bf16[1024,64]{0,1:T(8,128)(2,1)S(1)}, bf16[1024,64]{0,1:T(8,128)(2,1)}, u32[]{:S(2)}) copy-start(bf16[1024,64]{0,1:T(8,128)(2,1)} %param.18) | copy-start | bytes 393220
  150.2 11.4 %copy-start.6 = (bf16[1024,64]{0,1:T(8,128)(2,1)S(1)}, bf16[1024,64]{0,1:T(8,128)(2,1)}, u32[]{:S(2)}) copy-start(bf16[1024,64]{0,1:T(8,128)(2,1)} %param.19) | copy-start | bytes 393220
  151.1 22.8 %all-to-all-start.4 = ((bf16[64,2,16,128]{3,2,1,0:T(8,128)(2,1)}), bf16[64,2,16,128]{3,2,1,0:T(8,128)(2,1)S(1)}, u32[]{:S(2)}, u32[]{:S(2)}) async-start(bf16[64,2,16,128]{3,2,1,0:T(8,128)(2,1)} %broadcast_in_dim.100), calls=%async_computation.4 | async-start | bytes 1048576 | tf_op jit(solution)/shard_map/all_to_all | solution.py:210
  173.8 0.8 copy-start.2
Sparse Core Ops, SparseCore 0:
  10.8 60.8 all-gather.4
  123.5 36.5 all-gather.6

commit v7 on v6

--- a/solution.py
+++ b/solution.py
@@ -175,6 +175,17 @@
         batch_ids[:, None] == jnp.arange(owned, dtype=jnp.int32)[None, :]
     ).astype(BF)
     whole_grad_two = mm(whole_cot, seed_rows, ((1,), (0,))).astype(BF)
+
+    halo_history, hidden, whole_grad_two = lax.optimization_barrier(
+        (halo_history, hidden, whole_grad_two)
+    )
+    mean_two = (
+        (halo_sum(halo_history[tile_owner]) + mm(hidden, dense, ((1,), (1,)))) * inverse
+    ).astype(BF)
+    layer_two = jnp.concatenate([hidden, mean_two], axis=0)
+
+    twos = mm(whole_grad_two, layer_two, ((1,), (1,))).astype(BF)
+    twos, columns, pre_one, gate = lax.optimization_barrier((twos, columns, pre_one, gate))
     back = mm(columns, whole_grad_two, ((0,), (0,)))
     scaled = (back[width:] * inverse).astype(BF)
     own_grad = mm(scaled, dense, ((1,), (0,)))
@@ -189,18 +200,8 @@
     low = width // high
     ones = ones.astype(BF).reshape(high, low, 2 * depth // lanes, lanes).transpose(0, 2, 1, 3)
     ones = ones.reshape(parts, 1, low, lanes)
-
-    halo_history, ones, hidden, whole_grad_two = lax.optimization_barrier(
-        (halo_history, ones, hidden, whole_grad_two)
-    )
-    mean_two = (
-        (halo_sum(halo_history[tile_owner]) + mm(hidden, dense, ((1,), (1,)))) * inverse
-    ).astype(BF)
-    layer_two = jnp.concatenate([hidden, mean_two], axis=0)
-
-    twos = mm(whole_grad_two, layer_two, ((1,), (1,))).astype(BF)
     twos = lax.all_to_all(twos.reshape(slices, width, 2 * width), "feat", 0, 0, tiled=True)
-    layer_two, twos = lax.optimization_barrier((layer_two, twos))
+    layer_two, twos, ones = lax.optimization_barrier((layer_two, twos, ones))
     whole_two = lax.all_gather(layer_two, "feat", axis=0, tiled=False)
     pieces = jnp.concatenate([ones, twos.reshape(parts, 1, low, lanes)], axis=1)
     pieces = with_layout_constraint(pieces, Layout(major_to_minor=(0, 1, 2, 3)))
@@ -213,6 +214,7 @@
         in_specs=[pl.BlockSpec(memory_space=pl.ANY)],
         out_shape=[jax.ShapeDtypeStruct((width, depth), F32)] * 4,
         scratch_shapes=[pltpu.VMEM(sums.shape, BF)],
+        compiler_params=pltpu.CompilerParams(vmem_limit_bytes=6 << 20),
     )(sums)
 
     whole_hidden = whole_two[:, :width].reshape(depth, owned)

time: 187 us -> 182 us (0.973)
  starting transfers between devices: 46.8 us -> 50.6 us
  blocking collectives: 47.5 us -> 44.8 us
  matrix products: 9 us -> 6.99 us
    all_to_all x1, starting transfers between devices: 7.76 us -> 11.6 us  [on_device(): lax.all_to_all(twos.reshape(slices, width, 2 * width), 'feat', 0, 0, tile...]
    all_to_all x1, blocking collectives: 26.7 us -> 24 us  [on_device(): got = lax.all_to_all(pieces, 'dom', 0, 0, tiled=True)]
    all_to_all x1, waiting for transfers between devices: 11 us -> 8.99 us  [on_device(): lax.all_to_all(twos.reshape(slices, width, 2 * width), 'feat', 0, 0, tile...]
    dynamic_slice x0 -> x1, local copies, waits for them, and re-layouts: none -> 1.96 us  [on_device(): lax.dynamic_index_in_dim(whole, own_blocks + 1 + lax.axis_index('feat'),...]
  transfers between devices with their start and end apart: 6 -> 6, of which waited for: 4 -> 5; matrix products, arithmetic and copies ran while one was open for 10% -> 9% of each run, Pallas kernels for 0% -> 0%
where the time goes in v7:
time: 182 us; the launch traced here: 179 us
  starting transfers between devices  50.6 us (28%)
  waiting for transfers between devices  45.4 us (25%)
  blocking collectives  44.8 us (25%)
  between operations  14.5 us (8%)
  local copies, waits for them, and re-layouts  9.57 us (5%)
  matrix products  6.99 us (4%)
  Pallas kernels  4.1 us (2%)
  other arithmetic  3.24 us (2%)
    all_to_all x1, blocking collectives, on_device(): got = lax.all_to_all(pieces, 'dom', 0, 0, tiled=True)  24 us
    all_to_all x1, starting transfers between devices, on_device(): halo_feats = lax.all_to_all(send_feats, 'dom', 0, 0, tiled=True)  23.2 us
    all_to_all x1, waiting for transfers between devices, on_device(): halo_feats = lax.all_to_all(send_feats, 'dom', 0, 0, tiled=True)  22.2 us
    all_gather x1, blocking collectives, on_device(): lax.all_gather(mean_one.astype(BF), 'feat', axis=0, tiled=True)  20.8 us
    all_to_all x1, starting transfers between devices, on_device(): lax.all_to_all(twos.reshape(slices, width, 2 * width), 'feat', 0, 0, tile...  11.6 us
    all_to_all x1, waiting for transfers between devices, on_device(): sums = lax.all_to_all(spread, 'dom', 0, 0, tiled=True)  11.5 us
    all_to_all x1, starting transfers between devices, on_device(): halo_history = lax.all_to_all(send_history, 'dom', 0, 0, tiled=True)  9.37 us
    all_to_all x1, waiting for transfers between devices, on_device(): lax.all_to_all(twos.reshape(slices, width, 2 * width), 'feat', 0, 0, tile...  8.99 us
  transfers between devices with their start and end apart: 6, of which 5 were waited for; matrix products, arithmetic and copies ran while one was open for 9% of the time, Pallas kernels for 0%

profile of v7, /device:TPU:1, one launch (start us, length us, event | category | flops | bytes accessed | tf_op | source)
XLA Modules:
  0.0 179.2 jit_solution(886806858156924800)
XLA Ops:
  7.3 3.0 %shard_map.146 = (bf16[64,64,128]{2,1,0:T(8,128)(2,1)}, bf16[19,64,128]{2,1,0:T(8,128)(2,1)}) custom-call(s32[1]{0:T(128)} %bitcast.5.second_ref, s32[32,64]{1,0:T(8,128)} %bitcast.112, bf16[64,256]{1,0:T(8,128)(2,1)} %bitcast.113, bf16[64,128]{1,0:T(8,128)(2,1)} %bitcast.115, bf16[64,1024]{1,0:T(8,128)(2,1)} %bitcast.104, bf16[64,1024]{1,0:T(8,128)(2,1)} %bitcast.105), custom_call_target="tpu_custom_call" | custom-call | tf_op jit(solution)/shard_map/pallas_call | solution.py:109
  10.3 23.2 %all-to-all-start = ((bf16[64,64,128]{2,1,0:T(8,128)(2,1)}), bf16[64,64,128]{2,1,0:T(8,128)(2,1)S(1)}, u32[]{:S(2)}, u32[]{:S(2)}) async-start(bf16[64,64,128]{2,1,0:T(8,128)(2,1)} %get-tuple-element.31), calls=%async_computation | async-start | bytes 2097152 | tf_op jit(solution)/shard_map/all_to_all | solution.py:130
  33.8 0.8 gather_fusion
  34.7 0.4 convert_element_type.50
  35.1 0.5 select_reduce_fusion
  35.8 0.7 copy.44
  36.5 0.3 convert_reduce_fusion
  36.8 1.1 broadcast_select_fusion
  38.0 22.2 %all-to-all-done = bf16[64,64,128]{2,1,0:T(8,128)(2,1)S(1)} async-done(((bf16[64,64,128]{2,1,0:T(8,128)(2,1)}), bf16[64,64,128]{2,1,0:T(8,128)(2,1)S(1)}, u32[]{:S(2)}, u32[]{:S(2)}) %all-to-all-start) | async-done | bytes 1048608 | tf_op jit(solution)/shard_map/all_to_all | solution.py:130
  60.2 9.4 %all-to-all-start.1 = ((bf16[64,64,128]{2,1,0:T(8,128)(2,1)}), bf16[64,64,128]{2,1,0:T(8,128)(2,1)}, u32[]{:S(2)}, u32[]{:S(2)}) async-start(bf16[64,64,128]{2,1,0:T(8,128)(2,1)} %broadcast_select_fusion), calls=%async_computation.1 | async-start | bytes 2097152 | tf_op jit(solution)/shard_map/all_to_all | solution.py:159
  69.7 0.7 gather_fusion.1
  70.4 0.7 convolution_bitcast_fusion.2
  71.5 20.8 %all_gather.17 = bf16[1024,256]{1,0:T(8,128)(2,1)S(1)} all-gather(bf16[64,256]{1,0:T(8,128)(2,1)S(1)} %fusion.6), channel_id=1, replica_groups=mesh['dom'=64,'feat'=16] {'feat'}, dimensions={0}, use_global_device_ids=true | all-gather | bytes 557056 | tf_op jit(solution)/shard_map/all_gather | solution.py:167
  92.3 2.0 %constant_dynamic-slice_fusion = (bf16[16,1,64,128]{3,2,1,0:T(8,128)(2,1)}, bf16[16,1,64,128]{3,2,1,0:T(8,128)(2,1)S(1)}, bf16[16,1,64,128]{3,2,1,0:T(8,128)(2,1)S(1)}, bf16[16,1,64,128]{3,2,1,0:T(8,128)(2,1)S(1)}) fusion(bf16[16,19,64,128]{3,2,1,0:T(8,128)(2,1)} %bitcast.111, s32[]{:T(128)S(6)} %select_n.43), kind=kLoop, calls=%fused_computation.71 | loop fusion | bytes 2097156 | tf_op jit(solution)/shard_map/jit(dynamic_index_in_dim)/dynamic_slice | solution.py:149
  94.5 0.3 convolution_convert_fusion.1
  95.1 0.9 add_divide_fusion
  96.0 1.9 %gather_fusion.2 = bf16[48,64,128]{2,1,0:T(8,128)(2,1)S(1)} fusion(bf16[64,64,128]{2,1,0:T(8,128)(2,1)} %all-to-all-done.1, s32[1024]{0:T(1024)S(1)} %pad_clamp_fusion), kind=kCustom, calls=%fused_computation.2 | custom fusion | bytes 1573056 | tf_op jit(solution)/shard_map/gather | solution.py:183
  98.0 0.7 convolution_bitcast_fusion.1
  99.1 1.0 convolution_convert_fusion.2
  100.1 11.6 %all-to-all-start.2 = ((bf16[16,64,128]{2,1,0:T(8,128)(2,1)}), bf16[16,64,128]{2,1,0:T(8,128)(2,1)S(1)}, u32[]{:S(2)}, u32[]{:S(2)}) async-start(bf16[16,64,128]{2,1,0:T(8,128)(2,1)} %bitcast.27), calls=%async_computation.2 | async-start | bytes 524288 | tf_op jit(solution)/shard_map/all_to_all | solution.py:203
  111.8 1.2 fusion.45
  113.0 0.5 fusion
  113.8 0.6 pad_maximum_fusion.1
  114.4 9.0 %all-to-all-done.2 = bf16[16,64,128]{2,1,0:T(8,128)(2,1)S(1)} async-done(((bf16[16,64,128]{2,1,0:T(8,128)(2,1)}), bf16[16,64,128]{2,1,0:T(8,128)(2,1)S(1)}, u32[]{:S(2)}, u32[]{:S(2)}) %all-to-all-start.2) | async-done | bytes 262176 | tf_op jit(solution)/shard_map/all_to_all | solution.py:203
  123.5 24.0 %all_to_all.25 = bf16[64,2,16,128]{3,2,1,0:T(8,128)(2,1)S(1)} all-to-all(bf16[64,2,16,128]{3,2,1,0:T(8,128)(2,1)S(1)} %pad_maximum_fusion), channel_id=1, replica_groups=mesh['dom'=64,'feat'=16] {'dom'}, dimensions={0} | all-to-all | bytes 1048576 | tf_op jit(solution)/shard_map/all_to_all | solution.py:208
  147.6 0.9 broadcast_in_dim.100
  148.5 6.4 %all-to-all-start.4 = ((bf16[64,2,16,128]{3,2,1,0:T(8,128)(2,1)}), bf16[64,2,16,128]{3,2,1,0:T(8,128)(2,1)S(1)}, u32[]{:S(2)}, u32[]{:S(2)}) async-start(bf16[64,2,16,128]{3,2,1,0:T(8,128)(2,1)} %broadcast_in_dim.100), calls=%async_computation.4 | async-start | bytes 1048576 | tf_op jit(solution)/shard_map/all_to_all | solution.py:211
  154.9 2.5 %all-gather.7.cloned.1.call-done = bf16[2048,256]{1,0:T(8,128)(2,1)} async-done(((bf16[128,256]{1,0:T(8,128)(2,1)}), bf16[2048,256]{1,0:T(8,128)(2,1)}) %all-gather.7.cloned.1.call-update) | async-done | bytes 1048592 | tf_op jit(solution)/shard_map/all_gather | solution.py:205
  157.4 1.3 fusion.43
  158.9 0.8 fusion.9
  159.7 11.5 %all-to-all-done.4.sums_any = bf16[64,2,16,128]{3,2,1,0:T(8,128)(2,1)S(1)} async-done(((bf16[64,2,16,128]{3,2,1,0:T(8,128)(2,1)}), bf16[64,2,16,128]{3,2,1,0:T(8,128)(2,1)S(1)}, u32[]{:S(2)}, u32[]{:S(2)}) %all-to-all-start.4) | async-done | bytes 524320 | tf_op jit(solution)/shard_map/all_to_all | solution.py:211
  171.2 1.1 shard_map.147
  (71 shorter events, 2.7 us)
Async XLA Ops:
  7.2 87.9 %copy-start = (bf16[1024,64]{0,1:T(8,128)(2,1)S(1)}, bf16[1024,64]{0,1:T(8,128)(2,1)}, u32[]{:S(2)}) copy-start(bf16[1024,64]{0,1:T(8,128)(2,1)} %param.17) | copy-start | bytes 393220
  7.2 26.3 %copy-start.13 = (s32[64,32]{0,1:T(8,128)S(1)}, s32[64,32]{0,1:T(8,128)}, u32[]{:S(2)}) copy-start(s32[64,32]{0,1:T(8,128)} %param.13) | copy-start | bytes 24580
  7.2 26.3 %copy-start.18 = (s32[2,24]{1,0:T(2,128)S(1)}, s32[2,24]{1,0:T(2,128)}, u32[]{:S(2)}) copy-start(s32[2,24]{1,0:T(2,128)} %param.14) | copy-start | bytes 580
  7.2 27.5 %copy-start.1 = (bf16[2,24,128,128]{3,2,1,0:T(8,128)(2,1)S(1)}, bf16[2,24,128,128]{3,2,1,0:T(8,128)(2,1)}, u32[]{:S(2)}) copy-start(bf16[2,24,128,128]{3,2,1,0:T(8,128)(2,1)} %param.15) | copy-start | bytes 4718596
  7.2 85.1 %all-gather.5.cloned.1.call-start = ((), (), s32[]{:S(2)}) async-start(), calls=%async_computation.5 | async-start | bytes 5292032 | tf_op jit(solution)/shard_map/all_gather | solution.py:144
  10.3 49.9 %all-to-all-start = ((bf16[64,64,128]{2,1,0:T(8,128)(2,1)}), bf16[64,64,128]{2,1,0:T(8,128)(2,1)S(1)}, u32[]{:S(2)}, u32[]{:S(2)}) async-start(bf16[64,64,128]{2,1,0:T(8,128)(2,1)} %get-tuple-element.31), calls=%async_computation | async-start | bytes 2097152 | tf_op jit(solution)/shard_map/all_to_all | solution.py:130
  35.1 1.7 copy-start.17
  60.2 35.8 %all-to-all-start.1 = ((bf16[64,64,128]{2,1,0:T(8,128)(2,1)}), bf16[64,64,128]{2,1,0:T(8,128)(2,1)}, u32[]{:S(2)}, u32[]{:S(2)}) async-start(bf16[64,64,128]{2,1,0:T(8,128)(2,1)} %broadcast_select_fusion), calls=%async_computation.1 | async-start | bytes 2097152 | tf_op jit(solution)/shard_map/all_to_all | solution.py:159
  70.4 0.9 copy-start.2
  70.4 0.9 copy-start.14
  70.4 23.9 %copy-start.20 = (bf16[1024,64]{0,1:T(8,128)(2,1)S(1)}, bf16[1024,64]{0,1:T(8,128)(2,1)}, u32[]{:S(2)}) copy-start(bf16[1024,64]{0,1:T(8,128)(2,1)} %param.16) | copy-start | bytes 393220
  71.1 23.4 %copy-start.19 = (s32[128]{0:T(128)S(1)}, s32[128]{0:T(128)}, u32[]{:S(2)}) copy-start(s32[128]{0:T(128)} %param.20) | copy-start | bytes 1540
  94.3 0.7 copy-start.9
  94.3 0.8 copy-start.11
  98.0 0.9 copy-start.3
  98.0 0.9 copy-start.7
  98.9 14.1 %copy-start.4 = (bf16[32,8,2,128]{3,1,2,0:T(8,128)(2,1)S(1)}, bf16[32,8,2,128]{3,1,2,0:T(8,128)(2,1)}, u32[]{:S(2)}) copy-start(bf16[32,8,2,128]{3,1,2,0:T(8,128)(2,1)} %copy.44) | copy-start | bytes 393220
  98.9 14.1 %copy-start.10 = (bf16[16,1,64,128]{3,2,1,0:T(8,128)(2,1)S(1)}, bf16[16,1,64,128]{3,2,1,0:T(8,128)(2,1)}, u32[]{:S(2)}) copy-start(bf16[16,1,64,128]{3,2,1,0:T(8,128)(2,1)} %copy-done.9) | copy-start | bytes 786436
  98.9 14.1 %copy-start.12 = (bf16[16,1,64,128]{3,2,1,0:T(8,128)(2,1)S(1)}, bf16[16,1,64,128]{3,2,1,0:T(8,128)(2,1)}, u32[]{:S(2)}) copy-start(bf16[16,1,64,128]{3,2,1,0:T(8,128)(2,1)} %copy-done.11) | copy-start | bytes 786436
  98.9 14.1 %copy-start.15 = (f32[64,256]{1,0:T(8,128)S(1)}, f32[64,256]{1,0:T(8,128)}, u32[]{:S(2)}) copy-start(f32[64,256]{1,0:T(8,128)} %get-tuple-element.44) | copy-start | bytes 196612
  98.9 14.1 %copy-start.16 = (f32[64,256]{1,0:T(8,128)S(1)}, f32[64,256]{1,0:T(8,128)}, u32[]{:S(2)}) copy-start(f32[64,256]{1,0:T(8,128)} %get-tuple-element.45) | copy-start | bytes 196612
  100.1 23.3 %all-to-all-start.2 = ((bf16[16,64,128]{2,1,0:T(8,128)(2,1)}), bf16[16,64,128]{2,1,0:T(8,128)(2,1)S(1)}, u32[]{:S(2)}, u32[]{:S(2)}) async-start(bf16[16,64,128]{2,1,0:T(8,128)(2,1)} %bitcast.27), calls=%async_computation.2 | async-start | bytes 524288 | tf_op jit(solution)/shard_map/all_to_all | solution.py:203
  111.7 45.7 %all-gather.7.cloned.1.call-start = ((), (), s32[]{:S(2)}) async-start(), calls=%async_computation.6 | async-start | bytes 1114112 | tf_op jit(solution)/shard_map/all_gather | solution.py:205
  113.0 0.8 copy-start.8
  147.5 11.2 %copy-start.5 = (bf16[1024,64]{0,1:T(8,128)(2,1)S(1)}, bf16[1024,64]{0,1:T(8,128)(2,1)}, u32[]{:S(2)}) copy-start(bf16[1024,64]{0,1:T(8,128)(2,1)} %param.18) | copy-start | bytes 393220
  147.6 11.4 %copy-start.6 = (bf16[1024,64]{0,1:T(8,128)(2,1)S(1)}, bf16[1024,64]{0,1:T(8,128)(2,1)}, u32[]{:S(2)}) copy-start(bf16[1024,64]{0,1:T(8,128)(2,1)} %param.19) | copy-start | bytes 393220
  148.5 22.8 %all-to-all-start.4 = ((bf16[64,2,16,128]{3,2,1,0:T(8,128)(2,1)}), bf16[64,2,16,128]{3,2,1,0:T(8,128)(2,1)S(1)}, u32[]{:S(2)}, u32[]{:S(2)}) async-start(bf16[64,2,16,128]{3,2,1,0:T(8,128)(2,1)} %broadcast_in_dim.100), calls=%async_computation.4 | async-start | bytes 1048576 | tf_op jit(solution)/shard_map/all_to_all | solution.py:211
Sparse Core Ops, SparseCore 0:
  10.8 60.8 all-gather.4
  123.6 33.8 all-gather.6

commit v8 on v6

--- a/solution.py
+++ b/solution.py
@@ -175,6 +175,7 @@
         batch_ids[:, None] == jnp.arange(owned, dtype=jnp.int32)[None, :]
     ).astype(BF)
     whole_grad_two = mm(whole_cot, seed_rows, ((1,), (0,))).astype(BF)
+
     back = mm(columns, whole_grad_two, ((0,), (0,)))
     scaled = (back[width:] * inverse).astype(BF)
     own_grad = mm(scaled, dense, ((1,), (0,)))
@@ -199,8 +200,9 @@
     layer_two = jnp.concatenate([hidden, mean_two], axis=0)
 
     twos = mm(whole_grad_two, layer_two, ((1,), (1,))).astype(BF)
+    twos, layer_two, ones = lax.optimization_barrier((twos, layer_two, ones))
     twos = lax.all_to_all(twos.reshape(slices, width, 2 * width), "feat", 0, 0, tiled=True)
-    layer_two, twos = lax.optimization_barrier((layer_two, twos))
+    layer_two, twos, ones = lax.optimization_barrier((layer_two, twos, ones))
     whole_two = lax.all_gather(layer_two, "feat", axis=0, tiled=False)
     pieces = jnp.concatenate([ones, twos.reshape(parts, 1, low, lanes)], axis=1)
     pieces = with_layout_constraint(pieces, Layout(major_to_minor=(0, 1, 2, 3)))
@@ -213,6 +215,7 @@
         in_specs=[pl.BlockSpec(memory_space=pl.ANY)],
         out_shape=[jax.ShapeDtypeStruct((width, depth), F32)] * 4,
         scratch_shapes=[pltpu.VMEM(sums.shape, BF)],
+        compiler_params=pltpu.CompilerParams(vmem_limit_bytes=6 << 20),
     )(sums)
 
     whole_hidden = whole_two[:, :width].reshape(depth, owned)

time: 187 us -> 184 us (0.984)
  blocking collectives: 47.5 us -> 66.8 us
  waiting for transfers between devices: 46.2 us -> 36.2 us
  starting transfers between devices: 46.8 us -> 39.1 us
  matrix products: 9 us -> 6.9 us
    all_to_all x0 -> x1, blocking collectives: none -> 20.4 us  [on_device(): lax.all_to_all(twos.reshape(slices, width, 2 * width), 'feat', 0, 0, tile...]
    all_to_all x1 -> x0, waiting for transfers between devices: 11 us -> none  [on_device(): lax.all_to_all(twos.reshape(slices, width, 2 * width), 'feat', 0, 0, tile...]
    all_to_all x1 -> x0, starting transfers between devices: 7.76 us -> none  [on_device(): lax.all_to_all(twos.reshape(slices, width, 2 * width), 'feat', 0, 0, tile...]
  transfers between devices with their start and end apart: 6 -> 5, of which waited for: 4 -> 3; matrix products, arithmetic and copies ran while one was open for 10% -> 9% of each run, Pallas kernels for 0% -> 0%
where the time goes in v8:
time: 184 us; the launch traced here: 180 us
  blocking collectives  66.8 us (36%)
  starting transfers between devices  39.1 us (21%)
  waiting for transfers between devices  36.2 us (20%)
  between operations  14.5 us (8%)
  local copies, waits for them, and re-layouts  9.5 us (5%)
  matrix products  6.9 us (4%)
  Pallas kernels  4.1 us (2%)
  other arithmetic  3.28 us (2%)
    all_to_all x1, blocking collectives, on_device(): got = lax.all_to_all(pieces, 'dom', 0, 0, tiled=True)  25.5 us
    all_to_all x1, starting transfers between devices, on_device(): halo_feats = lax.all_to_all(send_feats, 'dom', 0, 0, tiled=True)  23.2 us
    all_to_all x1, waiting for transfers between devices, on_device(): halo_feats = lax.all_to_all(send_feats, 'dom', 0, 0, tiled=True)  22.2 us
    all_gather x1, blocking collectives, on_device(): lax.all_gather(mean_one.astype(BF), 'feat', axis=0, tiled=True)  20.8 us
    all_to_all x1, blocking collectives, on_device(): lax.all_to_all(twos.reshape(slices, width, 2 * width), 'feat', 0, 0, tile...  20.4 us
    all_to_all x1, waiting for transfers between devices, on_device(): sums = lax.all_to_all(spread, 'dom', 0, 0, tiled=True)  11.4 us
    all_to_all x1, starting transfers between devices, on_device(): halo_history = lax.all_to_all(send_history, 'dom', 0, 0, tiled=True)  9.37 us
    all_to_all x1, starting transfers between devices, on_device(): sums = lax.all_to_all(spread, 'dom', 0, 0, tiled=True)  6.43 us
  transfers between devices with their start and end apart: 5, of which 3 were waited for; matrix products, arithmetic and copies ran while one was open for 9% of the time, Pallas kernels for 0%

profile of v8, /device:TPU:1, one launch (start us, length us, event | category | flops | bytes accessed | tf_op | source)
XLA Modules:
  0.0 180.3 jit_solution(13090167530539189872)
XLA Ops:
  7.3 3.0 %shard_map.146 = (bf16[64,64,128]{2,1,0:T(8,128)(2,1)}, bf16[19,64,128]{2,1,0:T(8,128)(2,1)}) custom-call(s32[1]{0:T(128)} %bitcast.5.second_ref, s32[32,64]{1,0:T(8,128)} %bitcast.113, bf16[64,256]{1,0:T(8,128)(2,1)} %bitcast.114, bf16[64,128]{1,0:T(8,128)(2,1)} %bitcast.116, bf16[64,1024]{1,0:T(8,128)(2,1)} %bitcast.105, bf16[64,1024]{1,0:T(8,128)(2,1)} %bitcast.106), custom_call_target="tpu_custom_call" | custom-call | tf_op jit(solution)/shard_map/pallas_call | solution.py:109
  10.3 23.2 %all-to-all-start = ((bf16[64,64,128]{2,1,0:T(8,128)(2,1)}), bf16[64,64,128]{2,1,0:T(8,128)(2,1)S(1)}, u32[]{:S(2)}, u32[]{:S(2)}) async-start(bf16[64,64,128]{2,1,0:T(8,128)(2,1)} %get-tuple-element.31), calls=%async_computation | async-start | bytes 2097152 | tf_op jit(solution)/shard_map/all_to_all | solution.py:130
  33.6 0.4 convert_element_type.50
  34.0 0.5 select_reduce_fusion
  34.6 0.7 copy.44
  35.6 0.8 gather_fusion
  36.5 0.3 convert_reduce_fusion
  36.9 1.2 broadcast_select_fusion
  38.0 22.2 %all-to-all-done = bf16[64,64,128]{2,1,0:T(8,128)(2,1)S(1)} async-done(((bf16[64,64,128]{2,1,0:T(8,128)(2,1)}), bf16[64,64,128]{2,1,0:T(8,128)(2,1)S(1)}, u32[]{:S(2)}, u32[]{:S(2)}) %all-to-all-start) | async-done | bytes 1048608 | tf_op jit(solution)/shard_map/all_to_all | solution.py:130
  60.2 9.4 %all-to-all-start.1 = ((bf16[64,64,128]{2,1,0:T(8,128)(2,1)}), bf16[64,64,128]{2,1,0:T(8,128)(2,1)}, u32[]{:S(2)}, u32[]{:S(2)}) async-start(bf16[64,64,128]{2,1,0:T(8,128)(2,1)} %broadcast_select_fusion), calls=%async_computation.1 | async-start | bytes 2097152 | tf_op jit(solution)/shard_map/all_to_all | solution.py:159
  69.7 0.7 gather_fusion.1
  70.5 0.7 convolution_bitcast_fusion.2
  71.6 20.8 %all_gather.17 = bf16[1024,256]{1,0:T(8,128)(2,1)S(1)} all-gather(bf16[64,256]{1,0:T(8,128)(2,1)S(1)} %fusion.7), channel_id=1, replica_groups=mesh['dom'=64,'feat'=16] {'feat'}, dimensions={0}, use_global_device_ids=true | all-gather | bytes 557056 | tf_op jit(solution)/shard_map/all_gather | solution.py:167
  92.4 1.3 fusion.43
  94.0 0.3 convolution_convert_fusion.1
  94.3 0.2 multiply_convert_fusion
  94.6 0.9 fusion.46
  95.5 2.1 %fusion = bf16[8,8,16,128]{3,1,2,0:T(8,128)(2,1)} fusion(bf16[256,256]{1,0:T(8,128)(2,1)S(1)} %bitcast.95, bf16[1024,256]{1,0:T(8,128)(2,1)S(1)} %all_gather.17, bf16[1024,128]{1,0:T(8,128)(2,1)S(1)} %bitcast.111, bf16[1024,128]{1,0:T(8,128)(2,1)S(1)} %bitcast.109, f32[128,256]{1,0:T(8,128)} %fusion.46, f32[64,256]{1,0:T(8,128)S(1)} %get-tuple-element.62, ...), kind=kOutput, calls=%fused_computation.7 | convolution fusion | flops 78970880 | bytes 1639424 | tf_op jit(solution)/shard_map/dot_general | solution.py:14
  97.6 1.0 copy.40
  98.7 2.0 %gather_fusion.2 = bf16[48,64,128]{2,1,0:T(8,128)(2,1)S(1)} fusion(bf16[64,64,128]{2,1,0:T(8,128)(2,1)} %all-to-all-done.1, s32[1024]{0:T(1024)} %copy-done.11), kind=kCustom, calls=%fused_computation.2 | custom fusion | bytes 1573056 | tf_op jit(solution)/shard_map/gather | solution.py:198
  100.7 0.7 convolution_bitcast_fusion.1
  101.6 0.7 pad_maximum_fusion.1
  102.3 0.3 convolution_convert_fusion.2
  102.6 20.4 %all_to_all.25 = bf16[16,64,128]{2,1,0:T(8,128)(2,1)S(1)} all-to-all(bf16[16,64,128]{2,1,0:T(8,128)(2,1)S(1)} %bitcast.100), channel_id=1, replica_groups=mesh['dom'=64,'feat'=16] {'feat'}, dimensions={0} | all-to-all | bytes 524288 | tf_op jit(solution)/shard_map/all_to_all | solution.py:204
  123.1 25.5 %all_to_all.26 = bf16[64,2,16,128]{3,2,1,0:T(8,128)(2,1)S(1)} all-to-all(bf16[64,2,16,128]{3,2,1,0:T(8,128)(2,1)S(1)} %pad_maximum_fusion), channel_id=1, replica_groups=mesh['dom'=64,'feat'=16] {'dom'}, dimensions={0} | all-to-all | bytes 1048576 | tf_op jit(solution)/shard_map/all_to_all | solution.py:209
  148.7 0.9 broadcast_in_dim.100
  149.6 6.4 %all-to-all-start.4 = ((bf16[64,2,16,128]{3,2,1,0:T(8,128)(2,1)}), bf16[64,2,16,128]{3,2,1,0:T(8,128)(2,1)S(1)}, u32[]{:S(2)}, u32[]{:S(2)}) async-start(bf16[64,2,16,128]{3,2,1,0:T(8,128)(2,1)} %broadcast_in_dim.100), calls=%async_computation.4 | async-start | bytes 1048576 | tf_op jit(solution)/shard_map/all_to_all | solution.py:212
  156.0 2.5 %all-gather.7.cloned.1.call-done = bf16[2048,256]{1,0:T(8,128)(2,1)} async-done(((bf16[128,256]{1,0:T(8,128)(2,1)}), bf16[2048,256]{1,0:T(8,128)(2,1)}) %all-gather.7.cloned.1.call-update) | async-done | bytes 1048592 | tf_op jit(solution)/shard_map/all_gather | solution.py:206
  158.5 1.3 fusion.44
  160.1 0.8 fusion.9
  160.9 11.4 %all-to-all-done.4.sums_any = bf16[64,2,16,128]{3,2,1,0:T(8,128)(2,1)S(1)} async-done(((bf16[64,2,16,128]{3,2,1,0:T(8,128)(2,1)}), bf16[64,2,16,128]{3,2,1,0:T(8,128)(2,1)S(1)}, u32[]{:S(2)}, u32[]{:S(2)}) %all-to-all-start.4) | async-done | bytes 524320 | tf_op jit(solution)/shard_map/all_to_all | solution.py:212
  172.4 1.1 shard_map.147
  (62 shorter events, 2.0 us)
Async XLA Ops:
  7.2 87.1 %copy-start = (bf16[1024,64]{0,1:T(8,128)(2,1)S(1)}, bf16[1024,64]{0,1:T(8,128)(2,1)}, u32[]{:S(2)}) copy-start(bf16[1024,64]{0,1:T(8,128)(2,1)} %param.17) | copy-start | bytes 393220
  7.2 26.4 %copy-start.6 = (s32[64,32]{0,1:T(8,128)S(1)}, s32[64,32]{0,1:T(8,128)}, u32[]{:S(2)}) copy-start(s32[64,32]{0,1:T(8,128)} %param.13) | copy-start | bytes 24580
  7.2 26.3 %copy-start.14 = (s32[2,24]{1,0:T(2,128)S(1)}, s32[2,24]{1,0:T(2,128)}, u32[]{:S(2)}) copy-start(s32[2,24]{1,0:T(2,128)} %param.14) | copy-start | bytes 580
  7.2 26.4 %copy-start.1 = (bf16[2,24,128,128]{3,2,1,0:T(8,128)(2,1)S(1)}, bf16[2,24,128,128]{3,2,1,0:T(8,128)(2,1)}, u32[]{:S(2)}) copy-start(bf16[2,24,128,128]{3,2,1,0:T(8,128)(2,1)} %param.15) | copy-start | bytes 4718596
  7.2 85.2 %all-gather.5.cloned.1.call-start = ((), (), s32[]{:S(2)}) async-start(), calls=%async_computation.5 | async-start | bytes 5292032 | tf_op jit(solution)/shard_map/all_gather | solution.py:144
  10.3 49.9 %all-to-all-start = ((bf16[64,64,128]{2,1,0:T(8,128)(2,1)}), bf16[64,64,128]{2,1,0:T(8,128)(2,1)S(1)}, u32[]{:S(2)}, u32[]{:S(2)}) async-start(bf16[64,64,128]{2,1,0:T(8,128)(2,1)} %get-tuple-element.31), calls=%async_computation | async-start | bytes 2097152 | tf_op jit(solution)/shard_map/all_to_all | solution.py:130
  34.5 2.3 %copy-start.8 = (bf16[256,64]{0,1:T(8,128)(2,1)S(1)}, bf16[256,64]{0,1:T(8,128)(2,1)}, u32[]{:S(2)}) copy-start(bf16[256,64]{0,1:T(8,128)(2,1)} %param.12) | copy-start | bytes 98308
  36.8 33.7 %copy-start.12 = (pred[2,24]{1,0:T(4,128)(4,1)}, pred[2,24]{1,0:T(4,128)(4,1)S(1)}, u32[]{:S(2)}) copy-start(pred[2,24]{1,0:T(4,128)(4,1)S(1)} %broadcast_compare_fusion) | copy-start | bytes 148
  36.8 34.4 %copy-start.9 = (f32[2,128]{1,0:T(2,128)}, f32[2,128]{1,0:T(2,128)S(1)}, u32[]{:S(2)}) copy-start(f32[2,128]{1,0:T(2,128)S(1)} %broadcast_divide_fusion) | copy-start | bytes 3076
  60.2 38.5 %all-to-all-start.1 = ((bf16[64,64,128]{2,1,0:T(8,128)(2,1)}), bf16[64,64,128]{2,1,0:T(8,128)(2,1)}, u32[]{:S(2)}, u32[]{:S(2)}) async-start(bf16[64,64,128]{2,1,0:T(8,128)(2,1)} %broadcast_select_fusion), calls=%async_computation.1 | async-start | bytes 2097152 | tf_op jit(solution)/shard_map/all_to_all | solution.py:159
  69.6 89.0 %all-gather.7.cloned.1.call-start = ((), (), s32[]{:S(2)}) async-start(), calls=%async_computation.6 | async-start | bytes 1114112 | tf_op jit(solution)/shard_map/all_gather | solution.py:206
  69.7 1.8 %copy-start.11 = (s32[1024]{0:T(1024)}, s32[1024]{0:T(1024)S(1)}, u32[]{:S(2)}) copy-start(s32[1024]{0:T(1024)S(1)} %pad_clamp_fusion) | copy-start | bytes 12292
  70.5 0.9 copy-start.2
  70.5 0.9 copy-start.7
  70.5 23.2 %copy-start.16 = (bf16[1024,64]{0,1:T(8,128)(2,1)S(1)}, bf16[1024,64]{0,1:T(8,128)(2,1)}, u32[]{:S(2)}) copy-start(bf16[1024,64]{0,1:T(8,128)(2,1)} %param.16) | copy-start | bytes 393220
  71.2 22.7 %copy-start.15 = (s32[128]{0:T(128)S(1)}, s32[128]{0:T(128)}, u32[]{:S(2)}) copy-start(s32[128]{0:T(128)} %param.20) | copy-start | bytes 1540
  93.7 1.8 copy-start.3
  93.7 1.8 copy-start.10
  95.5 5.2 %copy-start.13 = (pred[2,24]{1,0:T(4,128)(4,1)S(1)}, pred[2,24]{1,0:T(4,128)(4,1)}, u32[]{:S(2)}) copy-start(pred[2,24]{1,0:T(4,128)(4,1)} %copy-done.12) | copy-start | bytes 148
  148.6 11.3 %copy-start.4 = (bf16[1024,64]{0,1:T(8,128)(2,1)S(1)}, bf16[1024,64]{0,1:T(8,128)(2,1)}, u32[]{:S(2)}) copy-start(bf16[1024,64]{0,1:T(8,128)(2,1)} %param.18) | copy-start | bytes 393220
  148.7 11.4 %copy-start.5 = (bf16[1024,64]{0,1:T(8,128)(2,1)S(1)}, bf16[1024,64]{0,1:T(8,128)(2,1)}, u32[]{:S(2)}) copy-start(bf16[1024,64]{0,1:T(8,128)(2,1)} %param.19) | copy-start | bytes 393220
  149.6 22.8 %all-to-all-start.4 = ((bf16[64,2,16,128]{3,2,1,0:T(8,128)(2,1)}), bf16[64,2,16,128]{3,2,1,0:T(8,128)(2,1)S(1)}, u32[]{:S(2)}, u32[]{:S(2)}) async-start(bf16[64,2,16,128]{3,2,1,0:T(8,128)(2,1)} %broadcast_in_dim.100), calls=%async_computation.4 | async-start | bytes 1048576 | tf_op jit(solution)/shard_map/all_to_all | solution.py:212
Sparse Core Ops, SparseCore 0:
  10.8 60.9 all-gather.4
  123.2 35.3 all-gather.6

commit v9 on v7

--- a/solution.py
+++ b/solution.py
@@ -18,12 +18,42 @@
 
 
 def lay_out(
-    second_ref, halo_ref, rows_ref, seeds_ref, self_ref, neigh_ref, out_ref, side_ref, picked, sems
+    me_ref,
+    halo_any,
+    rows_any,
+    seeds_any,
+    self_any,
+    neigh_any,
+    out_any,
+    side_any,
+    halo_ref,
+    rows_ref,
+    seeds_ref,
+    self_ref,
+    neigh_ref,
+    picked,
+    side_ref,
+    in_sems,
+    out_sems,
 ):
+    def fetch(source, target, index):
+        copy = pltpu.make_async_copy(source, target, in_sems.at[index])
+        copy.start()
+        return copy
+
+    get_halo = fetch(halo_any, halo_ref, 0)
+    get_rows = fetch(rows_any, rows_ref, 1)
+    get_seeds = fetch(seeds_any, seeds_ref, 2)
+    get_self = fetch(self_any, self_ref, 3)
+    get_neigh = fetch(neigh_any, neigh_ref, 4)
     parts, width, lanes = picked.shape
-    names = jnp.where(halo_ref[...] == second_ref[0], 1.0, 0.0)
+    get_halo.wait()
+    names = jnp.where(halo_ref[...] == 2 * me_ref[0] + 1, 1.0, 0.0)
     names = jnp.max(names, axis=0, keepdims=True)
+    readers = lax.broadcasted_iota(jnp.int32, (1, parts), 1)
+    names = jnp.where(readers == me_ref[0], 2.0, names)
     names = jnp.broadcast_to(names, (lanes, parts)).T
+    get_rows.wait()
     low = rows_ref[:, :lanes].astype(F32)
     high = rows_ref[:, lanes:].astype(F32)
     step = parts // CHUNKS
@@ -31,14 +61,18 @@
     for chunk in range(CHUNKS):
         for reader in range(chunk * step, (chunk + 1) * step):
             name = jnp.broadcast_to(names[reader : reader + 1, :], low.shape)
-            picked[reader] = jnp.where(name > 0.5, high, low).astype(picked.dtype)
+            block = jnp.where(name > 1.5, 0.0, jnp.where(name > 0.5, high, low))
+            picked[reader] = block.astype(picked.dtype)
         part = pl.ds(chunk * step, step)
-        copy = pltpu.make_async_copy(picked.at[part], out_ref.at[part], sems.at[chunk])
+        copy = pltpu.make_async_copy(picked.at[part], out_any.at[part], out_sems.at[chunk])
         copy.start()
         copies.append(copy)
     side_ref[0] = rows_ref[:, :lanes]
     side_ref[1] = rows_ref[:, lanes:]
+    get_seeds.wait()
     side_ref[2] = seeds_ref[...]
+    get_self.wait()
+    get_neigh.wait()
     for pair in range(self_ref.shape[1] // lanes):
         across = slice(pair * lanes, (pair + 1) * lanes)
         own = self_ref[:, across].astype(F32)
@@ -47,6 +81,9 @@
         right = jnp.concatenate([own[:, width:], near[:, width:]], axis=1)
         side_ref[3 + 2 * pair] = left.astype(side_ref.dtype)
         side_ref[4 + 2 * pair] = right.astype(side_ref.dtype)
+    copy = pltpu.make_async_copy(side_ref, side_any, out_sems.at[CHUNKS])
+    copy.start()
+    copies.append(copy)
     for copy in copies:
         copy.wait()
 
@@ -106,32 +143,30 @@
 
     second = own_blocks * me + 1
     slices = self_two_t.shape[1] // width
+    side_shape = (own_blocks + 1 + slices, width, rows)
+    operands = (halo_blocks.T, feats_t, cot_t, self_two_t, neigh_two_t)
     send_feats, side = pl.pallas_call(
         lay_out,
         in_specs=[pl.BlockSpec(memory_space=pltpu.SMEM)]
-        + [pl.BlockSpec(memory_space=pltpu.VMEM)] * 5,
-        out_specs=[pl.BlockSpec(memory_space=pl.ANY), pl.BlockSpec(memory_space=pltpu.VMEM)],
+        + [pl.BlockSpec(memory_space=pl.ANY)] * len(operands),
+        out_specs=[pl.BlockSpec(memory_space=pl.ANY)] * 2,
         out_shape=[
             jax.ShapeDtypeStruct((parts, width, rows), BF),
-            jax.ShapeDtypeStruct((own_blocks + 1 + slices, width, rows), BF),
+            jax.ShapeDtypeStruct(side_shape, BF),
         ],
-        scratch_shapes=[
+        scratch_shapes=[pltpu.VMEM(operand.shape, operand.dtype) for operand in operands]
+        + [
             pltpu.VMEM((parts, width, rows), BF),
-            pltpu.SemaphoreType.DMA((CHUNKS,)),
+            pltpu.VMEM(side_shape, BF),
+            pltpu.SemaphoreType.DMA((len(operands),)),
+            pltpu.SemaphoreType.DMA((CHUNKS + 1,)),
         ],
-    )(
-        second.reshape(1).astype(jnp.int32),
-        halo_blocks.T,
-        feats_t,
-        cot_t,
-        self_two_t,
-        neigh_two_t,
-    )
+    )(me.reshape(1).astype(jnp.int32), *operands)
     halo_feats = lax.all_to_all(send_feats, "dom", 0, 0, tiled=True)
     wanted = lax.dynamic_index_in_dim(halo_blocks, me, 0, keepdims=False)
     is_own = tile_index < own_blocks
     tile_block = wanted[jnp.clip(tile_index - own_blocks, 0, wanted.shape[0] - 1)]
-    tile_owner = jnp.clip(tile_block // own_blocks, 0, parts - 1)
+    tile_slot = jnp.where(is_own, me, jnp.clip(tile_block // own_blocks, 0, parts - 1))
 
     onehot = tile_index[:, :, None] == jnp.arange(own_blocks, dtype=jnp.int32)[None, None, :]
     dense = jnp.sum(
@@ -150,20 +185,21 @@
         whole, own_blocks + 1 + lax.axis_index("feat"), 1, keepdims=False
     ).reshape(-1, 2 * width)
 
-    named = jnp.any(halo_blocks == second, axis=1)[:, None, None]
+    named = jnp.any(halo_blocks == second, axis=1).astype(jnp.int32)
+    named = jnp.where(jnp.arange(parts, dtype=jnp.int32) == me, 2, named)[:, None, None]
     history_t, named = lax.optimization_barrier((history.T, named))
-    send_history = jnp.where(named, history_t[None, :, rows:], history_t[None, :, :rows])
-    send_history, dense, inverse, tile_owner, is_own, halo_feats = lax.optimization_barrier(
-        (send_history, dense, inverse, tile_owner, is_own, halo_feats)
+    send_history = jnp.where(named == 1, history_t[None, :, rows:], history_t[None, :, :rows])
+    send_history = jnp.where(named == 2, jnp.zeros((), BF), send_history)
+    send_history, dense, inverse, tile_slot, halo_feats = lax.optimization_barrier(
+        (send_history, dense, inverse, tile_slot, halo_feats)
     )
     halo_history = lax.all_to_all(send_history, "dom", 0, 0, tiled=True)
 
     def halo_sum(picked):
-        picked = jnp.where(is_own[:, :, None, None], jnp.zeros((), BF), picked)
         out = jnp.einsum("bkfc,bkvc->fbv", picked, tile_weight, preferred_element_type=F32)
         return out.reshape(width, owned)
 
-    mean_one = (halo_sum(halo_feats[tile_owner]) + mm(feats_t, dense, ((1,), (1,)))) * inverse
+    mean_one = (halo_sum(halo_feats[tile_slot]) + mm(feats_t, dense, ((1,), (1,)))) * inverse
     whole_mean_one = lax.all_gather(mean_one.astype(BF), "feat", axis=0, tiled=True)
     pre_one = mm(self_one_t, whole_feats, ((1,), (0,))) + mm(
         neigh_one_t, whole_mean_one, ((1,), (0,))
@@ -180,7 +216,7 @@
         (halo_history, hidden, whole_grad_two)
     )
     mean_two = (
-        (halo_sum(halo_history[tile_owner]) + mm(hidden, dense, ((1,), (1,)))) * inverse
+        (halo_sum(halo_history[tile_slot]) + mm(hidden, dense, ((1,), (1,)))) * inverse
     ).astype(BF)
     layer_two = jnp.concatenate([hidden, mean_two], axis=0)
 

time: 182 us -> 182 us (level)
  transfers between devices with their start and end apart: 6 -> 6, of which waited for: 5 -> 4; matrix products, arithmetic and copies ran while one was open for 9% -> 9% of each run, Pallas kernels for 0% -> 0%
where the time goes in v9:
time: 182 us; the launch traced here: 178 us
  starting transfers between devices  50.4 us (28%)
  waiting for transfers between devices  45.2 us (25%)
  blocking collectives  44.8 us (25%)
  between operations  14.5 us (8%)
  local copies, waits for them, and re-layouts  10.1 us (6%)
  matrix products  6.85 us (4%)
  other arithmetic  3.31 us (2%)
  Pallas kernels  3.25 us (2%)
    all_to_all x1, blocking collectives, on_device(): got = lax.all_to_all(pieces, 'dom', 0, 0, tiled=True)  24 us
    all_to_all x1, starting transfers between devices, on_device(): halo_feats = lax.all_to_all(send_feats, 'dom', 0, 0, tiled=True)  23.2 us
    all_to_all x1, waiting for transfers between devices, on_device(): halo_feats = lax.all_to_all(send_feats, 'dom', 0, 0, tiled=True)  22.2 us
    all_gather x1, blocking collectives, on_device(): lax.all_gather(mean_one.astype(BF), 'feat', axis=0, tiled=True)  20.9 us
    all_to_all x1, waiting for transfers between devices, on_device(): sums = lax.all_to_all(spread, 'dom', 0, 0, tiled=True)  11.4 us
    all_to_all x1, starting transfers between devices, on_device(): lax.all_to_all(twos.reshape(slices, width, 2 * width), 'feat', 0, 0, tile...  11.3 us
    all_to_all x1, starting transfers between devices, on_device(): halo_history = lax.all_to_all(send_history, 'dom', 0, 0, tiled=True)  9.37 us
    all_to_all x1, waiting for transfers between devices, on_device(): lax.all_to_all(twos.reshape(slices, width, 2 * width), 'feat', 0, 0, tile...  8.99 us
  transfers between devices with their start and end apart: 6, of which 4 were waited for; matrix products, arithmetic and copies ran while one was open for 9% of the time, Pallas kernels for 0%

profile of v9, /device:TPU:1, one launch (start us, length us, event | category | flops | bytes accessed | tf_op | source)
XLA Modules:
  0.0 178.3 jit_solution(7043830576348050664)
XLA Ops:
  7.3 2.2 %shard_map.146 = (bf16[64,64,128]{2,1,0:T(8,128)(2,1)}, bf16[19,64,128]{2,1,0:T(8,128)(2,1)}) custom-call(s32[1]{0:T(128)} %bitcast.6.me_ref, s32[32,64]{1,0:T(8,128)} %bitcast.118, bf16[64,256]{1,0:T(8,128)(2,1)} %bitcast.119, bf16[64,128]{1,0:T(8,128)(2,1)} %bitcast.121, bf16[64,1024]{1,0:T(8,128)(2,1)} %bitcast.110, bf16[64,1024]{1,0:T(8,128)(2,1)} %bitcast.111), custom_call_target="tpu_custom_call" | custom-call | tf_op jit(solution)/shard_map/pallas_call | solution.py:148
  9.5 23.2 %all-to-all-start = ((bf16[64,64,128]{2,1,0:T(8,128)(2,1)}), bf16[64,64,128]{2,1,0:T(8,128)(2,1)S(1)}, u32[]{:S(2)}, u32[]{:S(2)}) async-start(bf16[64,64,128]{2,1,0:T(8,128)(2,1)} %get-tuple-element.30), calls=%async_computation | async-start | bytes 2097152 | tf_op jit(solution)/shard_map/all_to_all | solution.py:165
  33.0 0.8 gather_fusion
  33.8 0.4 convert_element_type.65
  34.3 0.5 select_reduce_fusion
  35.0 0.7 copy.44
  36.0 1.2 select_select_fusion
  37.2 22.2 %all-to-all-done = bf16[64,64,128]{2,1,0:T(8,128)(2,1)S(1)} async-done(((bf16[64,64,128]{2,1,0:T(8,128)(2,1)}), bf16[64,64,128]{2,1,0:T(8,128)(2,1)S(1)}, u32[]{:S(2)}, u32[]{:S(2)}) %all-to-all-start) | async-done | bytes 1048608 | tf_op jit(solution)/shard_map/all_to_all | solution.py:165
  59.4 9.4 %all-to-all-start.1 = ((bf16[64,64,128]{2,1,0:T(8,128)(2,1)}), bf16[64,64,128]{2,1,0:T(8,128)(2,1)}, u32[]{:S(2)}, u32[]{:S(2)}) async-start(bf16[64,64,128]{2,1,0:T(8,128)(2,1)} %select_select_fusion), calls=%async_computation.1 | async-start | bytes 2097152 | tf_op jit(solution)/shard_map/all_to_all | solution.py:196
  68.8 0.7 gather_fusion.1
  69.6 0.7 convolution_bitcast_fusion.2
  70.6 20.9 %all_gather.17 = bf16[1024,256]{1,0:T(8,128)(2,1)S(1)} all-gather(bf16[64,256]{1,0:T(8,128)(2,1)S(1)} %fusion.6), channel_id=1, replica_groups=mesh['dom'=64,'feat'=16] {'feat'}, dimensions={0}, use_global_device_ids=true | all-gather | bytes 557056 | tf_op jit(solution)/shard_map/all_gather | solution.py:203
  91.5 2.0 %constant_dynamic-slice_fusion = (bf16[16,1,64,128]{3,2,1,0:T(8,128)(2,1)}, bf16[16,1,64,128]{3,2,1,0:T(8,128)(2,1)S(1)}, bf16[16,1,64,128]{3,2,1,0:T(8,128)(2,1)S(1)}, bf16[16,1,64,128]{3,2,1,0:T(8,128)(2,1)S(1)}) fusion(bf16[16,19,64,128]{3,2,1,0:T(8,128)(2,1)} %bitcast.117, s32[]{:T(128)S(6)} %select_n.56), kind=kLoop, calls=%fused_computation.67 | loop fusion | bytes 2097156 | tf_op jit(solution)/shard_map/jit(dynamic_index_in_dim)/dynamic_slice | solution.py:184
  93.7 0.5 copy-done.9
  94.2 0.3 convolution_convert_fusion.1
  94.6 0.9 add_divide_fusion
  95.5 1.9 %gather_fusion.2 = bf16[48,64,128]{2,1,0:T(8,128)(2,1)S(1)} fusion(bf16[64,64,128]{2,1,0:T(8,128)(2,1)} %all-to-all-done.1, s32[1024]{0:T(1024)S(1)} %pad_clamp_fusion), kind=kCustom, calls=%fused_computation.2 | custom fusion | bytes 1573056 | tf_op jit(solution)/shard_map/gather | solution.py:219
  97.4 0.6 convolution_bitcast_fusion.1
  98.5 1.0 convolution_convert_fusion.2
  99.5 11.3 %all-to-all-start.2 = ((bf16[16,64,128]{2,1,0:T(8,128)(2,1)}), bf16[16,64,128]{2,1,0:T(8,128)(2,1)S(1)}, u32[]{:S(2)}, u32[]{:S(2)}) async-start(bf16[16,64,128]{2,1,0:T(8,128)(2,1)} %bitcast.28), calls=%async_computation.2 | async-start | bytes 524288 | tf_op jit(solution)/shard_map/all_to_all | solution.py:239
  110.9 1.2 fusion.36
  112.2 0.5 fusion
  112.9 0.6 pad_maximum_fusion.1
  113.6 9.0 %all-to-all-done.2 = bf16[16,64,128]{2,1,0:T(8,128)(2,1)S(1)} async-done(((bf16[16,64,128]{2,1,0:T(8,128)(2,1)}), bf16[16,64,128]{2,1,0:T(8,128)(2,1)S(1)}, u32[]{:S(2)}, u32[]{:S(2)}) %all-to-all-start.2) | async-done | bytes 262176 | tf_op jit(solution)/shard_map/all_to_all | solution.py:239
  122.6 24.0 %all_to_all.25 = bf16[64,2,16,128]{3,2,1,0:T(8,128)(2,1)S(1)} all-to-all(bf16[64,2,16,128]{3,2,1,0:T(8,128)(2,1)S(1)} %pad_maximum_fusion), channel_id=1, replica_groups=mesh['dom'=64,'feat'=16] {'dom'}, dimensions={0} | all-to-all | bytes 1048576 | tf_op jit(solution)/shard_map/all_to_all | solution.py:244
  146.7 0.9 broadcast_in_dim.104
  147.6 6.4 %all-to-all-start.4 = ((bf16[64,2,16,128]{3,2,1,0:T(8,128)(2,1)}), bf16[64,2,16,128]{3,2,1,0:T(8,128)(2,1)S(1)}, u32[]{:S(2)}, u32[]{:S(2)}) async-start(bf16[64,2,16,128]{3,2,1,0:T(8,128)(2,1)} %broadcast_in_dim.104), calls=%async_computation.4 | async-start | bytes 1048576 | tf_op jit(solution)/shard_map/all_to_all | solution.py:247
  154.0 2.5 %all-gather.7.cloned.1.call-done = bf16[2048,256]{1,0:T(8,128)(2,1)} async-done(((bf16[128,256]{1,0:T(8,128)(2,1)}), bf16[2048,256]{1,0:T(8,128)(2,1)}) %all-gather.7.cloned.1.call-update) | async-done | bytes 1048592 | tf_op jit(solution)/shard_map/all_gather | solution.py:241
  156.6 1.3 fusion.34
  158.1 0.8 fusion.9
  158.9 11.4 %all-to-all-done.4.sums_any = bf16[64,2,16,128]{3,2,1,0:T(8,128)(2,1)S(1)} async-done(((bf16[64,2,16,128]{3,2,1,0:T(8,128)(2,1)}), bf16[64,2,16,128]{3,2,1,0:T(8,128)(2,1)S(1)}, u32[]{:S(2)}, u32[]{:S(2)}) %all-to-all-start.4) | async-done | bytes 524320 | tf_op jit(solution)/shard_map/all_to_all | solution.py:247
  170.3 1.1 shard_map.147
  (72 shorter events, 2.8 us)
Async XLA Ops:
  7.2 87.4 %copy-start = (bf16[1024,64]{0,1:T(8,128)(2,1)S(1)}, bf16[1024,64]{0,1:T(8,128)(2,1)}, u32[]{:S(2)}) copy-start(bf16[1024,64]{0,1:T(8,128)(2,1)} %param.17) | copy-start | bytes 393220
  7.2 25.5 %copy-start.13 = (s32[64,32]{0,1:T(8,128)S(1)}, s32[64,32]{0,1:T(8,128)}, u32[]{:S(2)}) copy-start(s32[64,32]{0,1:T(8,128)} %param.13) | copy-start | bytes 24580
  7.2 25.5 %copy-start.18 = (s32[2,24]{1,0:T(2,128)S(1)}, s32[2,24]{1,0:T(2,128)}, u32[]{:S(2)}) copy-start(s32[2,24]{1,0:T(2,128)} %param.14) | copy-start | bytes 580
  7.2 26.6 %copy-start.1 = (bf16[2,24,128,128]{3,2,1,0:T(8,128)(2,1)S(1)}, bf16[2,24,128,128]{3,2,1,0:T(8,128)(2,1)}, u32[]{:S(2)}) copy-start(bf16[2,24,128,128]{3,2,1,0:T(8,128)(2,1)} %param.15) | copy-start | bytes 4718596
  7.2 84.3 %all-gather.5.cloned.1.call-start = ((), (), s32[]{:S(2)}) async-start(), calls=%async_computation.5 | async-start | bytes 5292032 | tf_op jit(solution)/shard_map/all_gather | solution.py:179
  9.5 49.9 %all-to-all-start = ((bf16[64,64,128]{2,1,0:T(8,128)(2,1)}), bf16[64,64,128]{2,1,0:T(8,128)(2,1)S(1)}, u32[]{:S(2)}, u32[]{:S(2)}) async-start(bf16[64,64,128]{2,1,0:T(8,128)(2,1)} %get-tuple-element.30), calls=%async_computation | async-start | bytes 2097152 | tf_op jit(solution)/shard_map/all_to_all | solution.py:165
  34.3 1.7 copy-start.17
  59.4 36.1 %all-to-all-start.1 = ((bf16[64,64,128]{2,1,0:T(8,128)(2,1)}), bf16[64,64,128]{2,1,0:T(8,128)(2,1)}, u32[]{:S(2)}, u32[]{:S(2)}) async-start(bf16[64,64,128]{2,1,0:T(8,128)(2,1)} %select_select_fusion), calls=%async_computation.1 | async-start | bytes 2097152 | tf_op jit(solution)/shard_map/all_to_all | solution.py:196
  69.6 0.9 copy-start.2
  69.6 0.9 copy-start.14
  70.2 23.2 %copy-start.20 = (bf16[1024,64]{0,1:T(8,128)(2,1)S(1)}, bf16[1024,64]{0,1:T(8,128)(2,1)}, u32[]{:S(2)}) copy-start(bf16[1024,64]{0,1:T(8,128)(2,1)} %param.16) | copy-start | bytes 393220
  70.2 24.0 %copy-start.19 = (s32[128]{0:T(128)S(1)}, s32[128]{0:T(128)}, u32[]{:S(2)}) copy-start(s32[128]{0:T(128)} %param.20) | copy-start | bytes 1540
  93.4 0.7 copy-start.9
  93.4 0.8 copy-start.11
  97.4 0.9 copy-start.3
  97.4 0.9 copy-start.7
  98.3 13.8 %copy-start.4 = (bf16[32,8,2,128]{3,1,2,0:T(8,128)(2,1)S(1)}, bf16[32,8,2,128]{3,1,2,0:T(8,128)(2,1)}, u32[]{:S(2)}) copy-start(bf16[32,8,2,128]{3,1,2,0:T(8,128)(2,1)} %copy.44) | copy-start | bytes 393220
  98.3 13.8 %copy-start.10 = (bf16[16,1,64,128]{3,2,1,0:T(8,128)(2,1)S(1)}, bf16[16,1,64,128]{3,2,1,0:T(8,128)(2,1)}, u32[]{:S(2)}) copy-start(bf16[16,1,64,128]{3,2,1,0:T(8,128)(2,1)} %copy-done.9) | copy-start | bytes 786436
  98.3 13.8 %copy-start.12 = (bf16[16,1,64,128]{3,2,1,0:T(8,128)(2,1)S(1)}, bf16[16,1,64,128]{3,2,1,0:T(8,128)(2,1)}, u32[]{:S(2)}) copy-start(bf16[16,1,64,128]{3,2,1,0:T(8,128)(2,1)} %copy-done.11) | copy-start | bytes 786436
  98.3 13.8 %copy-start.15 = (f32[64,256]{1,0:T(8,128)S(1)}, f32[64,256]{1,0:T(8,128)}, u32[]{:S(2)}) copy-start(f32[64,256]{1,0:T(8,128)} %get-tuple-element.42) | copy-start | bytes 196612
  98.3 13.8 %copy-start.16 = (f32[64,256]{1,0:T(8,128)S(1)}, f32[64,256]{1,0:T(8,128)}, u32[]{:S(2)}) copy-start(f32[64,256]{1,0:T(8,128)} %get-tuple-element.43) | copy-start | bytes 196612
  99.5 23.0 %all-to-all-start.2 = ((bf16[16,64,128]{2,1,0:T(8,128)(2,1)}), bf16[16,64,128]{2,1,0:T(8,128)(2,1)S(1)}, u32[]{:S(2)}, u32[]{:S(2)}) async-start(bf16[16,64,128]{2,1,0:T(8,128)(2,1)} %bitcast.28), calls=%async_computation.2 | async-start | bytes 524288 | tf_op jit(solution)/shard_map/all_to_all | solution.py:239
  110.9 45.7 %all-gather.7.cloned.1.call-start = ((), (), s32[]{:S(2)}) async-start(), calls=%async_computation.6 | async-start | bytes 1114112 | tf_op jit(solution)/shard_map/all_gather | solution.py:241
  112.2 0.8 copy-start.8
  146.6 11.3 %copy-start.5 = (bf16[1024,64]{0,1:T(8,128)(2,1)S(1)}, bf16[1024,64]{0,1:T(8,128)(2,1)}, u32[]{:S(2)}) copy-start(bf16[1024,64]{0,1:T(8,128)(2,1)} %param.18) | copy-start | bytes 393220
  146.7 11.4 %copy-start.6 = (bf16[1024,64]{0,1:T(8,128)(2,1)S(1)}, bf16[1024,64]{0,1:T(8,128)(2,1)}, u32[]{:S(2)}) copy-start(bf16[1024,64]{0,1:T(8,128)(2,1)} %param.19) | copy-start | bytes 393220
  147.6 22.8 %all-to-all-start.4 = ((bf16[64,2,16,128]{3,2,1,0:T(8,128)(2,1)}), bf16[64,2,16,128]{3,2,1,0:T(8,128)(2,1)S(1)}, u32[]{:S(2)}, u32[]{:S(2)}) async-start(bf16[64,2,16,128]{3,2,1,0:T(8,128)(2,1)} %broadcast_in_dim.104), calls=%async_computation.4 | async-start | bytes 1048576 | tf_op jit(solution)/shard_map/all_to_all | solution.py:247
Sparse Core Ops, SparseCore 0:
  10.8 60.8 all-gather.4
  122.7 33.8 all-gather.6

commit v10 on v9

--- a/solution.py
+++ b/solution.py
@@ -15,6 +15,17 @@
 
 
 CHUNKS = 4
+SIDE = 8
+MEMBERS = [(r % SIDE) * SIDE + (r // SIDE + r) % SIDE for r in range(SIDE * SIDE)]
+
+
+def member_of(partition):
+    first, second = partition // SIDE, partition % SIDE
+    return (second - first + SIDE) % SIDE * SIDE + first
+
+
+def exchange(pieces):
+    return lax.all_to_all(pieces, "dom", 0, 0, axis_index_groups=[MEMBERS], tiled=True)
 
 
 def lay_out(
@@ -60,7 +71,8 @@
     copies = []
     for chunk in range(CHUNKS):
         for reader in range(chunk * step, (chunk + 1) * step):
-            name = jnp.broadcast_to(names[reader : reader + 1, :], low.shape)
+            named = MEMBERS[reader]
+            name = jnp.broadcast_to(names[named : named + 1, :], low.shape)
             block = jnp.where(name > 1.5, 0.0, jnp.where(name > 0.5, high, low))
             picked[reader] = block.astype(picked.dtype)
         part = pl.ds(chunk * step, step)
@@ -162,11 +174,12 @@
             pltpu.SemaphoreType.DMA((CHUNKS + 1,)),
         ],
     )(me.reshape(1).astype(jnp.int32), *operands)
-    halo_feats = lax.all_to_all(send_feats, "dom", 0, 0, tiled=True)
+    halo_feats = exchange(send_feats)
     wanted = lax.dynamic_index_in_dim(halo_blocks, me, 0, keepdims=False)
     is_own = tile_index < own_blocks
     tile_block = wanted[jnp.clip(tile_index - own_blocks, 0, wanted.shape[0] - 1)]
-    tile_slot = jnp.where(is_own, me, jnp.clip(tile_block // own_blocks, 0, parts - 1))
+    tile_owner = jnp.clip(tile_block // own_blocks, 0, parts - 1)
+    tile_slot = member_of(jnp.where(is_own, me, tile_owner))
 
     onehot = tile_index[:, :, None] == jnp.arange(own_blocks, dtype=jnp.int32)[None, None, :]
     dense = jnp.sum(
@@ -186,14 +199,15 @@
     ).reshape(-1, 2 * width)
 
     named = jnp.any(halo_blocks == second, axis=1).astype(jnp.int32)
-    named = jnp.where(jnp.arange(parts, dtype=jnp.int32) == me, 2, named)[:, None, None]
+    named = jnp.where(jnp.arange(parts, dtype=jnp.int32) == me, 2, named)
+    named = named[jnp.array(MEMBERS, dtype=jnp.int32)][:, None, None]
     history_t, named = lax.optimization_barrier((history.T, named))
     send_history = jnp.where(named == 1, history_t[None, :, rows:], history_t[None, :, :rows])
     send_history = jnp.where(named == 2, jnp.zeros((), BF), send_history)
     send_history, dense, inverse, tile_slot, halo_feats = lax.optimization_barrier(
         (send_history, dense, inverse, tile_slot, halo_feats)
     )
-    halo_history = lax.all_to_all(send_history, "dom", 0, 0, tiled=True)
+    halo_history = exchange(send_history)
 
     def halo_sum(picked):
         out = jnp.einsum("bkfc,bkvc->fbv", picked, tile_weight, preferred_element_type=F32)
@@ -241,10 +255,10 @@
     whole_two = lax.all_gather(layer_two, "feat", axis=0, tiled=False)
     pieces = jnp.concatenate([ones, twos.reshape(parts, 1, low, lanes)], axis=1)
     pieces = with_layout_constraint(pieces, Layout(major_to_minor=(0, 1, 2, 3)))
-    got = lax.all_to_all(pieces, "dom", 0, 0, tiled=True)
+    got = exchange(pieces)
     mine = jnp.sum(got.astype(F32), axis=0, keepdims=True).astype(BF)
     spread = jnp.broadcast_to(mine, pieces.shape)
-    sums = lax.all_to_all(spread, "dom", 0, 0, tiled=True)
+    sums = exchange(spread)
     grads = pl.pallas_call(
         unpack,
         in_specs=[pl.BlockSpec(memory_space=pl.ANY)],

time: 182 us -> 180 us (0.989); the launches traced: 178 us -> 179 us
  starting transfers between devices: 50.4 us -> 47.7 us
    all_to_all x3, starting transfers between devices: 39 us -> 36.2 us  [exchange(): lax.all_to_all(pieces, 'dom', 0, 0, axis_index_groups=[MEMBERS], tiled=True)]
    all_to_all x3, waiting for transfers between devices: 33.6 us -> 35.5 us  [exchange(): lax.all_to_all(pieces, 'dom', 0, 0, axis_index_groups=[MEMBERS], tiled=True)]
where the time goes in v10:
time: 180 us; the launch traced here: 179 us
  starting transfers between devices  47.7 us (26%)
  waiting for transfers between devices  46.8 us (26%)
  blocking collectives  45.8 us (25%)
  between operations  14.5 us (8%)
  local copies, waits for them, and re-layouts  10.5 us (6%)
  matrix products  6.86 us (4%)
  other arithmetic  3.33 us (2%)
  Pallas kernels  3.15 us (2%)
    all_to_all x3, starting transfers between devices, exchange(): lax.all_to_all(pieces, 'dom', 0, 0, axis_index_groups=[MEMBERS], tiled=True)  36.2 us
    all_to_all x3, waiting for transfers between devices, exchange(): lax.all_to_all(pieces, 'dom', 0, 0, axis_index_groups=[MEMBERS], tiled=True)  35.5 us
    all_to_all x1, blocking collectives, exchange(): lax.all_to_all(pieces, 'dom', 0, 0, axis_index_groups=[MEMBERS], tiled=True)  24.2 us
    all_gather x1, blocking collectives, on_device(): lax.all_gather(mean_one.astype(BF), 'feat', axis=0, tiled=True)  21.6 us
    all_to_all x1, starting transfers between devices, on_device(): lax.all_to_all(twos.reshape(slices, width, 2 * width), 'feat', 0, 0, tile...  11.4 us
    all_to_all x1, waiting for transfers between devices, on_device(): lax.all_to_all(twos.reshape(slices, width, 2 * width), 'feat', 0, 0, tile...  8.99 us
    dot_general x10, matrix products, mm(): return lax.dot_general(a, b, (dims, ((), ())), preferred_element_type=F32)  5.58 us
  transfers between devices with their start and end apart: 6, of which 4 were waited for; matrix products, arithmetic and copies ran while one was open for 9% of the time, Pallas kernels for 0%

profile of v10, /device:TPU:1, one launch (start us, length us, event | category | flops | bytes accessed | tf_op | source)
XLA Modules:
  0.0 178.6 jit_solution(18218303655117185652)
XLA Ops:
  7.3 2.1 %shard_map.155 = (bf16[64,64,128]{2,1,0:T(8,128)(2,1)}, bf16[19,64,128]{2,1,0:T(8,128)(2,1)}) custom-call(s32[1]{0:T(128)} %bitcast.6.me_ref, s32[32,64]{1,0:T(8,128)} %bitcast.117, bf16[64,256]{1,0:T(8,128)(2,1)} %bitcast.118, bf16[64,128]{1,0:T(8,128)(2,1)} %bitcast.120, bf16[64,1024]{1,0:T(8,128)(2,1)} %bitcast.109, bf16[64,1024]{1,0:T(8,128)(2,1)} %bitcast.110), custom_call_target="tpu_custom_call" | custom-call | tf_op jit(solution)/shard_map/pallas_call | solution.py:160
  9.4 23.3 %all-to-all-start = ((bf16[64,64,128]{2,1,0:T(8,128)(2,1)}), bf16[64,64,128]{2,1,0:T(8,128)(2,1)S(1)}, u32[]{:S(2)}, u32[]{:S(2)}) async-start(bf16[64,64,128]{2,1,0:T(8,128)(2,1)} %get-tuple-element.30), calls=%async_computation | async-start | bytes 2097152 | tf_op jit(solution)/shard_map/all_to_all | solution.py:28
  32.8 0.8 gather_fusion
  33.8 0.8 gather_fusion.1
  34.7 0.4 convert_element_type.54
  35.1 0.5 select_reduce_fusion
  35.8 0.7 copy.45
  36.8 1.2 select_select_fusion
  38.0 22.9 %all-to-all-done = bf16[64,64,128]{2,1,0:T(8,128)(2,1)S(1)} async-done(((bf16[64,64,128]{2,1,0:T(8,128)(2,1)}), bf16[64,64,128]{2,1,0:T(8,128)(2,1)S(1)}, u32[]{:S(2)}, u32[]{:S(2)}) %all-to-all-start) | async-done | bytes 1048608 | tf_op jit(solution)/shard_map/all_to_all | solution.py:28
  60.9 7.0 %all-to-all-start.1 = ((bf16[64,64,128]{2,1,0:T(8,128)(2,1)}), bf16[64,64,128]{2,1,0:T(8,128)(2,1)}, u32[]{:S(2)}, u32[]{:S(2)}) async-start(bf16[64,64,128]{2,1,0:T(8,128)(2,1)} %select_select_fusion), calls=%async_computation.1 | async-start | bytes 2097152 | tf_op jit(solution)/shard_map/all_to_all | solution.py:28
  68.1 0.7 gather_fusion.2
  68.8 0.6 convolution_bitcast_fusion.2
  69.9 21.6 %all_gather.17 = bf16[1024,256]{1,0:T(8,128)(2,1)S(1)} all-gather(bf16[64,256]{1,0:T(8,128)(2,1)S(1)} %fusion.6), channel_id=1, replica_groups=mesh['dom'=64,'feat'=16] {'feat'}, dimensions={0}, use_global_device_ids=true | all-gather | bytes 557056 | tf_op jit(solution)/shard_map/all_gather | solution.py:217
  91.5 2.0 %constant_dynamic-slice_fusion = (bf16[16,1,64,128]{3,2,1,0:T(8,128)(2,1)}, bf16[16,1,64,128]{3,2,1,0:T(8,128)(2,1)S(1)}, bf16[16,1,64,128]{3,2,1,0:T(8,128)(2,1)S(1)}, bf16[16,1,64,128]{3,2,1,0:T(8,128)(2,1)S(1)}) fusion(bf16[16,19,64,128]{3,2,1,0:T(8,128)(2,1)} %bitcast.116, s32[]{:T(128)S(6)} %select_n.70), kind=kLoop, calls=%fused_computation.82 | loop fusion | bytes 2097156 | tf_op jit(solution)/shard_map/jit(dynamic_index_in_dim)/dynamic_slice | solution.py:197
  93.7 0.3 convolution_convert_fusion.1
  94.2 0.9 add_divide_fusion
  95.1 1.9 %gather_fusion.3 = bf16[48,64,128]{2,1,0:T(8,128)(2,1)S(1)} fusion(bf16[64,64,128]{2,1,0:T(8,128)(2,1)} %all-to-all-done.1, s32[1024]{0:T(1024)S(1)} %pad_clamp_fusion), kind=kCustom, calls=%fused_computation.3 | custom fusion | bytes 1573056 | tf_op jit(solution)/shard_map/gather | solution.py:233
  97.0 0.6 convolution_bitcast_fusion.1
  98.1 1.0 convolution_convert_fusion.2
  99.2 11.4 %all-to-all-start.2 = ((bf16[16,64,128]{2,1,0:T(8,128)(2,1)}), bf16[16,64,128]{2,1,0:T(8,128)(2,1)S(1)}, u32[]{:S(2)}, u32[]{:S(2)}) async-start(bf16[16,64,128]{2,1,0:T(8,128)(2,1)} %bitcast.28), calls=%async_computation.2 | async-start | bytes 524288 | tf_op jit(solution)/shard_map/all_to_all | solution.py:253
  110.6 1.2 fusion.40
  111.9 0.5 fusion
  112.7 0.6 pad_maximum_fusion.1
  113.3 9.0 %all-to-all-done.2 = bf16[16,64,128]{2,1,0:T(8,128)(2,1)S(1)} async-done(((bf16[16,64,128]{2,1,0:T(8,128)(2,1)}), bf16[16,64,128]{2,1,0:T(8,128)(2,1)S(1)}, u32[]{:S(2)}, u32[]{:S(2)}) %all-to-all-start.2) | async-done | bytes 262176 | tf_op jit(solution)/shard_map/all_to_all | solution.py:253
  122.4 24.2 %all_to_all.25 = bf16[64,2,16,128]{3,2,1,0:T(8,128)(2,1)S(1)} all-to-all(bf16[64,2,16,128]{3,2,1,0:T(8,128)(2,1)S(1)} %pad_maximum_fusion), channel_id=1, replica_groups={{0,144,288,432,576,720,864,1008,16,160,304,448,592,736,880,896,32,176,3..., dimensions={0} | all-to-all | bytes 1048576 | tf_op jit(solution)/shard_map/all_to_all | solution.py:28
  146.7 0.9 broadcast_in_dim.111
  147.6 5.8 %all-to-all-start.4 = ((bf16[64,2,16,128]{3,2,1,0:T(8,128)(2,1)}), bf16[64,2,16,128]{3,2,1,0:T(8,128)(2,1)S(1)}, u32[]{:S(2)}, u32[]{:S(2)}) async-start(bf16[64,2,16,128]{3,2,1,0:T(8,128)(2,1)} %broadcast_in_dim.111), calls=%async_computation.4 | async-start | bytes 1048576 | tf_op jit(solution)/shard_map/all_to_all | solution.py:28
  153.4 2.3 %all-gather.7.cloned.1.call-done = bf16[2048,256]{1,0:T(8,128)(2,1)} async-done(((bf16[128,256]{1,0:T(8,128)(2,1)}), bf16[2048,256]{1,0:T(8,128)(2,1)}) %all-gather.7.cloned.1.call-update) | async-done | bytes 1048592 | tf_op jit(solution)/shard_map/all_gather | solution.py:255
  155.7 1.3 fusion.38
  157.3 0.8 fusion.9
  158.1 12.6 %all-to-all-done.4.sums_any = bf16[64,2,16,128]{3,2,1,0:T(8,128)(2,1)S(1)} async-done(((bf16[64,2,16,128]{3,2,1,0:T(8,128)(2,1)}), bf16[64,2,16,128]{3,2,1,0:T(8,128)(2,1)S(1)}, u32[]{:S(2)}, u32[]{:S(2)}) %all-to-all-start.4) | async-done | bytes 524320 | tf_op jit(solution)/shard_map/all_to_all | solution.py:28
  170.7 1.1 shard_map.156
  (76 shorter events, 3.0 us)
Async XLA Ops:
  7.2 87.1 %copy-start = (bf16[1024,64]{0,1:T(8,128)(2,1)S(1)}, bf16[1024,64]{0,1:T(8,128)(2,1)}, u32[]{:S(2)}) copy-start(bf16[1024,64]{0,1:T(8,128)(2,1)} %param.18) | copy-start | bytes 393220
  7.2 25.6 %copy-start.19 = (s32[64]{0:T(128)S(1)}, s32[64]{0:T(128)}, u32[]{:S(2)}) copy-start(s32[64]{0:T(128)} %constant.101) | copy-start | bytes 772
  7.2 25.5 %copy-start.13 = (s32[64,32]{0,1:T(8,128)S(1)}, s32[64,32]{0,1:T(8,128)}, u32[]{:S(2)}) copy-start(s32[64,32]{0,1:T(8,128)} %param.14) | copy-start | bytes 24580
  7.2 25.5 %copy-start.18 = (s32[2,24]{1,0:T(2,128)S(1)}, s32[2,24]{1,0:T(2,128)}, u32[]{:S(2)}) copy-start(s32[2,24]{1,0:T(2,128)} %param.15) | copy-start | bytes 580
  7.2 84.3 %all-gather.5.cloned.1.call-start = ((), (), s32[]{:S(2)}) async-start(), calls=%async_computation.5 | async-start | bytes 5292032 | tf_op jit(solution)/shard_map/all_gather | solution.py:192
  9.3 25.4 %copy-start.1 = (bf16[2,24,128,128]{3,2,1,0:T(8,128)(2,1)S(1)}, bf16[2,24,128,128]{3,2,1,0:T(8,128)(2,1)}, u32[]{:S(2)}) copy-start(bf16[2,24,128,128]{3,2,1,0:T(8,128)(2,1)} %param.16) | copy-start | bytes 4718596
  9.4 51.6 %all-to-all-start = ((bf16[64,64,128]{2,1,0:T(8,128)(2,1)}), bf16[64,64,128]{2,1,0:T(8,128)(2,1)S(1)}, u32[]{:S(2)}, u32[]{:S(2)}) async-start(bf16[64,64,128]{2,1,0:T(8,128)(2,1)} %get-tuple-element.30), calls=%async_computation | async-start | bytes 2097152 | tf_op jit(solution)/shard_map/all_to_all | solution.py:28
  35.1 1.7 copy-start.17
  60.9 34.2 %all-to-all-start.1 = ((bf16[64,64,128]{2,1,0:T(8,128)(2,1)}), bf16[64,64,128]{2,1,0:T(8,128)(2,1)}, u32[]{:S(2)}, u32[]{:S(2)}) async-start(bf16[64,64,128]{2,1,0:T(8,128)(2,1)} %select_select_fusion), calls=%async_computation.1 | async-start | bytes 2097152 | tf_op jit(solution)/shard_map/all_to_all | solution.py:28
  68.8 0.9 copy-start.2
  68.8 0.9 copy-start.14
  68.8 24.6 %copy-start.21 = (bf16[1024,64]{0,1:T(8,128)(2,1)S(1)}, bf16[1024,64]{0,1:T(8,128)(2,1)}, u32[]{:S(2)}) copy-start(bf16[1024,64]{0,1:T(8,128)(2,1)} %param.17) | copy-start | bytes 393220
  69.5 24.2 %copy-start.20 = (s32[128]{0:T(128)S(1)}, s32[128]{0:T(128)}, u32[]{:S(2)}) copy-start(s32[128]{0:T(128)} %param.21) | copy-start | bytes 1540
  93.4 0.7 copy-start.9
  93.4 0.8 copy-start.11
  97.0 0.9 copy-start.3
  97.0 0.9 copy-start.7
  97.9 13.9 %copy-start.4 = (bf16[32,8,2,128]{3,1,2,0:T(8,128)(2,1)S(1)}, bf16[32,8,2,128]{3,1,2,0:T(8,128)(2,1)}, u32[]{:S(2)}) copy-start(bf16[32,8,2,128]{3,1,2,0:T(8,128)(2,1)} %copy.45) | copy-start | bytes 393220
  97.9 13.9 %copy-start.10 = (bf16[16,1,64,128]{3,2,1,0:T(8,128)(2,1)S(1)}, bf16[16,1,64,128]{3,2,1,0:T(8,128)(2,1)}, u32[]{:S(2)}) copy-start(bf16[16,1,64,128]{3,2,1,0:T(8,128)(2,1)} %copy-done.9) | copy-start | bytes 786436
  97.9 14.0 %copy-start.12 = (bf16[16,1,64,128]{3,2,1,0:T(8,128)(2,1)S(1)}, bf16[16,1,64,128]{3,2,1,0:T(8,128)(2,1)}, u32[]{:S(2)}) copy-start(bf16[16,1,64,128]{3,2,1,0:T(8,128)(2,1)} %copy-done.11) | copy-start | bytes 786436
  97.9 14.0 %copy-start.15 = (f32[64,256]{1,0:T(8,128)S(1)}, f32[64,256]{1,0:T(8,128)}, u32[]{:S(2)}) copy-start(f32[64,256]{1,0:T(8,128)} %get-tuple-element.42) | copy-start | bytes 196612
  98.0 14.0 %copy-start.16 = (f32[64,256]{1,0:T(8,128)S(1)}, f32[64,256]{1,0:T(8,128)}, u32[]{:S(2)}) copy-start(f32[64,256]{1,0:T(8,128)} %get-tuple-element.43) | copy-start | bytes 196612
  99.2 23.1 %all-to-all-start.2 = ((bf16[16,64,128]{2,1,0:T(8,128)(2,1)}), bf16[16,64,128]{2,1,0:T(8,128)(2,1)S(1)}, u32[]{:S(2)}, u32[]{:S(2)}) async-start(bf16[16,64,128]{2,1,0:T(8,128)(2,1)} %bitcast.28), calls=%async_computation.2 | async-start | bytes 524288 | tf_op jit(solution)/shard_map/all_to_all | solution.py:253
  110.6 45.1 %all-gather.7.cloned.1.call-start = ((), (), s32[]{:S(2)}) async-start(), calls=%async_computation.6 | async-start | bytes 1114112 | tf_op jit(solution)/shard_map/all_gather | solution.py:255
  111.9 0.8 copy-start.8
  146.6 10.5 %copy-start.5 = (bf16[1024,64]{0,1:T(8,128)(2,1)S(1)}, bf16[1024,64]{0,1:T(8,128)(2,1)}, u32[]{:S(2)}) copy-start(bf16[1024,64]{0,1:T(8,128)(2,1)} %param.19) | copy-start | bytes 393220
  146.7 10.6 %copy-start.6 = (bf16[1024,64]{0,1:T(8,128)(2,1)S(1)}, bf16[1024,64]{0,1:T(8,128)(2,1)}, u32[]{:S(2)}) copy-start(bf16[1024,64]{0,1:T(8,128)(2,1)} %param.20) | copy-start | bytes 393220
  147.6 23.1 %all-to-all-start.4 = ((bf16[64,2,16,128]{3,2,1,0:T(8,128)(2,1)}), bf16[64,2,16,128]{3,2,1,0:T(8,128)(2,1)S(1)}, u32[]{:S(2)}, u32[]{:S(2)}) async-start(bf16[64,2,16,128]{3,2,1,0:T(8,128)(2,1)} %broadcast_in_dim.111), calls=%async_computation.4 | async-start | bytes 1048576 | tf_op jit(solution)/shard_map/all_to_all | solution.py:28
Sparse Core Ops, SparseCore 0:
  10.8 60.8 all-gather.4
  122.5 33.2 all-gather.6

commit v11 on v10

--- a/solution.py
+++ b/solution.py
@@ -19,13 +19,22 @@
 MEMBERS = [(r % SIDE) * SIDE + (r // SIDE + r) % SIDE for r in range(SIDE * SIDE)]
 
 
-def member_of(partition):
+BACKWARD = [MEMBERS[-r % len(MEMBERS)] for r in range(len(MEMBERS))]
+
+
+def member_of(partition, turned):
     first, second = partition // SIDE, partition % SIDE
-    return (second - first + SIDE) % SIDE * SIDE + first
+    place = (second - first + SIDE) % SIDE * SIDE + first
+    return jnp.where(turned == 1, (len(MEMBERS) - place) % len(MEMBERS), place)
 
 
 def exchange(pieces):
-    return lax.all_to_all(pieces, "dom", 0, 0, axis_index_groups=[MEMBERS], tiled=True)
+    feats = lax.axis_size("feat")
+    groups = [
+        [part * feats + feat for part in (BACKWARD if feat % 2 else MEMBERS)]
+        for feat in range(feats)
+    ]
+    return lax.all_to_all(pieces, ("dom", "feat"), 0, 0, axis_index_groups=groups, tiled=True)
 
 
 def lay_out(
@@ -42,6 +51,7 @@
     seeds_ref,
     self_ref,
     neigh_ref,
+    names_ref,
     picked,
     side_ref,
     in_sems,
@@ -63,7 +73,7 @@
     names = jnp.max(names, axis=0, keepdims=True)
     readers = lax.broadcasted_iota(jnp.int32, (1, parts), 1)
     names = jnp.where(readers == me_ref[0], 2.0, names)
-    names = jnp.broadcast_to(names, (lanes, parts)).T
+    names_ref[...] = jnp.broadcast_to(names, (lanes, parts)).T
     get_rows.wait()
     low = rows_ref[:, :lanes].astype(F32)
     high = rows_ref[:, lanes:].astype(F32)
@@ -71,8 +81,8 @@
     copies = []
     for chunk in range(CHUNKS):
         for reader in range(chunk * step, (chunk + 1) * step):
-            named = MEMBERS[reader]
-            name = jnp.broadcast_to(names[named : named + 1, :], low.shape)
+            named = jnp.where(me_ref[1] == 1, BACKWARD[reader], MEMBERS[reader])
+            name = jnp.broadcast_to(names_ref[pl.ds(named, 1), :], low.shape)
             block = jnp.where(name > 1.5, 0.0, jnp.where(name > 0.5, high, low))
             picked[reader] = block.astype(picked.dtype)
         part = pl.ds(chunk * step, step)
@@ -143,6 +153,7 @@
     parts = halo_blocks.shape[0]
     seeds = cotangent.shape[0]
     me = lax.axis_index("dom")
+    turned = lax.axis_index("feat") % 2
 
     feats_t = node_feats.T
     cot_t = cotangent.T
@@ -168,18 +179,19 @@
         ],
         scratch_shapes=[pltpu.VMEM(operand.shape, operand.dtype) for operand in operands]
         + [
+            pltpu.VMEM((parts, rows), F32),
             pltpu.VMEM((parts, width, rows), BF),
             pltpu.VMEM(side_shape, BF),
             pltpu.SemaphoreType.DMA((len(operands),)),
             pltpu.SemaphoreType.DMA((CHUNKS + 1,)),
         ],
-    )(me.reshape(1).astype(jnp.int32), *operands)
+    )(jnp.stack([me, turned]).astype(jnp.int32), *operands)
     halo_feats = exchange(send_feats)
     wanted = lax.dynamic_index_in_dim(halo_blocks, me, 0, keepdims=False)
     is_own = tile_index < own_blocks
     tile_block = wanted[jnp.clip(tile_index - own_blocks, 0, wanted.shape[0] - 1)]
     tile_owner = jnp.clip(tile_block // own_blocks, 0, parts - 1)
-    tile_slot = member_of(jnp.where(is_own, me, tile_owner))
+    tile_slot = member_of(jnp.where(is_own, me, tile_owner), turned)
 
     onehot = tile_index[:, :, None] == jnp.arange(own_blocks, dtype=jnp.int32)[None, None, :]
     dense = jnp.sum(
@@ -200,7 +212,10 @@
 
     named = jnp.any(halo_blocks == second, axis=1).astype(jnp.int32)
     named = jnp.where(jnp.arange(parts, dtype=jnp.int32) == me, 2, named)
-    named = named[jnp.array(MEMBERS, dtype=jnp.int32)][:, None, None]
+    order = jnp.where(
+        turned == 1, jnp.array(BACKWARD, dtype=jnp.int32), jnp.array(MEMBERS, dtype=jnp.int32)
+    )
+    named = named[order][:, None, None]
     history_t, named = lax.optimization_barrier((history.T, named))
     send_history = jnp.where(named == 1, history_t[None, :, rows:], history_t[None, :, :rows])
     send_history = jnp.where(named == 2, jnp.zeros((), BF), send_history)

time: 180 us -> 183 us (1.017)
  waiting for transfers between devices: 46.8 us -> 50.8 us
  starting transfers between devices: 47.7 us -> 45.8 us
    all_to_all x3, waiting for transfers between devices: 35.5 us -> 39.6 us  [exchange(): lax.all_to_all(pieces, ('dom', 'feat'), 0, 0, axis_index_groups=groups, t...]
  transfers between devices with their start and end apart: 6 -> 6, of which waited for: 4 -> 5; matrix products, arithmetic and copies ran while one was open for 9% -> 9% of each run, Pallas kernels for 0% -> 0%
where the time goes in v11:
time: 183 us; the launch traced here: 182 us
  waiting for transfers between devices  50.8 us (28%)
  starting transfers between devices  45.8 us (25%)
  blocking collectives  45.8 us (25%)
  between operations  14.5 us (8%)
  local copies, waits for them, and re-layouts  10.5 us (6%)
  matrix products  6.82 us (4%)
  other arithmetic  3.94 us (2%)
  Pallas kernels  3.78 us (2%)
    all_to_all x3, waiting for transfers between devices, exchange(): lax.all_to_all(pieces, ('dom', 'feat'), 0, 0, axis_index_groups=groups, t...  39.6 us
    all_to_all x3, starting transfers between devices, exchange(): lax.all_to_all(pieces, ('dom', 'feat'), 0, 0, axis_index_groups=groups, t...  35.5 us
    all_to_all x1, blocking collectives, exchange(): lax.all_to_all(pieces, ('dom', 'feat'), 0, 0, axis_index_groups=groups, t...  24.9 us
    all_gather x1, blocking collectives, on_device(): lax.all_gather(mean_one.astype(BF), 'feat', axis=0, tiled=True)  20.9 us
    all_to_all x1, starting transfers between devices, on_device(): lax.all_to_all(twos.reshape(slices, width, 2 * width), 'feat', 0, 0, tile...  10.2 us
    all_to_all x1, waiting for transfers between devices, on_device(): lax.all_to_all(twos.reshape(slices, width, 2 * width), 'feat', 0, 0, tile...  8.99 us
    dot_general x10, matrix products, mm(): return lax.dot_general(a, b, (dims, ((), ())), preferred_element_type=F32)  5.54 us
  transfers between devices with their start and end apart: 6, of which 5 were waited for; matrix products, arithmetic and copies ran while one was open for 9% of the time, Pallas kernels for 0%

profile of v11, /device:TPU:1, one launch (start us, length us, event | category | flops | bytes accessed | tf_op | source)
XLA Modules:
  0.0 182.0 jit_solution(12231253134744231652)
XLA Ops:
  7.3 0.6 pad_add_fusion.me_ref
  7.9 2.7 %shard_map.164 = (bf16[64,64,128]{2,1,0:T(8,128)(2,1)}, bf16[19,64,128]{2,1,0:T(8,128)(2,1)}) custom-call(s32[2]{0:T(128)} %pad_add_fusion.me_ref, s32[32,64]{1,0:T(8,128)} %bitcast.118, bf16[64,256]{1,0:T(8,128)(2,1)} %bitcast.119, bf16[64,128]{1,0:T(8,128)(2,1)} %bitcast.121, bf16[64,1024]{1,0:T(8,128)(2,1)} %bitcast.110, bf16[64,1024]{1,0:T(8,128)(2,1)} %bitcast.111), custom_call_target="tpu_custom_call" | custom-call | tf_op jit(solution)/shard_map/pallas_call | solution.py:171
  10.6 23.3 %all-to-all-start = ((bf16[64,64,128]{2,1,0:T(8,128)(2,1)}), bf16[64,64,128]{2,1,0:T(8,128)(2,1)S(1)}, u32[]{:S(2)}, u32[]{:S(2)}) async-start(bf16[64,64,128]{2,1,0:T(8,128)(2,1)} %get-tuple-element.30), calls=%async_computation | async-start | bytes 2097152 | tf_op jit(solution)/shard_map/all_to_all | solution.py:37
  34.0 0.8 gather_fusion
  35.1 0.8 gather_fusion.1
  36.4 0.5 select_reduce_fusion
  37.1 0.7 copy.46
  38.1 1.2 select_select_fusion
  39.3 23.4 %all-to-all-done = bf16[64,64,128]{2,1,0:T(8,128)(2,1)S(1)} async-done(((bf16[64,64,128]{2,1,0:T(8,128)(2,1)}), bf16[64,64,128]{2,1,0:T(8,128)(2,1)S(1)}, u32[]{:S(2)}, u32[]{:S(2)}) %all-to-all-start) | async-done | bytes 1048608 | tf_op jit(solution)/shard_map/all_to_all | solution.py:37
  62.7 7.1 %all-to-all-start.1 = ((bf16[64,64,128]{2,1,0:T(8,128)(2,1)}), bf16[64,64,128]{2,1,0:T(8,128)(2,1)}, u32[]{:S(2)}, u32[]{:S(2)}) async-start(bf16[64,64,128]{2,1,0:T(8,128)(2,1)} %select_select_fusion), calls=%async_computation.1 | async-start | bytes 2097152 | tf_op jit(solution)/shard_map/all_to_all | solution.py:37
  69.9 0.7 gather_fusion.2
  70.7 0.6 convolution_bitcast_fusion.2
  71.7 20.9 %all_gather.17 = bf16[1024,256]{1,0:T(8,128)(2,1)S(1)} all-gather(bf16[64,256]{1,0:T(8,128)(2,1)S(1)} %fusion.6), channel_id=1, replica_groups=mesh['dom'=64,'feat'=16] {'feat'}, dimensions={0}, use_global_device_ids=true | all-gather | bytes 557056 | tf_op jit(solution)/shard_map/all_gather | solution.py:232
  92.6 2.0 %constant_dynamic-slice_fusion = (bf16[16,1,64,128]{3,2,1,0:T(8,128)(2,1)}, bf16[16,1,64,128]{3,2,1,0:T(8,128)(2,1)S(1)}, bf16[16,1,64,128]{3,2,1,0:T(8,128)(2,1)S(1)}, bf16[16,1,64,128]{3,2,1,0:T(8,128)(2,1)S(1)}) fusion(bf16[16,19,64,128]{3,2,1,0:T(8,128)(2,1)} %bitcast.117, s32[]{:T(128)S(6)} %select_n.102), kind=kLoop, calls=%fused_computation.90 | loop fusion | bytes 2097156 | tf_op jit(solution)/shard_map/jit(dynamic_index_in_dim)/dynamic_slice | solution.py:209
  95.3 0.9 add_divide_fusion
  96.2 2.0 %all-to-all-done.1 = bf16[64,64,128]{2,1,0:T(8,128)(2,1)} async-done(((bf16[64,64,128]{2,1,0:T(8,128)(2,1)}), bf16[64,64,128]{2,1,0:T(8,128)(2,1)}, u32[]{:S(2)}, u32[]{:S(2)}) %all-to-all-start.1) | async-done | bytes 1048608 | tf_op jit(solution)/shard_map/all_to_all | solution.py:37
  98.2 1.9 %gather_fusion.3 = bf16[48,64,128]{2,1,0:T(8,128)(2,1)S(1)} fusion(bf16[64,64,128]{2,1,0:T(8,128)(2,1)} %all-to-all-done.1, s32[1024]{0:T(1024)S(1)} %pad_clamp_fusion), kind=kCustom, calls=%fused_computation.3 | custom fusion | bytes 1573056 | tf_op jit(solution)/shard_map/gather | solution.py:248
  100.2 0.6 convolution_bitcast_fusion.1
  101.2 1.0 convolution_convert_fusion.2
  102.3 10.2 %all-to-all-start.2 = ((bf16[16,64,128]{2,1,0:T(8,128)(2,1)}), bf16[16,64,128]{2,1,0:T(8,128)(2,1)S(1)}, u32[]{:S(2)}, u32[]{:S(2)}) async-start(bf16[16,64,128]{2,1,0:T(8,128)(2,1)} %bitcast.29), calls=%async_computation.2 | async-start | bytes 524288 | tf_op jit(solution)/shard_map/all_to_all | solution.py:268
  112.5 1.2 fusion.42
  113.8 0.5 fusion
  114.6 0.6 pad_maximum_fusion.1
  115.2 9.0 %all-to-all-done.2 = bf16[16,64,128]{2,1,0:T(8,128)(2,1)S(1)} async-done(((bf16[16,64,128]{2,1,0:T(8,128)(2,1)}), bf16[16,64,128]{2,1,0:T(8,128)(2,1)S(1)}, u32[]{:S(2)}, u32[]{:S(2)}) %all-to-all-start.2) | async-done | bytes 262176 | tf_op jit(solution)/shard_map/all_to_all | solution.py:268
  124.3 24.9 %all_to_all.25 = bf16[64,2,16,128]{3,2,1,0:T(8,128)(2,1)S(1)} all-to-all(bf16[64,2,16,128]{3,2,1,0:T(8,128)(2,1)S(1)} %pad_maximum_fusion), channel_id=1, replica_groups={{0,144,288,432,576,720,864,1008,16,160,304,448,592,736,880,896,32,176,3..., dimensions={0} | all-to-all | bytes 1048576 | tf_op jit(solution)/shard_map/all_to_all | solution.py:37
  149.3 0.9 broadcast_in_dim.111
  150.2 5.1 %all-to-all-start.4 = ((bf16[64,2,16,128]{3,2,1,0:T(8,128)(2,1)}), bf16[64,2,16,128]{3,2,1,0:T(8,128)(2,1)S(1)}, u32[]{:S(2)}, u32[]{:S(2)}) async-start(bf16[64,2,16,128]{3,2,1,0:T(8,128)(2,1)} %broadcast_in_dim.111), calls=%async_computation.4 | async-start | bytes 1048576 | tf_op jit(solution)/shard_map/all_to_all | solution.py:37
  155.2 2.2 %all-gather.7.cloned.1.call-done = bf16[2048,256]{1,0:T(8,128)(2,1)} async-done(((bf16[128,256]{1,0:T(8,128)(2,1)}), bf16[2048,256]{1,0:T(8,128)(2,1)}) %all-gather.7.cloned.1.call-update) | async-done | bytes 1048592 | tf_op jit(solution)/shard_map/all_gather | solution.py:270
  157.4 1.3 fusion.40
  158.9 0.8 fusion.9
  159.8 14.3 %all-to-all-done.4.sums_any = bf16[64,2,16,128]{3,2,1,0:T(8,128)(2,1)S(1)} async-done(((bf16[64,2,16,128]{3,2,1,0:T(8,128)(2,1)}), bf16[64,2,16,128]{3,2,1,0:T(8,128)(2,1)S(1)}, u32[]{:S(2)}, u32[]{:S(2)}) %all-to-all-start.4) | async-done | bytes 524320 | tf_op jit(solution)/shard_map/all_to_all | solution.py:37
  174.1 1.1 shard_map.165
  (80 shorter events, 3.7 us)
Async XLA Ops:
  7.2 88.2 %copy-start = (bf16[1024,64]{0,1:T(8,128)(2,1)S(1)}, bf16[1024,64]{0,1:T(8,128)(2,1)}, u32[]{:S(2)}) copy-start(bf16[1024,64]{0,1:T(8,128)(2,1)} %param.19) | copy-start | bytes 393220
  7.2 26.8 %copy-start.19 = (s32[64]{0:T(128)S(1)}, s32[64]{0:T(128)}, u32[]{:S(2)}) copy-start(s32[64]{0:T(128)} %constant.114.clone) | copy-start | bytes 772
  7.2 26.8 %copy-start.20 = (s32[64]{0:T(128)S(1)}, s32[64]{0:T(128)}, u32[]{:S(2)}) copy-start(s32[64]{0:T(128)} %constant.115.clone) | copy-start | bytes 772
  7.2 26.7 %copy-start.13 = (s32[64,32]{0,1:T(8,128)S(1)}, s32[64,32]{0,1:T(8,128)}, u32[]{:S(2)}) copy-start(s32[64,32]{0,1:T(8,128)} %param.15) | copy-start | bytes 24580
  7.2 26.8 %copy-start.18 = (s32[2,24]{1,0:T(2,128)S(1)}, s32[2,24]{1,0:T(2,128)}, u32[]{:S(2)}) copy-start(s32[2,24]{1,0:T(2,128)} %param.16) | copy-start | bytes 580
  7.2 85.4 %all-gather.5.cloned.1.call-start = ((), (), s32[]{:S(2)}) async-start(), calls=%async_computation.5 | async-start | bytes 5292032 | tf_op jit(solution)/shard_map/all_gather | solution.py:204
  10.6 25.4 %copy-start.1 = (bf16[2,24,128,128]{3,2,1,0:T(8,128)(2,1)S(1)}, bf16[2,24,128,128]{3,2,1,0:T(8,128)(2,1)}, u32[]{:S(2)}) copy-start(bf16[2,24,128,128]{3,2,1,0:T(8,128)(2,1)} %param.17) | copy-start | bytes 4718596
  10.6 52.1 %all-to-all-start = ((bf16[64,64,128]{2,1,0:T(8,128)(2,1)}), bf16[64,64,128]{2,1,0:T(8,128)(2,1)S(1)}, u32[]{:S(2)}, u32[]{:S(2)}) async-start(bf16[64,64,128]{2,1,0:T(8,128)(2,1)} %get-tuple-element.30), calls=%async_computation | async-start | bytes 2097152 | tf_op jit(solution)/shard_map/all_to_all | solution.py:37
  36.4 1.7 copy-start.17
  62.7 35.5 %all-to-all-start.1 = ((bf16[64,64,128]{2,1,0:T(8,128)(2,1)}), bf16[64,64,128]{2,1,0:T(8,128)(2,1)}, u32[]{:S(2)}, u32[]{:S(2)}) async-start(bf16[64,64,128]{2,1,0:T(8,128)(2,1)} %select_select_fusion), calls=%async_computation.1 | async-start | bytes 2097152 | tf_op jit(solution)/shard_map/all_to_all | solution.py:37
  70.6 0.9 copy-start.2
  70.6 0.9 copy-start.14
  70.7 23.9 %copy-start.22 = (bf16[1024,64]{0,1:T(8,128)(2,1)S(1)}, bf16[1024,64]{0,1:T(8,128)(2,1)}, u32[]{:S(2)}) copy-start(bf16[1024,64]{0,1:T(8,128)(2,1)} %param.18) | copy-start | bytes 393220
  71.3 23.5 %copy-start.21 = (s32[128]{0:T(128)S(1)}, s32[128]{0:T(128)}, u32[]{:S(2)}) copy-start(s32[128]{0:T(128)} %param.22) | copy-start | bytes 1540
  94.5 0.7 copy-start.9
  94.5 0.8 copy-start.11
  100.1 0.9 copy-start.3
  100.1 0.9 copy-start.7
  101.0 12.7 %copy-start.4 = (bf16[32,8,2,128]{3,1,2,0:T(8,128)(2,1)S(1)}, bf16[32,8,2,128]{3,1,2,0:T(8,128)(2,1)}, u32[]{:S(2)}) copy-start(bf16[32,8,2,128]{3,1,2,0:T(8,128)(2,1)} %copy.46) | copy-start | bytes 393220
  101.0 12.7 %copy-start.10 = (bf16[16,1,64,128]{3,2,1,0:T(8,128)(2,1)S(1)}, bf16[16,1,64,128]{3,2,1,0:T(8,128)(2,1)}, u32[]{:S(2)}) copy-start(bf16[16,1,64,128]{3,2,1,0:T(8,128)(2,1)} %copy-done.9) | copy-start | bytes 786436
  101.0 12.7 %copy-start.12 = (bf16[16,1,64,128]{3,2,1,0:T(8,128)(2,1)S(1)}, bf16[16,1,64,128]{3,2,1,0:T(8,128)(2,1)}, u32[]{:S(2)}) copy-start(bf16[16,1,64,128]{3,2,1,0:T(8,128)(2,1)} %copy-done.11) | copy-start | bytes 786436
  101.0 12.7 %copy-start.15 = (f32[64,256]{1,0:T(8,128)S(1)}, f32[64,256]{1,0:T(8,128)}, u32[]{:S(2)}) copy-start(f32[64,256]{1,0:T(8,128)} %get-tuple-element.42) | copy-start | bytes 196612
  101.1 12.7 %copy-start.16 = (f32[64,256]{1,0:T(8,128)S(1)}, f32[64,256]{1,0:T(8,128)}, u32[]{:S(2)}) copy-start(f32[64,256]{1,0:T(8,128)} %get-tuple-element.43) | copy-start | bytes 196612
  102.3 21.9 %all-to-all-start.2 = ((bf16[16,64,128]{2,1,0:T(8,128)(2,1)}), bf16[16,64,128]{2,1,0:T(8,128)(2,1)S(1)}, u32[]{:S(2)}, u32[]{:S(2)}) async-start(bf16[16,64,128]{2,1,0:T(8,128)(2,1)} %bitcast.29), calls=%async_computation.2 | async-start | bytes 524288 | tf_op jit(solution)/shard_map/all_to_all | solution.py:268
  112.5 44.9 %all-gather.7.cloned.1.call-start = ((), (), s32[]{:S(2)}) async-start(), calls=%async_computation.6 | async-start | bytes 1114112 | tf_op jit(solution)/shard_map/all_gather | solution.py:270
  113.8 0.8 copy-start.8
  149.2 9.5 %copy-start.5 = (bf16[1024,64]{0,1:T(8,128)(2,1)S(1)}, bf16[1024,64]{0,1:T(8,128)(2,1)}, u32[]{:S(2)}) copy-start(bf16[1024,64]{0,1:T(8,128)(2,1)} %param.20) | copy-start | bytes 393220
  149.3 9.6 %copy-start.6 = (bf16[1024,64]{0,1:T(8,128)(2,1)S(1)}, bf16[1024,64]{0,1:T(8,128)(2,1)}, u32[]{:S(2)}) copy-start(bf16[1024,64]{0,1:T(8,128)(2,1)} %param.21) | copy-start | bytes 393220
  150.2 23.9 %all-to-all-start.4 = ((bf16[64,2,16,128]{3,2,1,0:T(8,128)(2,1)}), bf16[64,2,16,128]{3,2,1,0:T(8,128)(2,1)S(1)}, u32[]{:S(2)}, u32[]{:S(2)}) async-start(bf16[64,2,16,128]{3,2,1,0:T(8,128)(2,1)} %broadcast_in_dim.111), calls=%async_computation.4 | async-start | bytes 1048576 | tf_op jit(solution)/shard_map/all_to_all | solution.py:37
Sparse Core Ops, SparseCore 0:
  10.8 60.8 all-gather.4
  124.3 33.0 all-gather.6

commit v12 on v10

--- a/solution.py
+++ b/solution.py
@@ -213,7 +213,7 @@
         out = jnp.einsum("bkfc,bkvc->fbv", picked, tile_weight, preferred_element_type=F32)
         return out.reshape(width, owned)
 
-    mean_one = (halo_sum(halo_feats[tile_slot]) + mm(feats_t, dense, ((1,), (1,)))) * inverse
+    mean_one = (halo_sum(halo_feats.at[tile_slot].get(mode="promise_in_bounds")) + mm(feats_t, dense, ((1,), (1,)))) * inverse
     whole_mean_one = lax.all_gather(mean_one.astype(BF), "feat", axis=0, tiled=True)
     pre_one = mm(self_one_t, whole_feats, ((1,), (0,))) + mm(
         neigh_one_t, whole_mean_one, ((1,), (0,))
@@ -230,7 +230,7 @@
         (halo_history, hidden, whole_grad_two)
     )
     mean_two = (
-        (halo_sum(halo_history[tile_slot]) + mm(hidden, dense, ((1,), (1,)))) * inverse
+        (halo_sum(halo_history.at[tile_slot].get(mode="promise_in_bounds")) + mm(hidden, dense, ((1,), (1,)))) * inverse
     ).astype(BF)
     layer_two = jnp.concatenate([hidden, mean_two], axis=0)
 

time: 180 us -> 180 us (level)
  no operation moved by 1% of the time
where the time goes in v12:
time: 180 us; the launch traced here: 179 us
  starting transfers between devices  47.7 us (26%)
  waiting for transfers between devices  46.8 us (26%)
  blocking collectives  45.8 us (25%)
  between operations  14.5 us (8%)
  local copies, waits for them, and re-layouts  10.5 us (6%)
  matrix products  6.86 us (4%)
  other arithmetic  3.33 us (2%)
  Pallas kernels  3.15 us (2%)
    all_to_all x3, starting transfers between devices, exchange(): lax.all_to_all(pieces, 'dom', 0, 0, axis_index_groups=[MEMBERS], tiled=True)  36.2 us
    all_to_all x3, waiting for transfers between devices, exchange(): lax.all_to_all(pieces, 'dom', 0, 0, axis_index_groups=[MEMBERS], tiled=True)  35.5 us
    all_to_all x1, blocking collectives, exchange(): lax.all_to_all(pieces, 'dom', 0, 0, axis_index_groups=[MEMBERS], tiled=True)  24.2 us
    all_gather x1, blocking collectives, on_device(): lax.all_gather(mean_one.astype(BF), 'feat', axis=0, tiled=True)  21.6 us
    all_to_all x1, starting transfers between devices, on_device(): lax.all_to_all(twos.reshape(slices, width, 2 * width), 'feat', 0, 0, tile...  11.4 us
    all_to_all x1, waiting for transfers between devices, on_device(): lax.all_to_all(twos.reshape(slices, width, 2 * width), 'feat', 0, 0, tile...  8.99 us
    dot_general x10, matrix products, mm(): return lax.dot_general(a, b, (dims, ((), ())), preferred_element_type=F32)  5.58 us
  transfers between devices with their start and end apart: 6, of which 4 were waited for; matrix products, arithmetic and copies ran while one was open for 9% of the time, Pallas kernels for 0%

profile of v12, /device:TPU:1, one launch (start us, length us, event | category | flops | bytes accessed | tf_op | source)
XLA Modules:
  0.0 178.6 jit_solution(18218303655117185652)
XLA Ops:
  7.3 2.1 %shard_map.155 = (bf16[64,64,128]{2,1,0:T(8,128)(2,1)}, bf16[19,64,128]{2,1,0:T(8,128)(2,1)}) custom-call(s32[1]{0:T(128)} %bitcast.6.me_ref, s32[32,64]{1,0:T(8,128)} %bitcast.117, bf16[64,256]{1,0:T(8,128)(2,1)} %bitcast.118, bf16[64,128]{1,0:T(8,128)(2,1)} %bitcast.120, bf16[64,1024]{1,0:T(8,128)(2,1)} %bitcast.109, bf16[64,1024]{1,0:T(8,128)(2,1)} %bitcast.110), custom_call_target="tpu_custom_call" | custom-call | tf_op jit(solution)/shard_map/pallas_call | solution.py:160
  9.4 23.3 %all-to-all-start = ((bf16[64,64,128]{2,1,0:T(8,128)(2,1)}), bf16[64,64,128]{2,1,0:T(8,128)(2,1)S(1)}, u32[]{:S(2)}, u32[]{:S(2)}) async-start(bf16[64,64,128]{2,1,0:T(8,128)(2,1)} %get-tuple-element.30), calls=%async_computation | async-start | bytes 2097152 | tf_op jit(solution)/shard_map/all_to_all | solution.py:28
  32.8 0.8 gather_fusion
  33.8 0.8 gather_fusion.1
  34.7 0.4 convert_element_type.54
  35.1 0.5 select_reduce_fusion
  35.8 0.7 copy.45
  36.8 1.2 select_select_fusion
  38.0 22.9 %all-to-all-done = bf16[64,64,128]{2,1,0:T(8,128)(2,1)S(1)} async-done(((bf16[64,64,128]{2,1,0:T(8,128)(2,1)}), bf16[64,64,128]{2,1,0:T(8,128)(2,1)S(1)}, u32[]{:S(2)}, u32[]{:S(2)}) %all-to-all-start) | async-done | bytes 1048608 | tf_op jit(solution)/shard_map/all_to_all | solution.py:28
  60.9 7.0 %all-to-all-start.1 = ((bf16[64,64,128]{2,1,0:T(8,128)(2,1)}), bf16[64,64,128]{2,1,0:T(8,128)(2,1)}, u32[]{:S(2)}, u32[]{:S(2)}) async-start(bf16[64,64,128]{2,1,0:T(8,128)(2,1)} %select_select_fusion), calls=%async_computation.1 | async-start | bytes 2097152 | tf_op jit(solution)/shard_map/all_to_all | solution.py:28
  68.1 0.7 gather_fusion.2
  68.8 0.6 convolution_bitcast_fusion.2
  69.9 21.6 %all_gather.17 = bf16[1024,256]{1,0:T(8,128)(2,1)S(1)} all-gather(bf16[64,256]{1,0:T(8,128)(2,1)S(1)} %fusion.6), channel_id=1, replica_groups=mesh['dom'=64,'feat'=16] {'feat'}, dimensions={0}, use_global_device_ids=true | all-gather | bytes 557056 | tf_op jit(solution)/shard_map/all_gather | solution.py:217
  91.5 2.0 %constant_dynamic-slice_fusion = (bf16[16,1,64,128]{3,2,1,0:T(8,128)(2,1)}, bf16[16,1,64,128]{3,2,1,0:T(8,128)(2,1)S(1)}, bf16[16,1,64,128]{3,2,1,0:T(8,128)(2,1)S(1)}, bf16[16,1,64,128]{3,2,1,0:T(8,128)(2,1)S(1)}) fusion(bf16[16,19,64,128]{3,2,1,0:T(8,128)(2,1)} %bitcast.116, s32[]{:T(128)S(6)} %select_n.70), kind=kLoop, calls=%fused_computation.82 | loop fusion | bytes 2097156 | tf_op jit(solution)/shard_map/jit(dynamic_index_in_dim)/dynamic_slice | solution.py:197
  93.7 0.3 convolution_convert_fusion.1
  94.2 0.9 add_divide_fusion
  95.1 1.9 %gather_fusion.3 = bf16[48,64,128]{2,1,0:T(8,128)(2,1)S(1)} fusion(bf16[64,64,128]{2,1,0:T(8,128)(2,1)} %all-to-all-done.1, s32[1024]{0:T(1024)S(1)} %pad_clamp_fusion), kind=kCustom, calls=%fused_computation.3 | custom fusion | bytes 1573056 | tf_op jit(solution)/shard_map/gather | solution.py:233
  97.0 0.6 convolution_bitcast_fusion.1
  98.1 1.0 convolution_convert_fusion.2
  99.2 11.4 %all-to-all-start.2 = ((bf16[16,64,128]{2,1,0:T(8,128)(2,1)}), bf16[16,64,128]{2,1,0:T(8,128)(2,1)S(1)}, u32[]{:S(2)}, u32[]{:S(2)}) async-start(bf16[16,64,128]{2,1,0:T(8,128)(2,1)} %bitcast.28), calls=%async_computation.2 | async-start | bytes 524288 | tf_op jit(solution)/shard_map/all_to_all | solution.py:253
  110.6 1.2 fusion.40
  111.9 0.5 fusion
  112.7 0.6 pad_maximum_fusion.1
  113.3 9.0 %all-to-all-done.2 = bf16[16,64,128]{2,1,0:T(8,128)(2,1)S(1)} async-done(((bf16[16,64,128]{2,1,0:T(8,128)(2,1)}), bf16[16,64,128]{2,1,0:T(8,128)(2,1)S(1)}, u32[]{:S(2)}, u32[]{:S(2)}) %all-to-all-start.2) | async-done | bytes 262176 | tf_op jit(solution)/shard_map/all_to_all | solution.py:253
  122.4 24.2 %all_to_all.25 = bf16[64,2,16,128]{3,2,1,0:T(8,128)(2,1)S(1)} all-to-all(bf16[64,2,16,128]{3,2,1,0:T(8,128)(2,1)S(1)} %pad_maximum_fusion), channel_id=1, replica_groups={{0,144,288,432,576,720,864,1008,16,160,304,448,592,736,880,896,32,176,3..., dimensions={0} | all-to-all | bytes 1048576 | tf_op jit(solution)/shard_map/all_to_all | solution.py:28
  146.7 0.9 broadcast_in_dim.111
  147.6 5.8 %all-to-all-start.4 = ((bf16[64,2,16,128]{3,2,1,0:T(8,128)(2,1)}), bf16[64,2,16,128]{3,2,1,0:T(8,128)(2,1)S(1)}, u32[]{:S(2)}, u32[]{:S(2)}) async-start(bf16[64,2,16,128]{3,2,1,0:T(8,128)(2,1)} %broadcast_in_dim.111), calls=%async_computation.4 | async-start | bytes 1048576 | tf_op jit(solution)/shard_map/all_to_all | solution.py:28
  153.4 2.3 %all-gather.7.cloned.1.call-done = bf16[2048,256]{1,0:T(8,128)(2,1)} async-done(((bf16[128,256]{1,0:T(8,128)(2,1)}), bf16[2048,256]{1,0:T(8,128)(2,1)}) %all-gather.7.cloned.1.call-update) | async-done | bytes 1048592 | tf_op jit(solution)/shard_map/all_gather | solution.py:255
  155.7 1.3 fusion.38
  157.3 0.8 fusion.9
  158.1 12.6 %all-to-all-done.4.sums_any = bf16[64,2,16,128]{3,2,1,0:T(8,128)(2,1)S(1)} async-done(((bf16[64,2,16,128]{3,2,1,0:T(8,128)(2,1)}), bf16[64,2,16,128]{3,2,1,0:T(8,128)(2,1)S(1)}, u32[]{:S(2)}, u32[]{:S(2)}) %all-to-all-start.4) | async-done | bytes 524320 | tf_op jit(solution)/shard_map/all_to_all | solution.py:28
  170.7 1.1 shard_map.156
  (76 shorter events, 3.0 us)
Async XLA Ops:
  7.2 87.1 %copy-start = (bf16[1024,64]{0,1:T(8,128)(2,1)S(1)}, bf16[1024,64]{0,1:T(8,128)(2,1)}, u32[]{:S(2)}) copy-start(bf16[1024,64]{0,1:T(8,128)(2,1)} %param.18) | copy-start | bytes 393220
  7.2 25.6 %copy-start.19 = (s32[64]{0:T(128)S(1)}, s32[64]{0:T(128)}, u32[]{:S(2)}) copy-start(s32[64]{0:T(128)} %constant.101) | copy-start | bytes 772
  7.2 25.5 %copy-start.13 = (s32[64,32]{0,1:T(8,128)S(1)}, s32[64,32]{0,1:T(8,128)}, u32[]{:S(2)}) copy-start(s32[64,32]{0,1:T(8,128)} %param.14) | copy-start | bytes 24580
  7.2 25.5 %copy-start.18 = (s32[2,24]{1,0:T(2,128)S(1)}, s32[2,24]{1,0:T(2,128)}, u32[]{:S(2)}) copy-start(s32[2,24]{1,0:T(2,128)} %param.15) | copy-start | bytes 580
  7.2 84.3 %all-gather.5.cloned.1.call-start = ((), (), s32[]{:S(2)}) async-start(), calls=%async_computation.5 | async-start | bytes 5292032 | tf_op jit(solution)/shard_map/all_gather | solution.py:192
  9.3 25.4 %copy-start.1 = (bf16[2,24,128,128]{3,2,1,0:T(8,128)(2,1)S(1)}, bf16[2,24,128,128]{3,2,1,0:T(8,128)(2,1)}, u32[]{:S(2)}) copy-start(bf16[2,24,128,128]{3,2,1,0:T(8,128)(2,1)} %param.16) | copy-start | bytes 4718596
  9.4 51.6 %all-to-all-start = ((bf16[64,64,128]{2,1,0:T(8,128)(2,1)}), bf16[64,64,128]{2,1,0:T(8,128)(2,1)S(1)}, u32[]{:S(2)}, u32[]{:S(2)}) async-start(bf16[64,64,128]{2,1,0:T(8,128)(2,1)} %get-tuple-element.30), calls=%async_computation | async-start | bytes 2097152 | tf_op jit(solution)/shard_map/all_to_all | solution.py:28
  35.1 1.7 copy-start.17
  60.9 34.2 %all-to-all-start.1 = ((bf16[64,64,128]{2,1,0:T(8,128)(2,1)}), bf16[64,64,128]{2,1,0:T(8,128)(2,1)}, u32[]{:S(2)}, u32[]{:S(2)}) async-start(bf16[64,64,128]{2,1,0:T(8,128)(2,1)} %select_select_fusion), calls=%async_computation.1 | async-start | bytes 2097152 | tf_op jit(solution)/shard_map/all_to_all | solution.py:28
  68.8 0.9 copy-start.2
  68.8 0.9 copy-start.14
  68.8 24.6 %copy-start.21 = (bf16[1024,64]{0,1:T(8,128)(2,1)S(1)}, bf16[1024,64]{0,1:T(8,128)(2,1)}, u32[]{:S(2)}) copy-start(bf16[1024,64]{0,1:T(8,128)(2,1)} %param.17) | copy-start | bytes 393220
  69.5 24.2 %copy-start.20 = (s32[128]{0:T(128)S(1)}, s32[128]{0:T(128)}, u32[]{:S(2)}) copy-start(s32[128]{0:T(128)} %param.21) | copy-start | bytes 1540
  93.4 0.7 copy-start.9
  93.4 0.8 copy-start.11
  97.0 0.9 copy-start.3
  97.0 0.9 copy-start.7
  97.9 13.9 %copy-start.4 = (bf16[32,8,2,128]{3,1,2,0:T(8,128)(2,1)S(1)}, bf16[32,8,2,128]{3,1,2,0:T(8,128)(2,1)}, u32[]{:S(2)}) copy-start(bf16[32,8,2,128]{3,1,2,0:T(8,128)(2,1)} %copy.45) | copy-start | bytes 393220
  97.9 13.9 %copy-start.10 = (bf16[16,1,64,128]{3,2,1,0:T(8,128)(2,1)S(1)}, bf16[16,1,64,128]{3,2,1,0:T(8,128)(2,1)}, u32[]{:S(2)}) copy-start(bf16[16,1,64,128]{3,2,1,0:T(8,128)(2,1)} %copy-done.9) | copy-start | bytes 786436
  97.9 14.0 %copy-start.12 = (bf16[16,1,64,128]{3,2,1,0:T(8,128)(2,1)S(1)}, bf16[16,1,64,128]{3,2,1,0:T(8,128)(2,1)}, u32[]{:S(2)}) copy-start(bf16[16,1,64,128]{3,2,1,0:T(8,128)(2,1)} %copy-done.11) | copy-start | bytes 786436
  97.9 14.0 %copy-start.15 = (f32[64,256]{1,0:T(8,128)S(1)}, f32[64,256]{1,0:T(8,128)}, u32[]{:S(2)}) copy-start(f32[64,256]{1,0:T(8,128)} %get-tuple-element.42) | copy-start | bytes 196612
  98.0 14.0 %copy-start.16 = (f32[64,256]{1,0:T(8,128)S(1)}, f32[64,256]{1,0:T(8,128)}, u32[]{:S(2)}) copy-start(f32[64,256]{1,0:T(8,128)} %get-tuple-element.43) | copy-start | bytes 196612
  99.2 23.1 %all-to-all-start.2 = ((bf16[16,64,128]{2,1,0:T(8,128)(2,1)}), bf16[16,64,128]{2,1,0:T(8,128)(2,1)S(1)}, u32[]{:S(2)}, u32[]{:S(2)}) async-start(bf16[16,64,128]{2,1,0:T(8,128)(2,1)} %bitcast.28), calls=%async_computation.2 | async-start | bytes 524288 | tf_op jit(solution)/shard_map/all_to_all | solution.py:253
  110.6 45.1 %all-gather.7.cloned.1.call-start = ((), (), s32[]{:S(2)}) async-start(), calls=%async_computation.6 | async-start | bytes 1114112 | tf_op jit(solution)/shard_map/all_gather | solution.py:255
  111.9 0.8 copy-start.8
  146.6 10.5 %copy-start.5 = (bf16[1024,64]{0,1:T(8,128)(2,1)S(1)}, bf16[1024,64]{0,1:T(8,128)(2,1)}, u32[]{:S(2)}) copy-start(bf16[1024,64]{0,1:T(8,128)(2,1)} %param.19) | copy-start | bytes 393220
  146.7 10.6 %copy-start.6 = (bf16[1024,64]{0,1:T(8,128)(2,1)S(1)}, bf16[1024,64]{0,1:T(8,128)(2,1)}, u32[]{:S(2)}) copy-start(bf16[1024,64]{0,1:T(8,128)(2,1)} %param.20) | copy-start | bytes 393220
  147.6 23.1 %all-to-all-start.4 = ((bf16[64,2,16,128]{3,2,1,0:T(8,128)(2,1)}), bf16[64,2,16,128]{3,2,1,0:T(8,128)(2,1)S(1)}, u32[]{:S(2)}, u32[]{:S(2)}) async-start(bf16[64,2,16,128]{3,2,1,0:T(8,128)(2,1)} %broadcast_in_dim.111), calls=%async_computation.4 | async-start | bytes 1048576 | tf_op jit(solution)/shard_map/all_to_all | solution.py:28
Sparse Core Ops, SparseCore 0:
  10.8 60.8 all-gather.4
  122.5 33.2 all-gather.6
